TPU v7x, 32 devices: a whole 2x2x4 slice. The times are simulated.
32 devices in a mesh: dp: 16 (over z, x, core), tensor: 2 (over y).
Axes of the slice: x: 2, y: 2, z: 4, core: 2. Of those that a mesh axis runs over, the one named last changes fastest.
Arguments:
- layer_input: bfloat16 [16384, 1024], P(('dp', 'tensor')), may hold values from -6 to 6
- qkv_weight: bfloat16 [3, 1024, 1024], P(None, None, 'tensor'), may hold values from -0.1875 to 0.1875
- qv_bias: float32 [2, 1024], P(None, 'tensor'), may hold values from -3 to 3
- out_weight: bfloat16 [1024, 1024], P('tensor'), may hold values from -1.5 to 1.5
- out_bias: float32 [1024], replicated, may hold values from -3 to 3
- norm1_gain: float32 [1024], replicated, may hold values from 0.5 to 1.5
- norm1_shift: float32 [1024], replicated, may hold values from -3 to 3
- up_weight: bfloat16 [1024, 4096], P(None, 'tensor'), may hold values from -0.1875 to 0.1875
- up_bias: bfloat16 [4096], P('tensor'), may hold values from -3 to 3
- down_weight: bfloat16 [4096, 1024], P('tensor'), may hold values from -0.09375 to 0.09375
- down_bias: float32 [1024], replicated, may hold values from -3 to 3
- norm2_gain: float32 [1024], replicated, may hold values from 0.5 to 1.5
- norm2_shift: float32 [1024], replicated, may hold values from -3 to 3
- lengths: int32 [32], P('dp'), may hold values from 64 to 512, as said below
- grad_output: bfloat16 [16384, 1024], P(('dp', 'tensor')), may hold values from -6 to 6
Outputs:
- layer_output: bfloat16 [16384, 1024], P(('dp', 'tensor'))
- grad_input: float32 [16384, 1024], P(('dp', 'tensor'))
- grad_qkv_weight: float32 [3, 1024, 1024], P(None, None, 'tensor')
- grad_qv_bias: float32 [2, 1024], P(None, 'tensor')
- grad_out_weight: float32 [1024, 1024], P('tensor')
- grad_out_bias: float32 [1024], replicated
- grad_norm1_gain: float32 [1024], replicated
- grad_norm1_shift: float32 [1024], replicated
- grad_up_weight: float32 [1024, 4096], P(None, 'tensor')
- grad_up_bias: float32 [4096], P('tensor')
- grad_down_weight: float32 [4096, 1024], P('tensor')
- grad_down_bias: float32 [1024], replicated
- grad_norm2_gain: float32 [1024], replicated
- grad_norm2_shift: float32 [1024], replicated
Inputs may be any that keep to these rules, and one draw needn't show every extreme that they name: `lengths`: each dp group holds 512 * 2 // 512 consecutive slots; in every group one slot, drawn from the seed, holds a full item of 512 residues, the others hold short items of 64 to 128 or long ones over 256.
All inputs are finite; a program needn't handle non-finite values.
Results may differ from a plain program's by a relative error of at most 0.013.
The roundings to bfloat16 on the way count: a program that leaves them out, or rounds other values in their place, can miss the bound.
Values may be sent and summed in bfloat16 or wider, within the bound.
No kernel may reach another device: no remote copies, remote signals or barrier semaphores. Data moves between devices by JAX's collectives and lax.ppermute only.
A program may use at most 192 MiB of HBM per device.

v0:
```python
import jax
import jax.numpy as jnp
from jax import lax
from jax.sharding import PartitionSpec as P

HD = 64
SEQ_LEN = 512


def norm_rows(hidden, gain, shift):
    center = hidden - jnp.mean(hidden, axis=-1, keepdims=True)
    spread = jnp.mean(center * center, axis=-1, keepdims=True)
    return center * lax.rsqrt(spread + 1e-05) * gain + shift


def gelu_exact(upward):
    return jax.nn.gelu(upward, approximate=False)


def slot_scores(query, keys, length):
    scores = jnp.einsum("qhd,khd->hqk", query, keys, preferred_element_type=jnp.float32) * HD ** (
        -0.5
    )
    valid = jnp.arange(query.shape[0]) < length
    return jnp.where(valid[None, None, :], scores, jnp.float32(-1000000000.0))


def attend_slot(member):
    query, keys, values, length = member
    scores = slot_scores(query, keys, length)
    highest = jnp.max(scores, axis=-1, keepdims=True)
    expo = jnp.exp(scores - highest)
    totals = jnp.sum(expo, axis=-1, keepdims=True)
    probs = (expo / totals).astype(jnp.bfloat16)
    mixed = jnp.einsum("hqk,khd->qhd", probs, values, preferred_element_type=jnp.float32)
    return (mixed.astype(jnp.bfloat16), highest[..., 0] + jnp.log(totals[..., 0]))


def attend_back(member):
    query, keys, values, length, log_total, grad_mixed = member
    scores = slot_scores(query, keys, length)
    probs = jnp.exp(scores - log_total[..., None])
    grad_values = jnp.einsum(
        "hqk,qhd->khd", probs.astype(jnp.bfloat16), grad_mixed, preferred_element_type=jnp.float32
    )
    grad_probs = jnp.einsum("qhd,khd->hqk", grad_mixed, values, preferred_element_type=jnp.float32)
    center = jnp.sum(probs * grad_probs, axis=-1, keepdims=True)
    grad_scores = (probs * (grad_probs - center)).astype(jnp.bfloat16)
    grad_query = jnp.einsum(
        "hqk,khd->qhd", grad_scores, keys, preferred_element_type=jnp.float32
    ) * HD ** (-0.5)
    grad_keys = jnp.einsum(
        "hqk,qhd->khd", grad_scores, query, preferred_element_type=jnp.float32
    ) * HD ** (-0.5)
    return (grad_query, grad_keys, grad_values)


def body(
    layer_input,
    qkv_weight,
    qv_bias,
    out_weight,
    out_bias,
    norm1_gain,
    norm1_shift,
    up_weight,
    up_bias,
    down_weight,
    down_bias,
    norm2_gain,
    norm2_shift,
    lengths,
    grad_output,
):
    local_width = qkv_weight.shape[2]
    heads_here = local_width // HD
    slot_count = lengths.shape[0]
    layout = (slot_count, SEQ_LEN, heads_here, HD)
    input_all = lax.all_gather(layer_input, "tensor", axis=0, tiled=True)
    projected = jnp.einsum("td,cde->cte", input_all, qkv_weight, preferred_element_type=jnp.float32)
    query = (projected[0] + qv_bias[0]).astype(jnp.bfloat16).reshape(layout)
    keys = projected[1].astype(jnp.bfloat16).reshape(layout)
    values = (projected[2] + qv_bias[1]).astype(jnp.bfloat16).reshape(layout)
    mixed_slots, log_total = lax.map(attend_slot, (query, keys, values, lengths))
    mixed = mixed_slots.reshape(-1, local_width)
    attention = lax.psum_scatter(
        jnp.dot(mixed, out_weight, preferred_element_type=jnp.float32),
        "tensor",
        scatter_dimension=0,
        tiled=True,
    )
    hidden_one = attention + out_bias + layer_input.astype(jnp.float32)
    normed_one, norm1_back = jax.vjp(norm_rows, hidden_one, norm1_gain, norm1_shift)
    normed_low = normed_one.astype(jnp.bfloat16)
    normed_all = lax.all_gather(normed_low, "tensor", axis=0, tiled=True)
    upward = jnp.dot(normed_all, up_weight, preferred_element_type=jnp.float32) + up_bias.astype(
        jnp.float32
    )
    active, gelu_back = jax.vjp(gelu_exact, upward)
    active_low = active.astype(jnp.bfloat16)
    feed = lax.psum_scatter(
        jnp.dot(active_low, down_weight, preferred_element_type=jnp.float32),
        "tensor",
        scatter_dimension=0,
        tiled=True,
    )
    hidden_two = feed + down_bias + normed_one
    result, norm2_back = jax.vjp(norm_rows, hidden_two, norm2_gain, norm2_shift)
    grad_two, grad_gain_two, grad_shift_two = norm2_back(grad_output.astype(jnp.float32))
    grad_two_low = grad_two.astype(jnp.bfloat16)
    grad_two_all = lax.all_gather(grad_two_low, "tensor", axis=0, tiled=True)
    grad_active = jnp.einsum(
        "td,fd->tf", grad_two_all, down_weight, preferred_element_type=jnp.float32
    )
    (grad_upward,) = gelu_back(grad_active)
    grad_up_low = grad_upward.astype(jnp.bfloat16)
    grad_normed = lax.psum_scatter(
        jnp.einsum("tf,df->td", grad_up_low, up_weight, preferred_element_type=jnp.float32),
        "tensor",
        scatter_dimension=0,
        tiled=True,
    )
    grad_up = jnp.einsum("td,tf->df", normed_all, grad_up_low, preferred_element_type=jnp.float32)
    grad_down = jnp.einsum(
        "tf,td->fd", active_low, grad_two_all, preferred_element_type=jnp.float32
    )
    grad_up_bias = jnp.sum(grad_up_low.astype(jnp.float32), axis=0)
    grad_one, grad_gain_one, grad_shift_one = norm1_back(grad_normed + grad_two)
    grad_one_all = lax.all_gather(grad_one.astype(jnp.bfloat16), "tensor", axis=0, tiled=True)
    grad_out = jnp.einsum("te,td->ed", mixed, grad_one_all, preferred_element_type=jnp.float32)
    grad_mixed = jnp.einsum(
        "td,ed->te", grad_one_all, out_weight, preferred_element_type=jnp.float32
    )
    grad_mixed = grad_mixed.astype(jnp.bfloat16).reshape(layout)
    grad_query, grad_keys, grad_values = lax.map(
        attend_back, (query, keys, values, lengths, log_total, grad_mixed)
    )
    grad_proj = (
        jnp.stack([grad_query, grad_keys, grad_values])
        .reshape(3, -1, local_width)
        .astype(jnp.bfloat16)
    )
    grad_input = (
        lax.psum_scatter(
            jnp.einsum("cte,cde->td", grad_proj, qkv_weight, preferred_element_type=jnp.float32),
            "tensor",
            scatter_dimension=0,
            tiled=True,
        )
        + grad_one
    )
    grad_qkv = jnp.einsum("td,cte->cde", input_all, grad_proj, preferred_element_type=jnp.float32)
    grad_bias_qv = jnp.stack(
        [
            jnp.sum(grad_proj[0].astype(jnp.float32), axis=0),
            jnp.sum(grad_proj[2].astype(jnp.float32), axis=0),
        ]
    )
    grad_qkv, grad_bias_qv, grad_out, grad_up, grad_up_bias, grad_down = lax.psum(
        (grad_qkv, grad_bias_qv, grad_out, grad_up, grad_up_bias, grad_down), "dp"
    )
    grad_out_bias, grad_gain_one, grad_shift_one, grad_down_bias, grad_gain_two, grad_shift_two = (
        lax.psum(
            (
                jnp.sum(grad_one, axis=0),
                grad_gain_one,
                grad_shift_one,
                jnp.sum(grad_two, axis=0),
                grad_gain_two,
                grad_shift_two,
            ),
            ("dp", "tensor"),
        )
    )
    return (
        result.astype(jnp.bfloat16),
        grad_input,
        grad_qkv,
        grad_bias_qv,
        grad_out,
        grad_out_bias,
        grad_gain_one,
        grad_shift_one,
        grad_up,
        grad_up_bias,
        grad_down,
        grad_down_bias,
        grad_gain_two,
        grad_shift_two,
    )


def solution(mesh):
    return jax.shard_map(
        body,
        mesh=mesh,
        in_specs=(
            P(("dp", "tensor"), None),
            P(None, None, "tensor"),
            P(None, "tensor"),
            P("tensor", None),
            P(),
            P(),
            P(),
            P(None, "tensor"),
            P("tensor"),
            P("tensor", None),
            P(),
            P(),
            P(),
            P("dp"),
            P(("dp", "tensor"), None),
        ),
        out_specs=(
            P(("dp", "tensor"), None),
            P(("dp", "tensor"), None),
            P(None, None, "tensor"),
            P(None, "tensor"),
            P("tensor", None),
            P(),
            P(),
            P(),
            P(None, "tensor"),
            P("tensor"),
            P("tensor", None),
            P(),
            P(),
            P(),
        ),
        check_vma=False,
    )
```

profile of v0, /device:TPU:0, one launch (start us, length us, event | category | flops | bytes accessed | tf_op | source)
XLA Modules:
  0.0 1047.4 jit_solution(12729809566171406961)
XLA Ops:
  9.0 36.4 %all-gather.5.cloned.1.call-done = bf16[1024,1024]{1,0:T(8,128)(2,1)} async-done(((bf16[512,1024]{1,0:T(8,128)(2,1)}), bf16[1024,1024]{1,0:T(8,128)(2,1)}) %all-gather.5.cloned.1.call-update) | async-done | bytes 2097168 | tf_op jit(solution)/shard_map/all_gather | solution.py:79
  45.4 5.1 convolution_bitcast_fusion.1
  54.0 4.1 squeeze.41
  58.1 4.0 squeeze.40
  62.1 2.6 convert_element_type.72
  67.1 4.2 fusion.66
  71.4 19.3 %while.26 = (s32[]{:T(128)}, bf16[2,512,8,64]{1,3,2,0:T(8,128)(2,1)}, f32[2,8,512]{2,1,0:T(8,128)S(1)}, bf16[2,512,8,64]{1,3,2,0:T(8,128)(2,1)}, s32[2]{0:T(128)...) while((s32[]{:T(128)}, bf16[2,512,8,64]{1,3,2,0:T(8,128)(2,1)}, ...), condition=%wide.region_3.4_spmd, body=%wide.region_0.3_spmd.sunk | while | flops 562295296 | bytes 39981252 | solution.py:84
  72.6 3.1 fusion.124
  82.2 3.1 fusion.124
  94.3 3.3 fusion.79
  97.8 54.4 %reduce-scatter.5.cloned.1.call-done = f32[512,1024]{1,0:T(8,128)} async-done(((f32[1024,1024]{1,0:T(8,128)}), f32[512,1024]{1,0:T(8,128)}) %reduce-scatter.5.cloned.1.call-update) | async-done | bytes 2097168 | tf_op jit(solution)/shard_map/reduce_scatter | solution.py:86
  157.2 33.2 %all-gather.7.cloned.1.call-done = bf16[1024,1024]{1,0:T(8,128)(2,1)} async-done(((bf16[512,1024]{1,0:T(8,128)(2,1)}), bf16[1024,1024]{1,0:T(8,128)(2,1)}) %all-gather.7.cloned.1.call-update) | async-done | bytes 2097168 | tf_op jit(solution)/shard_map/all_gather | solution.py:95
  190.4 26.2 %multiply_convert_fusion.1 = (bf16[1024,2048]{1,0:T(8,128)(2,1)S(1)}, f32[1024,2048]{1,0:T(8,128)}, f32[1024,2048]{1,0:T(8,128)}) fusion(f32[2048]{0:T(1024)S(1)} %convert_element_type.75, bf16[1024,1024]{1,0:T(8,128)(2,1)} %all-gather.7.cloned.1.call-done, bf16[1024,2048]{1,0:T(8,128)(2,1)} %param.26), kind=kOutput, calls=%fused_computation.65 | convolution fusion | flops 4433379328 | bytes 27271168 | tf_op jit(solution)/shard_map/dot_general | solution.py:96
  218.5 6.0 fusion.80
  224.6 54.4 %reduce-scatter.7.cloned.1.call-done = f32[512,1024]{1,0:T(8,128)} async-done(((f32[1024,1024]{1,0:T(8,128)}), f32[512,1024]{1,0:T(8,128)}) %reduce-scatter.7.cloned.1.call-update) | async-done | bytes 2097168 | tf_op jit(solution)/shard_map/reduce_scatter | solution.py:101
  279.0 3.0 fusion.75
  288.9 33.2 %all-gather.9.cloned.1.call-done = bf16[1024,1024]{1,0:T(8,128)(2,1)} async-done(((bf16[512,1024]{1,0:T(8,128)(2,1)}), bf16[1024,1024]{1,0:T(8,128)(2,1)}) %all-gather.9.cloned.1.call-update) | async-done | bytes 2097168 | tf_op jit(solution)/shard_map/all_gather | solution.py:111
  322.1 14.4 %convert_reduce_fusion = (f32[2048]{0:T(1024)}, bf16[1024,2048]{1,0:T(8,128)(2,1)S(1)}) fusion(f32[1024,2048]{1,0:T(8,128)} %get-tuple-element.237, f32[1024,2048]{1,0:T(8,128)} %get-tuple-element.251, f32[2048]{0:T(1024)S(1)} %convert_element_type.75, bf16[1024,1024]{1,0:T(8,128)(2,1)} %all-gather.9.cloned.1.call-done, bf16[2048,1024]{1,0:T(8,128)(2,1)} %param.28), kind=kOutput, calls=%fused_computation.63 | convolution fusion | flops 4330616832 | bytes 27279360 | tf_op jit(solution)/shard_map/td,fd->tf/dot_general | solution.py:112
  338.6 6.1 fusion.81
  344.7 54.4 %reduce-scatter.9.cloned.1.call-done = f32[512,1024]{1,0:T(8,128)} async-done(((f32[1024,1024]{1,0:T(8,128)}), f32[512,1024]{1,0:T(8,128)}) %reduce-scatter.9.cloned.1.call-update) | async-done | bytes 2097168 | tf_op jit(solution)/shard_map/reduce_scatter | solution.py:117
  399.1 4.6 multiply_reduce_fusion.1
  407.0 33.2 %all-gather.11.cloned.1.call-done = bf16[1024,1024]{1,0:T(8,128)(2,1)} async-done(((bf16[512,1024]{1,0:T(8,128)(2,1)}), bf16[1024,1024]{1,0:T(8,128)(2,1)}) %all-gather.11.cloned.1.call-update) | async-done | bytes 2097168 | tf_op jit(solution)/shard_map/all_gather | solution.py:129
  440.2 4.1 convolution_convert_fusion
  444.3 4.0 reshape.163
  448.3 3.3 copy.55
  451.6 32.0 %while.27 = (s32[]{:T(128)}, bf16[2,512,8,64]{1,3,2,0:T(8,128)(2,1)}, bf16[2,512,8,64]{1,3,2,0:T(8,128)(2,1)}, bf16[2,512,8,64]{1,3,2,0:T(8,128)(2,1)}, bf16[2,5...) while((s32[]{:T(128)}, ...), condition=%wide.region_17.18_spmd, body=%wide.region_15.17_spmd.sunk | while | flops 1374155264 | bytes 111795640 | solution.py:135
  451.7 2.6 fusion.135
  455.6 3.0 multiply_reduce_fusion.6
  458.6 2.9 multiply_convert_fusion.3
  467.7 2.6 fusion.135
  471.6 3.0 multiply_reduce_fusion.6
  474.6 2.9 multiply_convert_fusion.3
  483.7 3.3 copy.58
  491.9 3.5 copy.72
  495.3 4.2 reshape.164
  499.5 3.3 copy.56
  507.7 6.9 convolution_bitcast_fusion.2
  514.7 10.9 %fusion.83 = f32[1024,2048]{1,0:T(8,128)} fusion(bf16[1024,1024]{1,0:T(8,128)(2,1)} %all-gather.7.cloned.1.call-done, bf16[1024,2048]{1,0:T(8,128)(2,1)} %copy-done.44), kind=kOutput, calls=%fused_computation.141 | convolution fusion | flops 4294967296 | bytes 14680064 | tf_op jit(solution)/shard_map/td,tf->df/dot_general | solution.py:123
  525.6 7.1 fusion.84
  536.0 5.4 convolution_bitcast_fusion
  542.1 40.3 %all-reduce = (f32[1024]{0:T(1024)}, f32[1024]{0:T(1024)}, f32[1024]{0:T(1024)}, f32[1024]{0:T(1024)}, f32[1024]{0:T(1024)}, /*index=5*/f32[1024]{0:T(1024)}) all-reduce(f32[1024]{0:T(1024)S(1)} %get-tuple-element.249, f32[1024]{0:T(1024)S(1)} %copy-done.30, ...), channel_id=1, replica_groups=mesh['dp'=16,'tensor'=2] {'dp','tensor'}, use_global_device_ids=true, to_apply=%region_25.26 | all-reduce | flops 6144 | bytes 49152 | tf_op jit(solution)/shard_map/psum | solution.py:163
  585.3 64.5 %all-reduce.1 = (f32[2,512]{1,0:T(2,128)}, f32[2048]{0:T(1024)}) all-reduce(f32[2,512]{1,0:T(2,128)S(1)} %pad_maximum_fusion.3, f32[2048]{0:T(1024)S(1)} %copy-done.33), channel_id=1, replica_groups=mesh['dp'=16,'tensor'=2] {'dp'}, use_global_device_ids=true, to_apply=%region_22.23 | all-reduce | flops 3072 | bytes 24576 | tf_op jit(solution)/shard_map/psum | solution.py:159
  649.8 3.8 add_add_fusion.3
  653.6 365.6 %all-reduce.5.cloned.1.call-done = (f32[3,1024,512]{1,2,0:T(8,128)}, f32[512,1024]{1,0:T(8,128)}, f32[1024,2048]{1,0:T(8,128)}, f32[2048,1024]{1,0:T(8,128)}) async-done(((f32[3,1024,512]{1,2,0:T(8,128)}, f32[512,1024]{1,0:T(8,128)}, f32[1024,2048]{1,0:T(8,128)}, f32[2048,1024]{1,0:T(8,128)}), (f32[3,1024,512]{1,2,0:T(8,128)}, f32[512,1024]{1,0:T(8,128)}, f32[1024,2048]{1,0:T(8,128)}, ...) | async-done | bytes 25165840 | tf_op jit(solution)/shard_map/psum | solution.py:159
  1019.3 6.6 copy.63
  1025.8 3.3 copy.113
  1029.1 8.0 copy.114
  1037.2 3.4 copy.115
  (205 shorter events, 74.9 us)
Async XLA Ops:
  7.2 38.2 %copy-start = (bf16[3,1024,512]{2,1,0:T(8,128)(2,1)S(1)}, bf16[3,1024,512]{2,1,0:T(8,128)(2,1)}, u32[]{:S(2)}) copy-start(bf16[3,1024,512]{2,1,0:T(8,128)(2,1)} %param.20) | copy-start | bytes 9437188
  7.2 38.2 %all-gather.5.cloned.1.call-start = ((), (), s32[]{:S(2)}) async-start(), calls=%async_computation.4 | async-start | bytes 3145728 | tf_op jit(solution)/shard_map/all_gather | solution.py:79
  7.9 144.2 %reduce-scatter.5.cloned.1.call-start = ((), (), s32[]{:S(2)}) async-start(), calls=%async_computation.5 | async-start | bytes 6291456 | tf_op jit(solution)/shard_map/reduce_scatter | solution.py:86
  64.7 6.7 copy-start.43
  75.7 2.0 copy-start.8
  90.6 3.7 copy-start.24
  94.3 57.8 %copy-start.36 = (f32[1024]{0:T(1024)S(1)}, f32[1024]{0:T(1024)}, u32[]{:S(2)}) copy-start(f32[1024]{0:T(1024)} %param.23) | copy-start | bytes 12292
  97.7 58.0 %copy-start.25 = (f32[1024]{0:T(1024)S(1)}, f32[1024]{0:T(1024)}, u32[]{:S(2)}) copy-start(f32[1024]{0:T(1024)} %param.24) | copy-start | bytes 12292
  97.7 58.0 %copy-start.32 = (f32[1024]{0:T(1024)S(1)}, f32[1024]{0:T(1024)}, u32[]{:S(2)}) copy-start(f32[1024]{0:T(1024)} %param.25) | copy-start | bytes 12292
  97.7 92.7 %all-gather.7.cloned.1.call-start = ((), (), s32[]{:S(2)}) async-start(), calls=%async_computation.6 | async-start | bytes 3145728 | tf_op jit(solution)/shard_map/all_gather | solution.py:95
  154.4 2.8 copy-start.35
  157.1 121.9 %reduce-scatter.7.cloned.1.call-start = ((), (), s32[]{:S(2)}) async-start(), calls=%async_computation.7 | async-start | bytes 6291456 | tf_op jit(solution)/shard_map/reduce_scatter | solution.py:101
  190.4 28.1 %copy-start.38 = (bf16[2048,1024]{1,0:T(8,128)(2,1)S(1)}, bf16[2048,1024]{1,0:T(8,128)(2,1)}, u32[]{:S(2)}) copy-start(bf16[2048,1024]{1,0:T(8,128)(2,1)} %param.28) | copy-start | bytes 12582916
  224.5 54.5 %copy-start.37 = (f32[1024]{0:T(1024)S(1)}, f32[1024]{0:T(1024)}, u32[]{:S(2)}) copy-start(f32[1024]{0:T(1024)} %param.29) | copy-start | bytes 12292
  224.6 57.9 %copy-start.26 = (f32[1024]{0:T(1024)S(1)}, f32[1024]{0:T(1024)}, u32[]{:S(2)}) copy-start(f32[1024]{0:T(1024)} %param.30) | copy-start | bytes 12292
  224.6 97.6 %all-gather.9.cloned.1.call-start = ((), (), s32[]{:S(2)}) async-start(), calls=%async_computation.8 | async-start | bytes 3145728 | tf_op jit(solution)/shard_map/all_gather | solution.py:111
  279.0 3.4 copy-start.12
  288.8 110.3 %reduce-scatter.9.cloned.1.call-start = ((), (), s32[]{:S(2)}) async-start(), calls=%async_computation.9 | async-start | bytes 6291456 | tf_op jit(solution)/shard_map/reduce_scatter | solution.py:117
  322.1 16.5 %copy-start.39 = (bf16[1024,2048]{1,0:T(8,128)(2,1)S(1)}, bf16[1024,2048]{1,0:T(8,128)(2,1)}, u32[]{:S(2)}) copy-start(bf16[1024,2048]{1,0:T(8,128)(2,1)} %param.26) | copy-start | bytes 12582916
  344.7 95.5 %all-gather.11.cloned.1.call-start = ((), (), s32[]{:S(2)}) async-start(), calls=%async_computation.10 | async-start | bytes 3145728 | tf_op jit(solution)/shard_map/all_gather | solution.py:129
  399.1 4.6 copy-start.4
  406.9 242.9 %reduce-scatter.11.cloned.1.call-start = ((), (), s32[]{:S(2)}) async-start(), calls=%async_computation.11 | async-start | bytes 6291456 | tf_op jit(solution)/shard_map/reduce_scatter | solution.py:144
  451.6 3.9 copy-start.7
  451.7 3.9 copy-start.9
  458.6 2.9 copy-start.1
  458.6 2.9 copy-start.20
  462.3 4.3 copy-start.21
  462.3 2.1 copy-start.22
  464.4 2.3 copy-start.15
  467.7 3.9 copy-start.7
  467.7 3.9 copy-start.9
  474.6 2.9 copy-start.1
  474.6 2.9 copy-start.20
  478.3 4.3 copy-start.21
  478.3 2.1 copy-start.22
  480.4 2.3 copy-start.15
  514.6 504.7 %all-reduce.5.cloned.1.call-start = ((), (), s32[]{:S(2)}) async-start(), calls=%async_computation.12 | async-start | bytes 50331648 | tf_op jit(solution)/shard_map/psum | solution.py:159
  514.6 11.0 %copy-start.41 = (bf16[1024,1024]{1,0:T(8,128)(2,1)S(1)}, bf16[1024,1024]{1,0:T(8,128)(2,1)}, u32[]{:S(2)}) copy-start(bf16[1024,1024]{1,0:T(8,128)(2,1)} %all-gather.9.cloned.1.call-done) | copy-start | bytes 6291460
  514.6 11.0 %copy-start.46 = (bf16[1024,2048]{1,0:T(8,128)(2,1)S(1)}, bf16[1024,2048]{1,0:T(8,128)(2,1)}, u32[]{:S(2)}) copy-start(bf16[1024,2048]{1,0:T(8,128)(2,1)} %copy-done.45) | copy-start | bytes 12582916
  525.6 7.1 copy-start.11
  525.6 7.1 copy-start.42
  532.7 2.6 copy-start.13
  532.7 2.6 copy-start.18
  532.7 2.6 copy-start.19
  532.7 3.3 copy-start.40
  541.4 43.9 %copy-start.33 = (f32[2048]{0:T(1024)S(1)}, f32[2048]{0:T(1024)}, u32[]{:S(2)}) copy-start(f32[2048]{0:T(1024)} %get-tuple-element.227) | copy-start | bytes 24580
  1025.8 11.4 %slice-start = ((s8[8388608]{0:T(1024)(128)(4,1)}), s8[4194304]{0:T(1024)(128)(4,1)S(1)}, s32[]{:S(2)}) async-start(s8[8388608]{0:T(1024)(128)(4,1)} %bitcast.157), calls=%async_computation.13 | async-start | bytes 8388608
  1029.1 8.0 slice-start.1
  (23 other events, 29.9 us)
Sparse Core Ops, SparseCore 0:
  9.6 35.8 all-gather.4
  97.8 54.2 reduce-scatter.4
  157.2 33.1 all-gather.6
  224.7 54.3 reduce-scatter.6
  289.0 33.1 all-gather.8
  344.8 54.2 reduce-scatter.8
  407.0 33.1 all-gather.10
  514.7 55.0 reduce-scatter.10
  575.8 443.4 all-reduce.4
where the time goes:
time: 1050 us
  waiting for transfers between devices  666 us (63%)
  matrix products  129 us (12%)
  blocking collectives  105 us (10%)
  local copies, waits for them, and re-layouts  90.7 us (9%)
  other arithmetic  42.2 us (4%)
  between operations  14.4 us (1%)
    psum x1, waiting for transfers between devices, body(): lax.psum((grad_qkv, grad_bias_qv, grad_out, grad_up, grad_up_bias, grad_d...  366 us
    psum x1, blocking collectives, body(): lax.psum((grad_qkv, grad_bias_qv, grad_out, grad_up, grad_up_bias, grad_d...  64.5 us
    reduce_scatter x1, waiting for transfers between devices, body(): lax.psum_scatter(jnp.dot(active_low, down_weight, preferred_element_type=...  54.4 us
    reduce_scatter x1, waiting for transfers between devices, body(): lax.psum_scatter(jnp.einsum('tf,df->td', grad_up_low, up_weight, preferre...  54.4 us
    reduce_scatter x1, waiting for transfers between devices, body(): lax.psum_scatter(jnp.dot(mixed, out_weight, preferred_element_type=jnp.fl...  54.4 us
    psum x1, blocking collectives, body(): lax.psum((jnp.sum(grad_one, axis=0), grad_gain_one, grad_shift_one, jnp.s...  40.3 us
    all_gather x1, waiting for transfers between devices, body(): input_all = lax.all_gather(layer_input, 'tensor', axis=0, tiled=True)  36.4 us
    all_gather x1, waiting for transfers between devices, body(): grad_two_all = lax.all_gather(grad_two_low, 'tensor', axis=0, tiled=True)  33.2 us
  transfers between devices with their start and end apart: 9, of which 8 were waited for; matrix products, arithmetic and copies ran while one was open for 3% of the time, Pallas kernels for 0%

commit v1 on v0

v1 whole, which is shorter than its diff:
```python
import functools

import jax
import jax.numpy as jnp
from jax import lax
from jax.experimental import pallas as pl
from jax.experimental.pallas import tpu as pltpu
from jax.sharding import PartitionSpec as P

HD = 64
F32 = jnp.float32
BF16 = jnp.bfloat16
NEG = -1000000000.0

ERFC_P = 0.3275911
ERFC_C = (
    0.18510853909898187,
    0.17995808540893535,
    0.21032499893163595,
    0.011746556912990477,
    0.4777504794974274,
    -0.4314195259659222,
    0.5110037999525718,
    -0.14447299033990682,
)


def gelu_both(up):
    size = jnp.abs(up)
    t = 1.0 / (1.0 + (ERFC_P * 0.5**0.5) * size)
    poly = jnp.full_like(t, 0.5 * ERFC_C[-1])
    for c in ERFC_C[-2::-1]:
        poly = poly * t + 0.5 * c
    density = jnp.exp(-0.5 * up * up)
    tail = poly * t * density
    phi = jnp.where(up > 0, 1.0 - tail, tail)
    return up * phi, phi + up * (density * 0.3989422804014327)


def contract(a, b, ca, cb):
    return lax.dot_general(a, b, (((ca,), (cb,)), ((), ())), preferred_element_type=F32)


def attend_kernel(len_ref, q_ref, k_ref, v_ref, o_ref, lse_ref):
    length = len_ref[0]
    q, k, v = q_ref[...], k_ref[...], v_ref[...]
    rows, width = q.shape
    head = lax.broadcasted_iota(jnp.int32, (rows, width), 1) // HD
    key_pos = lax.broadcasted_iota(jnp.int32, (rows, rows), 0)
    out = None
    for h in range(width // HD):
        mine = head == h
        kh = jnp.where(mine, k, jnp.zeros_like(k)) * jnp.asarray(HD**-0.5, BF16)
        s = jnp.where(key_pos < length, contract(kh, q, 1, 1), F32(NEG))
        top = jnp.max(s, axis=0, keepdims=True)
        e = jnp.exp(s - top)
        total = jnp.sum(e, axis=0, keepdims=True)
        lse_ref[0, h : h + 1, :] = top + jnp.log(total)
        p = (e * (1.0 / total)).astype(BF16)
        o = contract(p, v, 0, 0)
        out = o if out is None else jnp.where(mine, o, out)
    o_ref[...] = out.astype(BF16)


def attend(length, q, k, v):
    rows, width = q.shape
    wide = min(2 * HD, width)
    steps = width // wide
    spec = pl.BlockSpec((rows, wide), lambda i: (0, i))
    return pl.pallas_call(
        attend_kernel,
        grid=(steps,),
        in_specs=[pl.BlockSpec(memory_space=pltpu.SMEM), spec, spec, spec],
        out_specs=[spec, pl.BlockSpec((1, wide // HD, rows), lambda i: (i, 0, 0))],
        out_shape=[
            jax.ShapeDtypeStruct((rows, width), BF16),
            jax.ShapeDtypeStruct((steps, wide // HD, rows), F32),
        ],
        compiler_params=pltpu.CompilerParams(vmem_limit_bytes=32 * 2**20),
        cost_estimate=pl.CostEstimate(
            flops=16 * rows * rows * width,
            bytes_accessed=8 * rows * width,
            transcendentals=rows * rows * width // HD,
        ),
        name="attend",
    )(length, q, k, v)


def attend_back_kernel(
    len_ref, q_ref, k_ref, v_ref, g_ref, lse_ref, dq_ref, dk_ref, dv_ref
):
    length = len_ref[0]
    q, k, v, g = q_ref[...], k_ref[...], v_ref[...], g_ref[...]
    rows, width = q.shape
    head = lax.broadcasted_iota(jnp.int32, (rows, width), 1) // HD
    head_t = lax.broadcasted_iota(jnp.int32, (width, rows), 0) // HD
    key_pos = lax.broadcasted_iota(jnp.int32, (rows, rows), 0)
    dq = dk = dv = None
    for h in range(width // HD):
        mine = head == h
        kh = jnp.where(mine, k, jnp.zeros_like(k)) * jnp.asarray(HD**-0.5, BF16)
        vh = jnp.where(mine, v, jnp.zeros_like(v))
        s = jnp.where(key_pos < length, contract(kh, q, 1, 1), F32(NEG))
        p = jnp.exp(s - lse_ref[0, h : h + 1, :])
        dp = contract(vh, g, 1, 1)
        dvh = contract(p.astype(BF16), g, 1, 0)
        center = jnp.sum(p * dp, axis=0, keepdims=True)
        ds = (p * (dp - center)).astype(BF16)
        dkh = contract(ds, q, 1, 0)
        dqh = contract(k, ds, 0, 0)
        dv = dvh if dv is None else jnp.where(mine, dvh, dv)
        dk = dkh if dk is None else jnp.where(mine, dkh, dk)
        dq = dqh if dq is None else jnp.where(head_t == h, dqh, dq)
    dq_ref[...] = (dq * (HD**-0.5)).T.astype(BF16)
    dk_ref[...] = (dk * (HD**-0.5)).astype(BF16)
    dv_ref[...] = dv.astype(BF16)


def attend_back(length, q, k, v, g, lse):
    rows, width = q.shape
    wide = min(2 * HD, width)
    spec = pl.BlockSpec((rows, wide), lambda i: (0, i))
    out = jax.ShapeDtypeStruct((rows, width), BF16)
    return pl.pallas_call(
        attend_back_kernel,
        grid=(width // wide,),
        in_specs=[pl.BlockSpec(memory_space=pltpu.SMEM), spec, spec, spec, spec]
        + [pl.BlockSpec((1, wide // HD, rows), lambda i: (i, 0, 0))],
        out_specs=[spec, spec, spec],
        out_shape=[out, out, out],
        compiler_params=pltpu.CompilerParams(vmem_limit_bytes=48 * 2**20),
        cost_estimate=pl.CostEstimate(
            flops=40 * rows * rows * width,
            bytes_accessed=14 * rows * width,
            transcendentals=rows * rows * width // HD,
        ),
        name="attend_back",
    )(length, q, k, v, g, lse)


class Moves:
    def __init__(self, n_dp, n_tensor):
        self.n_dp, self.n_tensor = n_dp, n_tensor
        self.dp = lax.axis_index("dp")
        self.core = self.dp & 1
        self.chip_bits = [b for b in (2, 4, 8, 16, 32, 64) if b < n_dp]

    def bit(self, mask):
        return (self.dp // mask) & 1

    def over_dp(self, a, mask):
        return lax.ppermute(a, "dp", [(i, i ^ mask) for i in range(self.n_dp)])

    def over_tensor(self, a, mask):
        return lax.ppermute(
            a, "tensor", [(i, i ^ mask) for i in range(self.n_tensor)]
        )

    def join(self, a, b, bit, axis):
        low, high = jnp.where(bit == 0, a, b), jnp.where(bit == 0, b, a)
        return jnp.concatenate([low, high], axis=axis)

    def fetch(self, w, masks, axis):
        index = sum(self.bit(m) << i for i, m in enumerate(masks))
        size = w.shape[axis] >> len(masks)
        piece = lax.dynamic_slice_in_dim(w, index * size, size, axis)
        parts = []
        for d in range(1, self.n_tensor):
            got = self.over_tensor(piece, d)
            for m in masks:
                got = self.join(got, self.over_dp(got, m), self.bit(m), axis)
            parts.append(got)
        return parts

    def reduce(self, parts):
        parts = list(parts)
        step = self.n_tensor // 2
        while step:
            for d in range(step):
                got = self.over_tensor(parts[d + step], step)
                parts[d] = add(parts[d], got)
            step //= 2
        own = parts[0]
        for m in self.chip_bits:
            half = own.shape[0] // 2
            bit = self.bit(m)
            send = lax.dynamic_slice_in_dim(own, (1 - bit) * half, half, 0)
            keep = lax.dynamic_slice_in_dim(own, bit * half, half, 0)
            own = add(keep, self.over_dp(send, m))
        for m in reversed(self.chip_bits):
            own = self.join(own, self.over_dp(own, m), self.bit(m), 0)
        return own


def add(a, b):
    return (a.astype(F32) + b.astype(F32)).astype(BF16)


def layer_norm(hidden):
    center = hidden - jnp.mean(hidden, axis=-1, keepdims=True)
    spread = jnp.mean(center * center, axis=-1, keepdims=True)
    scale = lax.rsqrt(spread + 1e-05)
    return center * scale, scale


def layer_norm_back(grad, normal, scale, gain):
    gy = grad * gain
    mean = jnp.mean(gy, axis=-1, keepdims=True)
    along = jnp.mean(gy * normal, axis=-1, keepdims=True)
    return scale * (gy - mean - normal * along)


def body(
    n_dp,
    n_tensor,
    layer_input,
    qkv_weight,
    qv_bias,
    out_weight,
    out_bias,
    norm1_gain,
    norm1_shift,
    up_weight,
    up_bias,
    down_weight,
    down_bias,
    norm2_gain,
    norm2_shift,
    lengths,
    grad_output,
):
    mv = Moves(n_dp, n_tensor)
    parts = range(n_tensor)
    width = layer_input.shape[1]
    half = width // 2
    core = mv.core
    hw = qkv_weight.shape[2]
    fw = up_weight.shape[1]
    x = layer_input
    length = lax.dynamic_slice_in_dim(lengths, lax.axis_index("tensor"), 1, 0)

    def swap(a):
        return mv.over_dp(a, 1)

    def my_half(a):
        return lax.dynamic_slice_in_dim(a, core * half, half, 1)

    def swap_half(a):
        return swap(lax.dynamic_slice_in_dim(a, (1 - core) * half, half, 1))

    qkv = [qkv_weight] + mv.fetch(qkv_weight, (1, 2, 4), 1)
    bias_pack = jnp.concatenate([qv_bias.reshape(-1), up_bias.astype(F32)])
    biases = [bias_pack] + [mv.over_tensor(bias_pack, d) for d in range(1, n_tensor)]
    out_w = [out_weight] + mv.fetch(out_weight, (1, 4, 2), 0)
    up_w = [up_weight] + mv.fetch(up_weight, (1, 2, 4), 0)
    down_w = [down_weight] + mv.fetch(down_weight, (1, 4, 2), 0)
    q_bias = [b[:hw] for b in biases]
    v_bias = [b[hw : 2 * hw] for b in biases]
    up_b = [b[2 * hw :] for b in biases]

    x_mine, x_sib = my_half(x), swap_half(x)
    q, k, v, mixed, lse = [], [], [], [], []
    for d in parts:
        q.append((contract(x, qkv[d][0], 1, 0) + q_bias[d]).astype(BF16))
        k.append(contract(x, qkv[d][1], 1, 0).astype(BF16))
        v.append((contract(x, qkv[d][2], 1, 0) + v_bias[d]).astype(BF16))
        m, l = attend(length, q[d], k[d], v[d])
        mixed.append(m)
        lse.append(l)
    hidden_one = x.astype(F32) + out_bias
    for d in parts:
        hidden_one = hidden_one + contract(mixed[d], out_w[d], 1, 0)
    normal_one, scale_one = layer_norm(hidden_one)
    normed_one = normal_one * norm1_gain + norm1_shift
    normed_b = normed_one.astype(BF16)
    nb_mine, nb_sib = my_half(normed_b), swap_half(normed_b)
    act, slope, act_sib = [], [], []
    for d in parts:
        a, s = gelu_both(contract(normed_b, up_w[d], 1, 0) + up_b[d])
        act.append(a.astype(BF16))
        slope.append(s.astype(BF16))
        act_sib.append(swap(act[d]))
    mixed_sib = [swap(m) for m in mixed]
    hidden_two = normed_one + down_bias
    for d in parts:
        hidden_two = hidden_two + contract(act[d], down_w[d], 1, 0)
    normal_two, scale_two = layer_norm(hidden_two)
    result = (normal_two * norm2_gain + norm2_shift).astype(BF16)

    grad = grad_output.astype(F32)
    g_gain2 = jnp.sum(grad * normal_two, axis=0)
    g_shift2 = jnp.sum(grad, axis=0)
    g_two = layer_norm_back(grad, normal_two, scale_two, norm2_gain)
    g_down_bias = jnp.sum(g_two, axis=0)
    g_two_b = g_two.astype(BF16)
    g2_mine, g2_sib = my_half(g_two_b), swap_half(g_two_b)

    order = list(parts)[::-1]
    down_sum = []
    chunk = fw // 2
    for lo in (0, chunk):
        made = [None] * n_tensor
        for d in order:
            made[d] = (
                contract(act[d][:, lo : lo + chunk], g2_mine, 0, 0)
                + contract(act_sib[d][:, lo : lo + chunk], g2_sib, 0, 0)
            ).astype(BF16)
        down_sum.append(mv.reduce(made))
    g_up, g_up_sib = [None] * n_tensor, [None] * n_tensor
    for d in order:
        g_up[d] = (contract(g_two_b, down_w[d], 1, 1) * slope[d]).astype(BF16)
        g_up_sib[d] = swap(g_up[d])
    g_up_bias = [jnp.sum(g.astype(F32), axis=0) for g in g_up]
    up_sum = []
    chunk = half // 2
    for lo in (0, chunk):
        made = [None] * n_tensor
        for d in order:
            made[d] = (
                contract(nb_mine[:, lo : lo + chunk], g_up[d], 0, 0)
                + contract(nb_sib[:, lo : lo + chunk], g_up_sib[d], 0, 0)
            ).astype(BF16)
        up_sum.append(mv.reduce(made))
    g_one_in = g_two
    for d in parts:
        g_one_in = g_one_in + contract(g_up[d], up_w[d], 1, 1)
    g_gain1 = jnp.sum(g_one_in * normal_one, axis=0)
    g_shift1 = jnp.sum(g_one_in, axis=0)
    g_one = layer_norm_back(g_one_in, normal_one, scale_one, norm1_gain)
    g_out_bias = jnp.sum(g_one, axis=0)
    g_one_b = g_one.astype(BF16)
    g1_mine, g1_sib = my_half(g_one_b), swap_half(g_one_b)
    made = [None] * n_tensor
    for d in order:
        made[d] = (
            contract(mixed[d], g1_mine, 0, 0) + contract(mixed_sib[d], g1_sib, 0, 0)
        ).astype(BF16)
    out_sum = mv.reduce(made)

    g_proj, g_proj_sib = [None] * n_tensor, [None] * n_tensor
    for d in order:
        g_mixed = contract(g_one_b, out_w[d], 1, 1).astype(BF16)
        g_proj[d] = attend_back(length, q[d], k[d], v[d], g_mixed, lse[d])
        g_proj_sib[d] = [swap(g) for g in g_proj[d]]
    qkv_sum = []
    for c in range(3):
        made = [None] * n_tensor
        for d in order:
            made[d] = (
                contract(x_mine, g_proj[d][c], 0, 0)
                + contract(x_sib, g_proj_sib[d][c], 0, 0)
            ).astype(BF16)
        qkv_sum.append(mv.reduce(made))
    g_input = g_one
    for d in parts:
        for c in range(3):
            g_input = g_input + contract(g_proj[d][c], qkv[d][c], 1, 1)

    whole = jnp.concatenate(
        [g_out_bias, g_gain1, g_shift1, g_down_bias, g_gain2, g_shift2]
    )
    packs = []
    for d in parts:
        gq = jnp.sum(g_proj[d][0].astype(F32), axis=0)
        gv = jnp.sum(g_proj[d][2].astype(F32), axis=0)
        packs.append(jnp.concatenate([whole, gq, gv, g_up_bias[d]]))
    step = n_tensor // 2
    while step:
        for d in range(step):
            packs[d] = packs[d] + mv.over_tensor(packs[d + step], step)
        step //= 2
    small = packs[0]
    for m in [1] + mv.chip_bits:
        small = small + mv.over_dp(small, m)

    def both_cores(sums, columns):
        pieces = [mv.join(s, swap(s), core, 1 if columns else 0) for s in sums]
        return pieces

    grad_down = jnp.concatenate(
        [p.astype(F32) for p in both_cores(down_sum, True)], axis=0
    )
    ups = [(s, swap(s)) for s in up_sum]
    mine = jnp.concatenate([a for a, _ in ups], axis=0)
    theirs = jnp.concatenate([b for _, b in ups], axis=0)
    grad_up = mv.join(mine, theirs, core, 0).astype(F32)
    grad_out = both_cores([out_sum], True)[0].astype(F32)
    grad_qkv = jnp.stack([p.astype(F32) for p in both_cores(qkv_sum, False)])
    vec = [small[i * width : (i + 1) * width] for i in range(6)]
    rest = small[6 * width :]
    grad_qv_bias = rest[: 2 * hw].reshape(2, hw)
    return (
        result,
        g_input,
        grad_qkv,
        grad_qv_bias,
        grad_out,
        vec[0],
        vec[1],
        vec[2],
        grad_up,
        rest[2 * hw :],
        grad_down,
        vec[3],
        vec[4],
        vec[5],
    )


def solution(mesh):
    return jax.shard_map(
        functools.partial(body, mesh.shape["dp"], mesh.shape["tensor"]),
        mesh=mesh,
        in_specs=(
            P(("dp", "tensor"), None),
            P(None, None, "tensor"),
            P(None, "tensor"),
            P("tensor", None),
            P(),
            P(),
            P(),
            P(None, "tensor"),
            P("tensor"),
            P("tensor", None),
            P(),
            P(),
            P(),
            P("dp"),
            P(("dp", "tensor"), None),
        ),
        out_specs=(
            P(("dp", "tensor"), None),
            P(("dp", "tensor"), None),
            P(None, None, "tensor"),
            P(None, "tensor"),
            P("tensor", None),
            P(),
            P(),
            P(),
            P(None, "tensor"),
            P("tensor"),
            P("tensor", None),
            P(),
            P(),
            P(),
        ),
        check_vma=False,
    )
```

time: 1050 us -> 690 us (0.66)
  waiting for transfers between devices: 666 us -> 372 us
  blocking collectives: 105 us -> 0 us
  starting transfers between devices: 0.37 us -> 86.4 us
  local copies, waits for them, and re-layouts: 90.7 us -> 20.8 us
  Pallas kernels: 0 us -> 32 us
  matrix products: 129 us -> 115 us
  between operations: 14.4 us -> 3.42 us
    ppermute x0 -> x102, waiting for transfers between devices: none -> 372 us  [the longest x88 257 us: over_dp(): return lax.ppermute(a, 'dp', [(i, i ^ mask) for i in range(self.n_dp)])]
    psum x1 -> x0, waiting for transfers between devices: 366 us -> none  [body(): lax.psum((grad_qkv, grad_bias_qv, grad_out, grad_up, grad_up_bias, grad_d...]
    reduce_scatter x4 -> x0, waiting for transfers between devices: 163 us -> none  [the longest x1 54.4 us: body(): lax.psum_scatter(jnp.dot(active_low, down_weight, preferred_element_type=...]
    all_gather x4 -> x0, waiting for transfers between devices: 136 us -> none  [the longest x1 36.4 us: body(): input_all = lax.all_gather(layer_input, 'tensor', axis=0, tiled=True)]
    psum x2 -> x0, blocking collectives: 105 us -> none  [the longest x1 64.5 us: body(): lax.psum((grad_qkv, grad_bias_qv, grad_out, grad_up, grad_up_bias, grad_d...]
    ppermute x0 -> x102, starting transfers between devices: none -> 86.4 us  [the longest x88 67.8 us: over_dp(): return lax.ppermute(a, 'dp', [(i, i ^ mask) for i in range(self.n_dp)])]
    pallas_call x0 -> x4, Pallas kernels: none -> 32 us  [the longest x2 18.6 us: attend_back(): pl.pallas_call(attend_back_kernel, grid=(width // wide,), in_specs=[pl.Bl...]
    unnamed x77 -> x139, local copies, waits for them, and re-layouts: 31.6 us -> 7.36 us
  transfers between devices with their start and end apart: 9 -> 102, of which waited for: 8 -> 56; matrix products, arithmetic and copies ran while one was open for 3% -> 24% of each run, Pallas kernels for 0% -> 5%
where the time goes in v1:
time: 690 us; the launch traced here: 680 us
  waiting for transfers between devices  372 us (54%)
  matrix products  115 us (17%)
  starting transfers between devices  86.4 us (13%)
  other arithmetic  50.9 us (7%)
  Pallas kernels  32 us (5%)
  local copies, waits for them, and re-layouts  20.8 us (3%)
    ppermute x88, waiting for transfers between devices, over_dp(): return lax.ppermute(a, 'dp', [(i, i ^ mask) for i in range(self.n_dp)])  257 us
    dot_general x56, matrix products, contract(): lax.dot_general(a, b, (((ca,), (cb,)), ((), ())), preferred_element_type=...  115 us
    ppermute x14, waiting for transfers between devices, over_tensor(): lax.ppermute(a, 'tensor', [(i, i ^ mask) for i in range(self.n_tensor)])  115 us
    ppermute x88, starting transfers between devices, over_dp(): return lax.ppermute(a, 'dp', [(i, i ^ mask) for i in range(self.n_dp)])  67.8 us
    pallas_call x2, Pallas kernels, attend_back(): pl.pallas_call(attend_back_kernel, grid=(width // wide,), in_specs=[pl.Bl...  18.6 us
    ppermute x14, starting transfers between devices, over_tensor(): lax.ppermute(a, 'tensor', [(i, i ^ mask) for i in range(self.n_tensor)])  18.6 us
    concatenate x1, other arithmetic, body(): jnp.concatenate([p.astype(F32) for p in both_cores(down_sum, True)], axis=0)  17.8 us
  transfers between devices with their start and end apart: 102, of which 56 were waited for; matrix products, arithmetic and copies ran while one was open for 24% of the time, Pallas kernels for 5%

profile of v1, /device:TPU:0, one launch (start us, length us, event | category | flops | bytes accessed | tf_op | source)
XLA Modules:
  0.0 680.1 jit_solution(5925460861060351777)
XLA Ops:
  16.3 6.9 %attend.2 = (bf16[512,512]{1,0:T(8,128)(2,1)}, f32[4,2,512]{2,1,0:T(2,128)S(1)}) custom-call(s32[1]{0:T(128)} %dynamic_slice.183.len_ref, bf16[512,512]{1,0:T(8,128)(2,1)S(1)} %fusion.23.q_ref, bf16[512,512]{1,0:T(8,128)(2,1)S(1)} %convolution_convert_fusion.3.k_ref, bf16[512,512]{1,0:T(8,128)(2,1)S(1)} %fusion.24.v_ref), custom_call_target="tpu_custom_call" | custom-call | flops 2147483648 | bytes 2097152 | tf_op jit(solution)/shard_map/attend/pallas_call | solution.py:70
  23.8 3.1 fusion.160
  39.9 7.2 %collective-permute-done.13 = bf16[256,1024]{1,0:T(8,128)(2,1)S(1)} collective-permute-done((bf16[256,1024]{1,0:T(8,128)(2,1)}, bf16[256,1024]{1,0:T(8,128)(2,1)S(1)}, u32[]{:S(2)}, u32[]{:S(2)}) %collective-permute-start.13) | collective-permute-done | bytes 524320 | tf_op jit(solution)/shard_map/ppermute | solution.py:155
  53.2 25.6 %collective-permute-done.2 = bf16[3,256,512]{2,1,0:T(8,128)(2,1)S(1)} collective-permute-done((bf16[3,256,512]{2,1,0:T(8,128)(2,1)S(1)}, bf16[3,256,512]{2,1,0:T(8,128)(2,1)S(1)}, u32[]{:S(2)}, u32[]{:S(2)}) %collective-permute-start.2) | collective-permute-done | bytes 786464 | tf_op jit(solution)/shard_map/ppermute | solution.py:152
  81.7 17.4 %collective-permute-done.11 = bf16[256,2048]{1,0:T(8,128)(2,1)S(1)} collective-permute-done((bf16[256,2048]{1,0:T(8,128)(2,1)S(1)}, bf16[256,2048]{1,0:T(8,128)(2,1)S(1)}, u32[]{:S(2)}, u32[]{:S(2)}) %collective-permute-start.11) | collective-permute-done | bytes 1048608 | tf_op jit(solution)/shard_map/ppermute | solution.py:152
  100.5 38.6 %collective-permute-done.15 = bf16[512,1024]{1,0:T(8,128)(2,1)S(1)} collective-permute-done((bf16[512,1024]{1,0:T(8,128)(2,1)S(1)}, bf16[512,1024]{1,0:T(8,128)(2,1)S(1)}, u32[]{:S(2)}, u32[]{:S(2)}) %collective-permute-start.15) | collective-permute-done | bytes 1048608 | tf_op jit(solution)/shard_map/ppermute | solution.py:152
  144.2 6.4 attend.3
  154.9 7.8 %multiply_convert_fusion.3 = (bf16[512,2048]{1,0:T(8,128)(2,1)S(1)}, f32[512,2048]{1,0:T(8,128)}) fusion(f32[2048]{0:T(1024)S(1)} %copy-done.53, bf16[512,1024]{1,0:T(8,128)(2,1)S(1)} %fusion.22, bf16[1024,2048]{1,0:T(8,128)(2,1)S(1)} %copy-done.50), kind=kOutput, calls=%fused_computation.23 | convolution fusion | flops 2176843776 | bytes 11542528 | tf_op jit(solution)/shard_map/dot_general | solution.py:41
  162.7 3.6 fusion.161
  166.4 12.5 %collective-permute-done.12 = bf16[512,2048]{1,0:T(8,128)(2,1)S(1)} collective-permute-done((bf16[512,2048]{1,0:T(8,128)(2,1)S(1)}, bf16[512,2048]{1,0:T(8,128)(2,1)S(1)}, u32[]{:S(2)}, u32[]{:S(2)}) %collective-permute-start.12) | collective-permute-done | bytes 2097184 | tf_op jit(solution)/shard_map/ppermute | solution.py:152
  180.1 7.5 %multiply_convert_fusion.2 = (bf16[512,2048]{1,0:T(8,128)(2,1)S(1)}, f32[512,2048]{1,0:T(8,128)}) fusion(f32[2048]{0:T(1024)S(1)} %slice.156, bf16[512,1024]{1,0:T(8,128)(2,1)S(1)} %fusion.22, bf16[512,2048]{1,0:T(8,128)(2,1)S(1)} %get-tuple-element.51, bf16[512,2048]{1,0:T(8,128)(2,1)S(1)} %get-tuple-element.50), kind=kOutput, calls=%fused_computation.16 | convolution fusion | flops 2185232384 | bytes 11542528 | tf_op jit(solution)/shard_map/dot_general | solution.py:41
  196.9 10.6 %convert_reduce_fusion = (f32[2048]{0:T(1024)S(1)}, bf16[512,2048]{1,0:T(8,128)(2,1)S(1)}) fusion(f32[512,2048]{1,0:T(8,128)} %get-tuple-element.149, f32[2048]{0:T(1024)S(1)} %slice.156, bf16[512,1024]{1,0:T(8,128)(2,1)S(1)} %convert_element_type.477, bf16[1024,1024]{1,0:T(8,128)(2,1)S(1)} %get-tuple-element.49, bf16[1024,1024]{1,0:T(8,128)(2,1)S(1)} %get-tuple-element.48), kind=kOutput, calls=%fused_computation.10 | convolution fusion | flops 2192570368 | bytes 11550720 | tf_op jit(solution)/shard_map/dot_general | solution.py:41
  207.5 9.0 %convert_reduce_fusion.1 = (f32[2048]{0:T(1024)S(1)}, bf16[512,2048]{1,0:T(8,128)(2,1)S(1)}) fusion(f32[512,2048]{1,0:T(8,128)} %get-tuple-element.147, f32[2048]{0:T(1024)S(1)} %copy-done.53, bf16[512,1024]{1,0:T(8,128)(2,1)S(1)} %convert_element_type.477, bf16[2048,1024]{1,0:T(8,128)(2,1)S(1)} %copy-done.49), kind=kOutput, calls=%fused_computation.11 | convolution fusion | flops 2184181760 | bytes 11550720 | tf_op jit(solution)/shard_map/dot_general | solution.py:41
  219.0 3.1 multiply_reduce_fusion
  225.8 8.8 %attend_back.2 = (bf16[512,512]{1,0:T(8,128)(2,1)S(1)}, bf16[512,512]{1,0:T(8,128)(2,1)S(1)}, bf16[512,512]{1,0:T(8,128)(2,1)S(1)}) custom-call(s32[1]{0:T(128)} %dynamic_slice.183.len_ref, bf16[512,512]{1,0:T(8,128)(2,1)S(1)} %fusion.23.q_ref, bf16[512,512]{1,0:T(8,128)(2,1)S(1)} %convolution_convert_fusion.3.k_ref, bf16[512,512]{1,0:T(8,128)(2,1)S(1)} %copy-done.3, ...), custom_call_target="tpu_custom_call" | custom-call | flops 5368709120 | bytes 3670016 | tf_op jit(solution)/shard_map/attend_back/pallas_call | solution.py:124
  238.1 9.8 %attend_back.3 = (bf16[512,512]{1,0:T(8,128)(2,1)S(1)}, bf16[512,512]{1,0:T(8,128)(2,1)}, bf16[512,512]{1,0:T(8,128)(2,1)S(1)}) custom-call(s32[1]{0:T(128)} %dynamic_slice.183.len_ref, bf16[512,512]{1,0:T(8,128)(2,1)S(1)} %fusion.86.q_ref, bf16[512,512]{1,0:T(8,128)(2,1)S(1)} %fusion.46.k_ref, bf16[512,512]{1,0:T(8,128)(2,1)S(1)} %fusion.47.v_ref, ...), custom_call_target="tpu_custom_call" | custom-call | flops 5368709120 | bytes 3670016 | tf_op jit(solution)/shard_map/attend_back/pallas_call | solution.py:124
  308.6 9.1 %collective-permute-done.40 = bf16[512,512]{1,0:T(8,128)(2,1)S(1)} collective-permute-done((bf16[512,512]{1,0:T(8,128)(2,1)S(1)}, bf16[512,512]{1,0:T(8,128)(2,1)S(1)}, u32[]{:S(2)}, u32[]{:S(2)}) %collective-permute-start.40) | collective-permute-done | bytes 524320 | tf_op jit(solution)/shard_map/ppermute | solution.py:155
  321.4 7.7 %collective-permute-done.30 = bf16[512,512]{1,0:T(8,128)(2,1)S(1)} collective-permute-done((bf16[512,512]{1,0:T(8,128)(2,1)S(1)}, bf16[512,512]{1,0:T(8,128)(2,1)S(1)}, u32[]{:S(2)}, u32[]{:S(2)}) %collective-permute-start.30) | collective-permute-done | bytes 524320 | tf_op jit(solution)/shard_map/ppermute | solution.py:155
  332.7 7.6 %collective-permute-done.20 = bf16[512,512]{1,0:T(8,128)(2,1)S(1)} collective-permute-done((bf16[512,512]{1,0:T(8,128)(2,1)S(1)}, bf16[512,512]{1,0:T(8,128)(2,1)S(1)}, u32[]{:S(2)}, u32[]{:S(2)}) %collective-permute-start.20) | collective-permute-done | bytes 524320 | tf_op jit(solution)/shard_map/ppermute | solution.py:155
  343.6 7.1 %collective-permute-done.56 = bf16[512,512]{1,0:T(8,128)(2,1)S(1)} collective-permute-done((bf16[512,512]{1,0:T(8,128)(2,1)S(1)}, bf16[512,512]{1,0:T(8,128)(2,1)S(1)}, u32[]{:S(2)}, u32[]{:S(2)}) %collective-permute-start.56) | collective-permute-done | bytes 524320 | tf_op jit(solution)/shard_map/ppermute | solution.py:155
  354.4 5.5 collective-permute-done.31
  361.8 3.8 collective-permute-done.21
  371.7 3.4 collective-permute-done.32
  383.5 3.1 collective-permute-done.43
  389.7 4.2 collective-permute-done.23
  396.9 3.8 collective-permute-done.44
  425.7 3.4 collective-permute-done.26
  431.6 4.1 collective-permute-done.62
  447.7 3.2 maximum_convert_fusion.2
  450.9 17.9 %collective-permute-done.67 = bf16[256,2048]{1,0:T(8,128)(2,1)S(1)} collective-permute-done((bf16[256,2048]{1,0:T(8,128)(2,1)S(1)}, bf16[256,2048]{1,0:T(8,128)(2,1)S(1)}, u32[]{:S(2)}, u32[]{:S(2)}) %collective-permute-start.67) | collective-permute-done | bytes 1048608 | tf_op jit(solution)/shard_map/ppermute | solution.py:155
  471.7 19.6 %collective-permute-done.74 = bf16[256,2048]{1,0:T(8,128)(2,1)S(1)} collective-permute-done((bf16[256,2048]{1,0:T(8,128)(2,1)S(1)}, bf16[256,2048]{1,0:T(8,128)(2,1)S(1)}, u32[]{:S(2)}, u32[]{:S(2)}) %collective-permute-start.74) | collective-permute-done | bytes 1048608 | tf_op jit(solution)/shard_map/ppermute | solution.py:155
  494.2 19.6 %collective-permute-done.94 = bf16[1024,512]{1,0:T(8,128)(2,1)S(1)} collective-permute-done((bf16[1024,512]{1,0:T(8,128)(2,1)S(1)}, bf16[1024,512]{1,0:T(8,128)(2,1)S(1)}, u32[]{:S(2)}, u32[]{:S(2)}) %collective-permute-start.94) | collective-permute-done | bytes 1048608 | tf_op jit(solution)/shard_map/ppermute | solution.py:155
  516.7 19.0 %collective-permute-done.86 = bf16[1024,512]{1,0:T(8,128)(2,1)S(1)} collective-permute-done((bf16[1024,512]{1,0:T(8,128)(2,1)S(1)}, bf16[1024,512]{1,0:T(8,128)(2,1)S(1)}, u32[]{:S(2)}, u32[]{:S(2)}) %collective-permute-start.86) | collective-permute-done | bytes 1048608 | tf_op jit(solution)/shard_map/ppermute | solution.py:155
  541.0 8.9 %collective-permute-done.87 = bf16[512,512]{1,0:T(8,128)(2,1)S(1)} collective-permute-done((bf16[512,512]{1,0:T(8,128)(2,1)S(1)}, bf16[512,512]{1,0:T(8,128)(2,1)S(1)}, u32[]{:S(2)}, u32[]{:S(2)}) %collective-permute-start.87) | collective-permute-done | bytes 524320 | tf_op jit(solution)/shard_map/ppermute | solution.py:152
  550.8 6.7 collective-permute-done.76
  557.7 6.4 collective-permute-done.96
  564.3 3.4 collective-permute-done.88
  570.9 10.8 %collective-permute-done.77 = bf16[32,2048]{1,0:T(8,128)(2,1)S(1)} collective-permute-done((bf16[32,2048]{1,0:T(8,128)(2,1)S(1)}, bf16[32,2048]{1,0:T(8,128)(2,1)S(1)}, u32[]{:S(2)}, u32[]{:S(2)}) %collective-permute-start.77) | collective-permute-done | bytes 131104 | tf_op jit(solution)/shard_map/ppermute | solution.py:152
  581.9 5.5 collective-permute-done.97
  587.5 4.1 collective-permute-done.89
  602.4 5.0 collective-permute-done.72
  608.3 4.8 collective-permute-done.79
  613.9 4.8 collective-permute-done.99
  619.5 4.7 collective-permute-done.91
  625.5 19.4 %collective-permute-done.100 = bf16[512,512]{1,0:T(8,128)(2,1)S(1)} collective-permute-done((bf16[512,512]{1,0:T(8,128)(2,1)S(1)}, bf16[512,512]{1,0:T(8,128)(2,1)S(1)}, u32[]{:S(2)}, u32[]{:S(2)}) %collective-permute-start.100) | collective-permute-done | bytes 524320 | tf_op jit(solution)/shard_map/ppermute | solution.py:152
  647.8 7.3 %collective-permute-done.92 = bf16[512,512]{1,0:T(8,128)(2,1)S(1)} collective-permute-done((bf16[512,512]{1,0:T(8,128)(2,1)S(1)}, bf16[512,512]{1,0:T(8,128)(2,1)S(1)}, u32[]{:S(2)}, u32[]{:S(2)}) %collective-permute-start.92) | collective-permute-done | bytes 524320 | tf_op jit(solution)/shard_map/ppermute | solution.py:152
  657.2 4.3 maximum_convert_fusion
  661.9 17.8 %maximum_convert_fusion.1 = f32[2048,1024]{1,0:T(8,128)} fusion(bf16[1024,512]{1,0:T(8,128)(2,1)S(1)} %get-tuple-element.58, bf16[1024,512]{1,0:T(8,128)(2,1)S(1)} %get-tuple-element.57, bf16[1024,512]{1,0:T(8,128)(2,1)S(1)} %get-tuple-element.56, bf16[1024,512]{1,0:T(8,128)(2,1)S(1)} %get-tuple-element.55), kind=kLoop, calls=%fused_computation.9 | loop fusion | flops 16777216 | bytes 12582912 | tf_op jit(solution)/shard_map/concatenate | solution.py:380
  (526 shorter events, 243.0 us)
Async XLA Ops:
  2.8 30.4 %collective-permute-start.4 = (f32[3072]{0:T(1024)}, f32[3072]{0:T(1024)}, u32[]{:S(2)}, u32[]{:S(2)}) collective-permute-start(f32[3072]{0:T(1024)} %pad_maximum_fusion.47), channel_id=1, source_target_pairs={{0,1},{1,0},{2,3},{3,2},{4,5},{5,4},{6,7},{7,6},{8,9},{9,8},{10,11... | collective-permute-start | bytes 36872 | tf_op jit(solution)/shard_map/ppermute | solution.py:155
  7.6 27.2 %collective-permute-start = (bf16[3,128,512]{2,1,0:T(8,128)(2,1)}, bf16[3,128,512]{2,1,0:T(8,128)(2,1)}, u32[]{:S(2)}, u32[]{:S(2)}) collective-permute-start(bf16[3,128,512]{2,1,0:T(8,128)(2,1)} %constant_dynamic-slice_fusion.31), channel_id=1, source_target_pairs={{0,1},{1,0},{2,3},{3,2},{4,5},{5,4},{6,7},{7,6},{8,9},{9,8},{10,11... | collective-permute-start | bytes 1179656 | tf_op jit(solution)/shard_map/ppermute | solution.py:155
  7.6 15.7 %collective-permute-start.5 = (bf16[64,1024]{1,0:T(8,128)(2,1)S(1)}, bf16[64,1024]{1,0:T(8,128)(2,1)S(1)}, u32[]{:S(2)}, u32[]{:S(2)}) collective-permute-start(bf16[64,1024]{1,0:T(8,128)(2,1)S(1)} %constant_dynamic-slice_fusion.30), channel_id=1, source_target_pairs={{0,1},{1,0},{2,3},{3,2},{4,5},{5,4},{6,7},{7,6},{8,9},{9,8},{10,11... | collective-permute-start | bytes 393224 | tf_op jit(solution)/shard_map/ppermute | solution.py:155
  11.5 26.7 %collective-permute-start.9 = (bf16[128,2048]{1,0:T(8,128)(2,1)}, bf16[128,2048]{1,0:T(8,128)(2,1)}, u32[]{:S(2)}, u32[]{:S(2)}) collective-permute-start(bf16[128,2048]{1,0:T(8,128)(2,1)} %constant_dynamic-slice_fusion.29), channel_id=1, source_target_pairs={{0,1},{1,0},{2,3},{3,2},{4,5},{5,4},{6,7},{7,6},{8,9},{9,8},{10,11... | collective-permute-start | bytes 1572872 | tf_op jit(solution)/shard_map/ppermute | solution.py:155
  23.2 318.5 %collective-permute-start.53 = (bf16[512,512]{1,0:T(8,128)(2,1)}, bf16[512,512]{1,0:T(8,128)(2,1)}, u32[]{:S(2)}, u32[]{:S(2)}) collective-permute-start(bf16[512,512]{1,0:T(8,128)(2,1)} %get-tuple-element.24), channel_id=1, source_target_pairs={{0,2},{2,0},{4,6},{6,4},{8,10},{10,8},{12,14},{14,12},{16,18},{18,... | collective-permute-start | bytes 1572872 | tf_op jit(solution)/shard_map/ppermute | solution.py:152
  38.2 259.6 %collective-permute-start.17 = (bf16[512,512]{1,0:T(8,128)(2,1)}, bf16[512,512]{1,0:T(8,128)(2,1)}, u32[]{:S(2)}, u32[]{:S(2)}) collective-permute-start(bf16[512,512]{1,0:T(8,128)(2,1)} %constant_dynamic-slice_fusion.27), channel_id=1, source_target_pairs={{0,2},{2,0},{4,6},{6,4},{8,10},{10,8},{12,14},{14,12},{16,18},{18,... | collective-permute-start | bytes 1572872 | tf_op jit(solution)/shard_map/ppermute | solution.py:152
  47.1 32.5 %collective-permute-start.8 = (bf16[256,1024]{1,0:T(8,128)(2,1)S(1)}, bf16[256,1024]{1,0:T(8,128)(2,1)S(1)}, u32[]{:S(2)}, u32[]{:S(2)}) collective-permute-start(bf16[256,1024]{1,0:T(8,128)(2,1)S(1)} %pad_maximum_fusion.25), channel_id=1, source_target_pairs={{0,4},{2,6},{4,0},{6,2},{8,12},{10,14},{12,8},{14,10},{16,20},{18,... | collective-permute-start | bytes 1572872 | tf_op jit(solution)/shard_map/ppermute | solution.py:152
  49.7 29.1 %collective-permute-start.2 = (bf16[3,256,512]{2,1,0:T(8,128)(2,1)S(1)}, bf16[3,256,512]{2,1,0:T(8,128)(2,1)S(1)}, u32[]{:S(2)}, u32[]{:S(2)}) collective-permute-start(bf16[3,256,512]{2,1,0:T(8,128)(2,1)S(1)} %pad_maximum_fusion.22), channel_id=1, source_target_pairs={{0,4},{2,6},{4,0},{6,2},{8,12},{10,14},{12,8},{14,10},{16,20},{18,... | collective-permute-start | bytes 2359304 | tf_op jit(solution)/shard_map/ppermute | solution.py:152
  51.5 47.6 %collective-permute-start.11 = (bf16[256,2048]{1,0:T(8,128)(2,1)S(1)}, bf16[256,2048]{1,0:T(8,128)(2,1)S(1)}, u32[]{:S(2)}, u32[]{:S(2)}) collective-permute-start(bf16[256,2048]{1,0:T(8,128)(2,1)S(1)} %pad_maximum_fusion.16), channel_id=1, source_target_pairs={{0,4},{2,6},{4,0},{6,2},{8,12},{10,14},{12,8},{14,10},{16,20},{18,... | collective-permute-start | bytes 3145736 | tf_op jit(solution)/shard_map/ppermute | solution.py:152
  79.2 62.2 %collective-permute-start.3 = (bf16[3,512,512]{2,1,0:T(8,128)(2,1)S(1)}, bf16[3,512,512]{2,1,0:T(8,128)(2,1)S(1)}, u32[]{:S(2)}, u32[]{:S(2)}) collective-permute-start(bf16[3,512,512]{2,1,0:T(8,128)(2,1)S(1)} %pad_maximum_fusion.9), channel_id=1, source_target_pairs={{0,8},{2,10},{4,12},{6,14},{8,0},{10,2},{12,4},{14,6},{16,24},{18,... | collective-permute-start | bytes 4718600 | tf_op jit(solution)/shard_map/ppermute | solution.py:152
  79.6 59.4 %collective-permute-start.15 = (bf16[512,1024]{1,0:T(8,128)(2,1)S(1)}, bf16[512,1024]{1,0:T(8,128)(2,1)S(1)}, u32[]{:S(2)}, u32[]{:S(2)}) collective-permute-start(bf16[512,1024]{1,0:T(8,128)(2,1)S(1)} %pad_maximum_fusion.17), channel_id=1, source_target_pairs={{0,8},{2,10},{4,12},{6,14},{8,0},{10,2},{12,4},{14,6},{16,24},{18,... | collective-permute-start | bytes 3145736 | tf_op jit(solution)/shard_map/ppermute | solution.py:152
  99.8 79.0 %collective-permute-start.12 = (bf16[512,2048]{1,0:T(8,128)(2,1)S(1)}, bf16[512,2048]{1,0:T(8,128)(2,1)S(1)}, u32[]{:S(2)}, u32[]{:S(2)}) collective-permute-start(bf16[512,2048]{1,0:T(8,128)(2,1)S(1)} %pad_maximum_fusion.6), channel_id=1, source_target_pairs={{0,8},{2,10},{4,12},{6,14},{8,0},{10,2},{12,4},{14,6},{16,24},{18,... | collective-permute-start | bytes 6291464 | tf_op jit(solution)/shard_map/ppermute | solution.py:152
  139.8 47.8 %collective-permute-start.16 = (bf16[1024,1024]{1,0:T(8,128)(2,1)S(1)}, bf16[1024,1024]{1,0:T(8,128)(2,1)S(1)}, u32[]{:S(2)}, u32[]{:S(2)}) collective-permute-start(bf16[1024,1024]{1,0:T(8,128)(2,1)S(1)} %pad_maximum_fusion.7), channel_id=1, source_target_pairs={{0,4},{2,6},{4,0},{6,2},{8,12},{10,14},{12,8},{14,10},{16,20},{18,... | collective-permute-start | bytes 6291464 | tf_op jit(solution)/shard_map/ppermute | solution.py:152
  249.3 49.1 %collective-permute-start.39 = (bf16[512,512]{1,0:T(8,128)(2,1)S(1)}, bf16[512,512]{1,0:T(8,128)(2,1)}, u32[]{:S(2)}, u32[]{:S(2)}) collective-permute-start(bf16[512,512]{1,0:T(8,128)(2,1)S(1)} %get-tuple-element.33), channel_id=1, source_target_pairs={{0,2},{2,0},{4,6},{6,4},{8,10},{10,8},{12,14},{14,12},{16,18},{18,... | collective-permute-start | bytes 1572872 | tf_op jit(solution)/shard_map/ppermute | solution.py:152
  257.0 43.6 %collective-permute-start.29 = (bf16[512,512]{1,0:T(8,128)(2,1)}, bf16[512,512]{1,0:T(8,128)(2,1)}, u32[]{:S(2)}, u32[]{:S(2)}) collective-permute-start(bf16[512,512]{1,0:T(8,128)(2,1)} %get-tuple-element.32), channel_id=1, source_target_pairs={{0,2},{2,0},{4,6},{6,4},{8,10},{10,8},{12,14},{14,12},{16,18},{18,... | collective-permute-start | bytes 1572872 | tf_op jit(solution)/shard_map/ppermute | solution.py:152
  302.9 14.8 %collective-permute-start.40 = (bf16[512,512]{1,0:T(8,128)(2,1)S(1)}, bf16[512,512]{1,0:T(8,128)(2,1)S(1)}, u32[]{:S(2)}, u32[]{:S(2)}) collective-permute-start(bf16[512,512]{1,0:T(8,128)(2,1)S(1)} %fusion.40), channel_id=1, source_target_pairs={{0,1},{1,0},{2,3},{3,2},{4,5},{5,4},{6,7},{7,6},{8,9},{9,8},{10,11... | collective-permute-start | bytes 1572872 | tf_op jit(solution)/shard_map/ppermute | solution.py:155
  306.4 22.6 %collective-permute-start.30 = (bf16[512,512]{1,0:T(8,128)(2,1)S(1)}, bf16[512,512]{1,0:T(8,128)(2,1)S(1)}, u32[]{:S(2)}, u32[]{:S(2)}) collective-permute-start(bf16[512,512]{1,0:T(8,128)(2,1)S(1)} %fusion.35), channel_id=1, source_target_pairs={{0,1},{1,0},{2,3},{3,2},{4,5},{5,4},{6,7},{7,6},{8,9},{9,8},{10,11... | collective-permute-start | bytes 1572872 | tf_op jit(solution)/shard_map/ppermute | solution.py:155
  308.4 185.8 %collective-permute-start.83 = (bf16[512,2048]{1,0:T(8,128)(2,1)S(1)}, bf16[512,2048]{1,0:T(8,128)(2,1)S(1)}, u32[]{:S(2)}, u32[]{:S(2)}) collective-permute-start(bf16[512,2048]{1,0:T(8,128)(2,1)S(1)} %copy-done.40), channel_id=1, source_target_pairs={{0,2},{2,0},{4,6},{6,4},{8,10},{10,8},{12,14},{14,12},{16,18},{18,... | collective-permute-start | bytes 6291464 | tf_op jit(solution)/shard_map/ppermute | solution.py:152
  317.8 14.8 %collective-permute-start.18 = (bf16[512,512]{1,0:T(8,128)(2,1)S(1)}, bf16[512,512]{1,0:T(8,128)(2,1)S(1)}, u32[]{:S(2)}, u32[]{:S(2)}) collective-permute-start(bf16[512,512]{1,0:T(8,128)(2,1)S(1)} %get-tuple-element.27), channel_id=1, source_target_pairs={{0,2},{2,0},{4,6},{6,4},{8,10},{10,8},{12,14},{14,12},{16,18},{18,... | collective-permute-start | bytes 1572872 | tf_op jit(solution)/shard_map/ppermute | solution.py:152
  319.5 20.8 %collective-permute-start.20 = (bf16[512,512]{1,0:T(8,128)(2,1)S(1)}, bf16[512,512]{1,0:T(8,128)(2,1)S(1)}, u32[]{:S(2)}, u32[]{:S(2)}) collective-permute-start(bf16[512,512]{1,0:T(8,128)(2,1)S(1)} %fusion.30), channel_id=1, source_target_pairs={{0,1},{1,0},{2,3},{3,2},{4,5},{5,4},{6,7},{7,6},{8,9},{9,8},{10,11... | collective-permute-start | bytes 1572872 | tf_op jit(solution)/shard_map/ppermute | solution.py:155
  329.0 21.7 %collective-permute-start.56 = (bf16[512,512]{1,0:T(8,128)(2,1)S(1)}, bf16[512,512]{1,0:T(8,128)(2,1)S(1)}, u32[]{:S(2)}, u32[]{:S(2)}) collective-permute-start(bf16[512,512]{1,0:T(8,128)(2,1)S(1)} %fusion.45), channel_id=1, source_target_pairs={{0,1},{1,0},{2,3},{3,2},{4,5},{5,4},{6,7},{7,6},{8,9},{9,8},{10,11... | collective-permute-start | bytes 1572872 | tf_op jit(solution)/shard_map/ppermute | solution.py:155
  332.6 106.0 %collective-permute-start.66 = (bf16[512,2048]{1,0:T(8,128)(2,1)S(1)}, bf16[512,2048]{1,0:T(8,128)(2,1)S(1)}, u32[]{:S(2)}, u32[]{:S(2)}) collective-permute-start(bf16[512,2048]{1,0:T(8,128)(2,1)S(1)} %copy-done.18), channel_id=1, source_target_pairs={{0,2},{2,0},{4,6},{6,4},{8,10},{10,8},{12,14},{14,12},{16,18},{18,... | collective-permute-start | bytes 6291464 | tf_op jit(solution)/shard_map/ppermute | solution.py:152
  340.2 96.2 %collective-permute-start.85 = (bf16[512,2048]{1,0:T(8,128)(2,1)S(1)}, bf16[512,2048]{1,0:T(8,128)(2,1)S(1)}, u32[]{:S(2)}, u32[]{:S(2)}) collective-permute-start(bf16[512,2048]{1,0:T(8,128)(2,1)S(1)} %copy-done.37), channel_id=1, source_target_pairs={{0,2},{2,0},{4,6},{6,4},{8,10},{10,8},{12,14},{14,12},{16,18},{18,... | collective-permute-start | bytes 6291464 | tf_op jit(solution)/shard_map/ppermute | solution.py:152
  435.9 15.0 %collective-permute-start.65 = (bf16[512,2048]{1,0:T(8,128)(2,1)S(1)}, bf16[512,2048]{1,0:T(8,128)(2,1)S(1)}, u32[]{:S(2)}, u32[]{:S(2)}) collective-permute-start(bf16[512,2048]{1,0:T(8,128)(2,1)S(1)} %copy-done.15), channel_id=1, source_target_pairs={{0,2},{2,0},{4,6},{6,4},{8,10},{10,8},{12,14},{14,12},{16,18},{18,... | collective-permute-start | bytes 6291464 | tf_op jit(solution)/shard_map/ppermute | solution.py:152
  442.7 26.1 %collective-permute-start.67 = (bf16[256,2048]{1,0:T(8,128)(2,1)S(1)}, bf16[256,2048]{1,0:T(8,128)(2,1)S(1)}, u32[]{:S(2)}, u32[]{:S(2)}) collective-permute-start(bf16[256,2048]{1,0:T(8,128)(2,1)S(1)} %fusion.9), channel_id=1, source_target_pairs={{0,1},{1,0},{2,3},{3,2},{4,5},{5,4},{6,7},{7,6},{8,9},{9,8},{10,11... | collective-permute-start | bytes 3145736 | tf_op jit(solution)/shard_map/ppermute | solution.py:155
  445.1 46.2 %collective-permute-start.74 = (bf16[256,2048]{1,0:T(8,128)(2,1)S(1)}, bf16[256,2048]{1,0:T(8,128)(2,1)S(1)}, u32[]{:S(2)}, u32[]{:S(2)}) collective-permute-start(bf16[256,2048]{1,0:T(8,128)(2,1)S(1)} %fusion.11), channel_id=1, source_target_pairs={{0,1},{1,0},{2,3},{3,2},{4,5},{5,4},{6,7},{7,6},{8,9},{9,8},{10,11... | collective-permute-start | bytes 3145736 | tf_op jit(solution)/shard_map/ppermute | solution.py:155
  445.4 68.4 %collective-permute-start.94 = (bf16[1024,512]{1,0:T(8,128)(2,1)S(1)}, bf16[1024,512]{1,0:T(8,128)(2,1)S(1)}, u32[]{:S(2)}, u32[]{:S(2)}) collective-permute-start(bf16[1024,512]{1,0:T(8,128)(2,1)S(1)} %add_convert_fusion.3), channel_id=1, source_target_pairs={{0,1},{1,0},{2,3},{3,2},{4,5},{5,4},{6,7},{7,6},{8,9},{9,8},{10,11... | collective-permute-start | bytes 3145736 | tf_op jit(solution)/shard_map/ppermute | solution.py:155
  450.9 84.8 %collective-permute-start.86 = (bf16[1024,512]{1,0:T(8,128)(2,1)S(1)}, bf16[1024,512]{1,0:T(8,128)(2,1)S(1)}, u32[]{:S(2)}, u32[]{:S(2)}) collective-permute-start(bf16[1024,512]{1,0:T(8,128)(2,1)S(1)} %add_convert_fusion.6), channel_id=1, source_target_pairs={{0,1},{1,0},{2,3},{3,2},{4,5},{5,4},{6,7},{7,6},{8,9},{9,8},{10,11... | collective-permute-start | bytes 3145736 | tf_op jit(solution)/shard_map/ppermute | solution.py:155
  469.6 68.6 %collective-permute-start.68 = (bf16[128,2048]{1,0:T(8,128)(2,1)S(1)}, bf16[128,2048]{1,0:T(8,128)(2,1)S(1)}, u32[]{:S(2)}, u32[]{:S(2)}) collective-permute-start(bf16[128,2048]{1,0:T(8,128)(2,1)S(1)} %constant_dynamic-slice_fusion.12), channel_id=1, source_target_pairs={{0,4},{2,6},{4,0},{6,2},{8,12},{10,14},{12,8},{14,10},{16,20},{18,... | collective-permute-start | bytes 1572872 | tf_op jit(solution)/shard_map/ppermute | solution.py:152
  492.1 46.4 %collective-permute-start.75 = (bf16[128,2048]{1,0:T(8,128)(2,1)S(1)}, bf16[128,2048]{1,0:T(8,128)(2,1)S(1)}, u32[]{:S(2)}, u32[]{:S(2)}) collective-permute-start(bf16[128,2048]{1,0:T(8,128)(2,1)S(1)} %constant_dynamic-slice_fusion.9), channel_id=1, source_target_pairs={{0,4},{2,6},{4,0},{6,2},{8,12},{10,14},{12,8},{14,10},{16,20},{18,... | collective-permute-start | bytes 1572872 | tf_op jit(solution)/shard_map/ppermute | solution.py:152
  514.6 26.2 %collective-permute-start.95 = (bf16[512,512]{1,0:T(8,128)(2,1)S(1)}, bf16[512,512]{1,0:T(8,128)(2,1)S(1)}, u32[]{:S(2)}, u32[]{:S(2)}) collective-permute-start(bf16[512,512]{1,0:T(8,128)(2,1)S(1)} %constant_dynamic-slice_fusion.2), channel_id=1, source_target_pairs={{0,4},{2,6},{4,0},{6,2},{8,12},{10,14},{12,8},{14,10},{16,20},{18,... | collective-permute-start | bytes 1572872 | tf_op jit(solution)/shard_map/ppermute | solution.py:152
  538.7 18.9 %collective-permute-start.76 = (bf16[64,2048]{1,0:T(8,128)(2,1)S(1)}, bf16[64,2048]{1,0:T(8,128)(2,1)S(1)}, u32[]{:S(2)}, u32[]{:S(2)}) collective-permute-start(bf16[64,2048]{1,0:T(8,128)(2,1)S(1)} %constant_dynamic-slice_fusion.8), channel_id=1, source_target_pairs={{0,8},{2,10},{4,12},{6,14},{8,0},{10,2},{12,4},{14,6},{16,24},{18,... | collective-permute-start | bytes 786440 | tf_op jit(solution)/shard_map/ppermute | solution.py:152
  540.9 23.2 %collective-permute-start.96 = (bf16[256,512]{1,0:T(8,128)(2,1)S(1)}, bf16[256,512]{1,0:T(8,128)(2,1)S(1)}, u32[]{:S(2)}, u32[]{:S(2)}) collective-permute-start(bf16[256,512]{1,0:T(8,128)(2,1)S(1)} %constant_dynamic-slice_fusion.1), channel_id=1, source_target_pairs={{0,8},{2,10},{4,12},{6,14},{8,0},{10,2},{12,4},{14,6},{16,24},{18,... | collective-permute-start | bytes 786440 | tf_op jit(solution)/shard_map/ppermute | solution.py:152
  550.1 17.6 %collective-permute-start.88 = (bf16[256,512]{1,0:T(8,128)(2,1)S(1)}, bf16[256,512]{1,0:T(8,128)(2,1)S(1)}, u32[]{:S(2)}, u32[]{:S(2)}) collective-permute-start(bf16[256,512]{1,0:T(8,128)(2,1)S(1)} %constant_dynamic-slice_fusion.4), channel_id=1, source_target_pairs={{0,8},{2,10},{4,12},{6,14},{8,0},{10,2},{12,4},{14,6},{16,24},{18,... | collective-permute-start | bytes 786440 | tf_op jit(solution)/shard_map/ppermute | solution.py:152
  550.3 17.6 %collective-permute-start.70 = (bf16[32,2048]{1,0:T(8,128)(2,1)S(1)}, bf16[32,2048]{1,0:T(8,128)(2,1)S(1)}, u32[]{:S(2)}, u32[]{:S(2)}) collective-permute-start(bf16[32,2048]{1,0:T(8,128)(2,1)S(1)} %constant_dynamic-slice_fusion.10), channel_id=1, source_target_pairs={{0,16},{2,18},{4,20},{6,22},{8,24},{10,26},{12,28},{14,30},{16,0},... | collective-permute-start | bytes 393224 | tf_op jit(solution)/shard_map/ppermute | solution.py:152
  557.6 24.1 %collective-permute-start.77 = (bf16[32,2048]{1,0:T(8,128)(2,1)S(1)}, bf16[32,2048]{1,0:T(8,128)(2,1)S(1)}, u32[]{:S(2)}, u32[]{:S(2)}) collective-permute-start(bf16[32,2048]{1,0:T(8,128)(2,1)S(1)} %constant_dynamic-slice_fusion.7), channel_id=1, source_target_pairs={{0,16},{2,18},{4,20},{6,22},{8,24},{10,26},{12,28},{14,30},{16,0},... | collective-permute-start | bytes 393224 | tf_op jit(solution)/shard_map/ppermute | solution.py:152
  564.2 23.2 %collective-permute-start.97 = (bf16[128,512]{1,0:T(8,128)(2,1)S(1)}, bf16[128,512]{1,0:T(8,128)(2,1)S(1)}, u32[]{:S(2)}, u32[]{:S(2)}) collective-permute-start(bf16[128,512]{1,0:T(8,128)(2,1)S(1)} %constant_dynamic-slice_fusion), channel_id=1, source_target_pairs={{0,16},{2,18},{4,20},{6,22},{8,24},{10,26},{12,28},{14,30},{16,0},... | collective-permute-start | bytes 393224 | tf_op jit(solution)/shard_map/ppermute | solution.py:152
  567.8 23.8 %collective-permute-start.89 = (bf16[128,512]{1,0:T(8,128)(2,1)S(1)}, bf16[128,512]{1,0:T(8,128)(2,1)S(1)}, u32[]{:S(2)}, u32[]{:S(2)}) collective-permute-start(bf16[128,512]{1,0:T(8,128)(2,1)S(1)} %constant_dynamic-slice_fusion.3), channel_id=1, source_target_pairs={{0,16},{2,18},{4,20},{6,22},{8,24},{10,26},{12,28},{14,30},{16,0},... | collective-permute-start | bytes 393224 | tf_op jit(solution)/shard_map/ppermute | solution.py:152
  568.0 26.4 %collective-permute-start.71 = (bf16[32,2048]{1,0:T(8,128)(2,1)S(1)}, bf16[32,2048]{1,0:T(8,128)(2,1)S(1)}, u32[]{:S(2)}, u32[]{:S(2)}) collective-permute-start(bf16[32,2048]{1,0:T(8,128)(2,1)S(1)} %add_convert_fusion.25), channel_id=1, source_target_pairs={{0,16},{2,18},{4,20},{6,22},{8,24},{10,26},{12,28},{14,30},{16,0},... | collective-permute-start | bytes 393224 | tf_op jit(solution)/shard_map/ppermute | solution.py:152
  581.8 15.5 %collective-permute-start.78 = (bf16[32,2048]{1,0:T(8,128)(2,1)S(1)}, bf16[32,2048]{1,0:T(8,128)(2,1)S(1)}, u32[]{:S(2)}, u32[]{:S(2)}) collective-permute-start(bf16[32,2048]{1,0:T(8,128)(2,1)S(1)} %add_convert_fusion.24), channel_id=1, source_target_pairs={{0,16},{2,18},{4,20},{6,22},{8,24},{10,26},{12,28},{14,30},{16,0},... | collective-permute-start | bytes 393224 | tf_op jit(solution)/shard_map/ppermute | solution.py:152
  597.4 15.7 %collective-permute-start.79 = (bf16[64,2048]{1,0:T(8,128)(2,1)S(1)}, bf16[64,2048]{1,0:T(8,128)(2,1)S(1)}, u32[]{:S(2)}, u32[]{:S(2)}) collective-permute-start(bf16[64,2048]{1,0:T(8,128)(2,1)S(1)} %pad_maximum_fusion.40), channel_id=1, source_target_pairs={{0,8},{2,10},{4,12},{6,14},{8,0},{10,2},{12,4},{14,6},{16,24},{18,... | collective-permute-start | bytes 786440 | tf_op jit(solution)/shard_map/ppermute | solution.py:152
  600.2 18.5 %collective-permute-start.99 = (bf16[256,512]{1,0:T(8,128)(2,1)S(1)}, bf16[256,512]{1,0:T(8,128)(2,1)S(1)}, u32[]{:S(2)}, u32[]{:S(2)}) collective-permute-start(bf16[256,512]{1,0:T(8,128)(2,1)S(1)} %pad_maximum_fusion.42), channel_id=1, source_target_pairs={{0,8},{2,10},{4,12},{6,14},{8,0},{10,2},{12,4},{14,6},{16,24},{18,... | collective-permute-start | bytes 786440 | tf_op jit(solution)/shard_map/ppermute | solution.py:152
  601.9 22.3 %collective-permute-start.91 = (bf16[256,512]{1,0:T(8,128)(2,1)S(1)}, bf16[256,512]{1,0:T(8,128)(2,1)S(1)}, u32[]{:S(2)}, u32[]{:S(2)}) collective-permute-start(bf16[256,512]{1,0:T(8,128)(2,1)S(1)} %pad_maximum_fusion.41), channel_id=1, source_target_pairs={{0,8},{2,10},{4,12},{6,14},{8,0},{10,2},{12,4},{14,6},{16,24},{18,... | collective-permute-start | bytes 786440 | tf_op jit(solution)/shard_map/ppermute | solution.py:152
  607.6 17.5 %collective-permute-start.73 = (bf16[128,2048]{1,0:T(8,128)(2,1)S(1)}, bf16[128,2048]{1,0:T(8,128)(2,1)S(1)}, u32[]{:S(2)}, u32[]{:S(2)}) collective-permute-start(bf16[128,2048]{1,0:T(8,128)(2,1)S(1)} %pad_maximum_fusion.30), channel_id=1, source_target_pairs={{0,4},{2,6},{4,0},{6,2},{8,12},{10,14},{12,8},{14,10},{16,20},{18,... | collective-permute-start | bytes 1572872 | tf_op jit(solution)/shard_map/ppermute | solution.py:152
  613.2 32.1 %collective-permute-start.80 = (bf16[128,2048]{1,0:T(8,128)(2,1)S(1)}, bf16[128,2048]{1,0:T(8,128)(2,1)S(1)}, u32[]{:S(2)}, u32[]{:S(2)}) collective-permute-start(bf16[128,2048]{1,0:T(8,128)(2,1)S(1)} %pad_maximum_fusion.31), channel_id=1, source_target_pairs={{0,4},{2,6},{4,0},{6,2},{8,12},{10,14},{12,8},{14,10},{16,20},{18,... | collective-permute-start | bytes 1572872 | tf_op jit(solution)/shard_map/ppermute | solution.py:152
  618.8 26.1 %collective-permute-start.100 = (bf16[512,512]{1,0:T(8,128)(2,1)S(1)}, bf16[512,512]{1,0:T(8,128)(2,1)S(1)}, u32[]{:S(2)}, u32[]{:S(2)}) collective-permute-start(bf16[512,512]{1,0:T(8,128)(2,1)S(1)} %pad_maximum_fusion.33), channel_id=1, source_target_pairs={{0,4},{2,6},{4,0},{6,2},{8,12},{10,14},{12,8},{14,10},{16,20},{18,... | collective-permute-start | bytes 1572872 | tf_op jit(solution)/shard_map/ppermute | solution.py:152
  624.3 30.8 %collective-permute-start.92 = (bf16[512,512]{1,0:T(8,128)(2,1)S(1)}, bf16[512,512]{1,0:T(8,128)(2,1)S(1)}, u32[]{:S(2)}, u32[]{:S(2)}) collective-permute-start(bf16[512,512]{1,0:T(8,128)(2,1)S(1)} %pad_maximum_fusion.32), channel_id=1, source_target_pairs={{0,4},{2,6},{4,0},{6,2},{8,12},{10,14},{12,8},{14,10},{16,20},{18,... | collective-permute-start | bytes 1572872 | tf_op jit(solution)/shard_map/ppermute | solution.py:152
  625.4 30.1 %collective-permute-start.81 = (bf16[256,2048]{1,0:T(8,128)(2,1)S(1)}, bf16[256,2048]{1,0:T(8,128)(2,1)S(1)}, u32[]{:S(2)}, u32[]{:S(2)}) collective-permute-start(bf16[256,2048]{1,0:T(8,128)(2,1)S(1)} %pad_maximum_fusion.18), channel_id=1, source_target_pairs={{0,2},{2,0},{4,6},{6,4},{8,10},{10,8},{12,14},{14,12},{16,18},{18,... | collective-permute-start | bytes 3145736 | tf_op jit(solution)/shard_map/ppermute | solution.py:152
  (117 other events, 1131.8 us)

commit v2 on v1

v2 whole, which is shorter than its diff:
```python
import functools

import jax
import jax.numpy as jnp
import numpy as np
from jax import lax
from jax.experimental import pallas as pl
from jax.experimental.pallas import tpu as pltpu
from jax.sharding import PartitionSpec as P

HD = 64
F32 = jnp.float32
BF16 = jnp.bfloat16
NEG = -1000000000.0
SCALE = 0
COST = [0.0]
LOG = []
FLOWN = []
HELD = []


def cost():
    flops = int(SCALE * COST[0] * 1.15e9)
    return pl.CostEstimate(flops=flops, bytes_accessed=0, transcendentals=0)


ERFC_P = 0.3275911
ERFC_C = (
    0.18510853909898187,
    0.17995808540893535,
    0.21032499893163595,
    0.011746556912990477,
    0.4777504794974274,
    -0.4314195259659222,
    0.5110037999525718,
    -0.14447299033990682,
)


def gelu_both(up):
    size = jnp.abs(up)
    t = 1.0 / (1.0 + (ERFC_P * 0.5**0.5) * size)
    poly = jnp.full_like(t, 0.5 * ERFC_C[-1])
    for c in ERFC_C[-2::-1]:
        poly = poly * t + 0.5 * c
    density = jnp.exp(-0.5 * up * up)
    tail = poly * t * density
    phi = jnp.where(up > 0, 1.0 - tail, tail)
    return up * phi, phi + up * (density * 0.3989422804014327)


def contract(a, b, ca, cb):
    return lax.dot_general(a, b, (((ca,), (cb,)), ((), ())), preferred_element_type=F32)


def params(mib):
    return pltpu.CompilerParams(vmem_limit_bytes=mib * 2**20)


def whole_spec(a):
    return pl.BlockSpec(a.shape, lambda *_: (0,) * len(a.shape))


BROUGHT = ((0, 0), (2, 0), (1, 0), (4, 0), (0, 1), (3, 0), (1, 1), (5, 0))


AT, CORES, DP, BITS = 0, 8, 10, 11


def attend_kernel(len_ref, q_ref, k_ref, v_ref, o_ref, lse_ref):
    length = len_ref[0]
    q, k, v = q_ref[0], k_ref[0], v_ref[0]
    rows, width = q.shape
    head = lax.broadcasted_iota(jnp.int32, (rows, width), 1) // HD
    key_pos = lax.broadcasted_iota(jnp.int32, (rows, rows), 0)
    out = None
    for h in range(width // HD):
        mine = head == h
        kh = jnp.where(mine, k, jnp.zeros_like(k)) * jnp.asarray(HD**-0.5, BF16)
        s = jnp.where(key_pos < length, contract(kh, q, 1, 1), F32(NEG))
        top = jnp.max(s, axis=0, keepdims=True)
        e = jnp.exp(s - top)
        total = jnp.sum(e, axis=0, keepdims=True)
        lse_ref[0, h : h + 1, :] = top + jnp.log(total)
        p = (e * (1.0 / total)).astype(BF16)
        o = contract(p, v, 0, 0)
        out = o if out is None else jnp.where(mine, o, out)
    o_ref[...] = out.astype(BF16)


def third(rows, wide, c):
    return pl.BlockSpec((1, rows, wide), lambda i, c=c: (c, 0, i))


def attend(length, qkv):
    _, rows, width = qkv.shape
    wide = min(2 * HD, width)
    steps = width // wide
    return pl.pallas_call(
        attend_kernel,
        grid=(steps,),
        in_specs=[pl.BlockSpec(memory_space=pltpu.SMEM)]
        + [third(rows, wide, c) for c in range(3)],
        out_specs=[
            pl.BlockSpec((rows, wide), lambda i: (0, i)),
            pl.BlockSpec((1, wide // HD, rows), lambda i: (i, 0, 0)),
        ],
        out_shape=[
            jax.ShapeDtypeStruct((rows, width), BF16),
            jax.ShapeDtypeStruct((steps, wide // HD, rows), F32),
        ],
        compiler_params=params(20),
        cost_estimate=cost(),
        name="attend",
    )(length, qkv, qkv, qkv)


def attend_back_kernel(
    len_ref, q_ref, k_ref, v_ref, g1_ref, w_ref, lse_ref, d_ref, sum_ref
):
    length = len_ref[0]
    q, k, v = q_ref[0], k_ref[0], v_ref[0]
    g = contract(g1_ref[...], w_ref[...], 1, 1).astype(BF16)
    rows, width = q.shape
    head = lax.broadcasted_iota(jnp.int32, (rows, width), 1) // HD
    head_t = lax.broadcasted_iota(jnp.int32, (width, rows), 0) // HD
    key_pos = lax.broadcasted_iota(jnp.int32, (rows, rows), 0)
    dq = dk = dv = None
    for h in range(width // HD):
        mine = head == h
        kh = jnp.where(mine, k, jnp.zeros_like(k)) * jnp.asarray(HD**-0.5, BF16)
        vh = jnp.where(mine, v, jnp.zeros_like(v))
        s = jnp.where(key_pos < length, contract(kh, q, 1, 1), F32(NEG))
        p = jnp.exp(s - lse_ref[0, h : h + 1, :])
        dp = contract(vh, g, 1, 1)
        dvh = contract(p.astype(BF16), g, 1, 0)
        center = jnp.sum(p * dp, axis=0, keepdims=True)
        ds = (p * (dp - center)).astype(BF16)
        dkh = contract(ds, q, 1, 0)
        dqh = contract(k, ds, 0, 0)
        dv = dvh if dv is None else jnp.where(mine, dvh, dv)
        dk = dkh if dk is None else jnp.where(mine, dkh, dk)
        dq = dqh if dq is None else jnp.where(head_t == h, dqh, dq)
    out = (
        (dq * (HD**-0.5)).T.astype(BF16),
        (dk * (HD**-0.5)).astype(BF16),
        dv.astype(BF16),
    )
    for c in range(3):
        d_ref[c] = out[c]
        sum_ref[c : c + 1, :] = jnp.sum(out[c].astype(F32), axis=0, keepdims=True)


def attend_back(length, qkv, g_one, out_w, lse):
    _, rows, width = qkv.shape
    wide = min(2 * HD, width)
    d = g_one.shape[1]
    return pl.pallas_call(
        attend_back_kernel,
        grid=(width // wide,),
        in_specs=[pl.BlockSpec(memory_space=pltpu.SMEM)]
        + [third(rows, wide, c) for c in range(3)]
        + [
            whole_spec(g_one),
            pl.BlockSpec((wide, d), lambda i: (i, 0)),
            pl.BlockSpec((1, wide // HD, rows), lambda i: (i, 0, 0)),
        ],
        out_specs=[
            pl.BlockSpec((3, rows, wide), lambda i: (0, 0, i)),
            pl.BlockSpec((3, wide), lambda i: (0, i)),
        ],
        out_shape=[
            jax.ShapeDtypeStruct((3, rows, width), BF16),
            jax.ShapeDtypeStruct((3, width), F32),
        ],
        compiler_params=params(28),
        cost_estimate=cost(),
        name="attend_back",
    )(length, qkv, qkv, qkv, g_one, out_w, lse)


def project(at, x, bias, *pieces):
    n = len(pieces)
    rows, depth = x.shape
    width = pieces[0].shape[2]
    size = depth // len(BROUGHT)

    def kernel(at_ref, x_ref, b_ref, *refs):
        w_ref = refs[0]
        if n > 1:
            w_ref = refs[n + 1]
            for i, (k, j) in enumerate(BROUGHT):
                row = pl.multiple_of(at_ref[i] * size, size)
                w_ref[0, pl.ds(row, size)] = refs[k][0, j * size : (j + 1) * size]
        refs[n][0] = (contract(x_ref[...], w_ref[0], 1, 0) + b_ref[0]).astype(BF16)

    out_specs = [pl.BlockSpec((1, rows, width), lambda c, at: (c, 0, 0))]
    out_shape = [jax.ShapeDtypeStruct((3, rows, width), BF16)]
    if n > 1:
        out_specs.append(pl.BlockSpec((1, depth, width), lambda c, at: (c, 0, 0)))
        out_shape.append(jax.ShapeDtypeStruct((3, depth, width), BF16))
    return pl.pallas_call(
        kernel,
        grid_spec=pltpu.PrefetchScalarGridSpec(
            num_scalar_prefetch=1,
            grid=(3,),
            in_specs=[
                whole_spec(x),
                pl.BlockSpec((1, 1, width), lambda c, at: (c, 0, 0)),
            ]
            + [
                pl.BlockSpec((1, p.shape[1], width), lambda c, at: (c, 0, 0))
                for p in pieces
            ],
            out_specs=out_specs,
        ),
        out_shape=out_shape,
        compiler_params=params(20),
        cost_estimate=cost(),
        name="project",
    )(at, x, bias, *pieces)


def norm(hidden):
    center = hidden - jnp.mean(hidden, axis=-1, keepdims=True)
    spread = jnp.mean(center * center, axis=-1, keepdims=True)
    scale = lax.rsqrt(spread + 1e-05)
    return center * scale, scale


def norm_back(grad, normal, scale, gain):
    gy = grad * gain
    mean = jnp.mean(gy, axis=-1, keepdims=True)
    along = jnp.mean(gy * normal, axis=-1, keepdims=True)
    return scale * (gy - mean - normal * along)


def attended(at, x, bias, gain, shift, mixed, weights):
    rows, d = x.shape
    step = min(128, rows)
    cut = [i for i, w in enumerate(weights) if len(w) > 1]
    flat = [p for w in weights for p in w]
    n = len(mixed)

    def kernel(at_ref, x_ref, b_ref, g_ref, s_ref, *refs):
        m, w = refs[:n], refs[n : n + len(flat)]
        low_ref, normal_ref, scale_ref = refs[n + len(flat) :][:3]
        outs = refs[n + len(flat) + 3 :]
        k = j = 0
        total = x_ref[...].astype(F32) + b_ref[...]
        for i, ps in enumerate(weights):
            if len(ps) > 1:
                size = ps[0].shape[0]
                held = outs[j]

                @pl.when(pl.program_id(0) == 0)
                def _(held=held, k=k, ps=ps, size=size):
                    for q in range(len(ps)):
                        row = pl.multiple_of(at_ref[CORES + q] * size, size)
                        held[pl.ds(row, size), :] = w[k + q][...]

                value = held[...]
                j += 1
            else:
                value = w[k][...]
            k += len(ps)
            total = total + contract(m[i][...], value, 1, 0)
        normal, scale = norm(total)
        normal_ref[...] = normal
        scale_ref[...] = scale
        low_ref[...] = (normal * g_ref[...] + s_ref[...]).astype(BF16)

    row = pl.BlockSpec((step, d), lambda i, at: (i, 0))
    out_specs = [row, row, pl.BlockSpec((step, 1), lambda i, at: (i, 0))]
    out_shape = [
        jax.ShapeDtypeStruct((rows, d), BF16),
        jax.ShapeDtypeStruct((rows, d), F32),
        jax.ShapeDtypeStruct((rows, 1), F32),
    ]
    for i in cut:
        out_shape.append(
            jax.ShapeDtypeStruct((len(weights[i]) * weights[i][0].shape[0], d), BF16)
        )
        out_specs.append(whole_spec(out_shape[-1]))
    vecs = [v.reshape(1, d) for v in (bias, gain, shift)]
    return pl.pallas_call(
        kernel,
        grid_spec=pltpu.PrefetchScalarGridSpec(
            num_scalar_prefetch=1,
            grid=(rows // step,),
            in_specs=[row]
            + [whole_spec(v) for v in vecs]
            + [pl.BlockSpec((step, m.shape[1]), lambda i, at: (i, 0)) for m in mixed]
            + [whole_spec(p) for p in flat],
            out_specs=out_specs,
        ),
        out_shape=out_shape,
        compiler_params=params(20),
        cost_estimate=cost(),
        name="attended",
    )(at, x, *vecs, *mixed, *flat)


def widened(at, low, bias, *pieces):
    rows, d = low.shape
    n = len(pieces)
    size, width = d // len(BROUGHT), pieces[0].shape[1]
    block, sub = bias.shape[2], min(128, rows)

    def kernel(at_ref, x_ref, b_ref, *refs):
        act_ref, slope_ref = refs[n : n + 2]
        w_ref = refs[0]
        if n > 1:
            w_ref = refs[n + 2]
            for i, (k, j) in enumerate(BROUGHT):
                row = pl.multiple_of(at_ref[i] * size, size)
                w_ref[pl.ds(row, size), :] = refs[k][j * size : (j + 1) * size, :]
        for i in range(0, rows, sub):
            up = contract(x_ref[i : i + sub, :], w_ref[...], 1, 0) + b_ref[0]
            act, slope = gelu_both(up)
            act_ref[i : i + sub, :] = act.astype(BF16)
            slope_ref[i : i + sub, :] = slope.astype(BF16)

    out = jax.ShapeDtypeStruct((rows, width), BF16)
    out_shape = [out, out]
    if n > 1:
        out_shape.append(jax.ShapeDtypeStruct((d, width), BF16))
    return pl.pallas_call(
        kernel,
        grid_spec=pltpu.PrefetchScalarGridSpec(
            num_scalar_prefetch=1,
            grid=(width // block,),
            in_specs=[
                whole_spec(low),
                pl.BlockSpec((1, 1, block), lambda i, at: (3 + i, 0, 0)),
            ]
            + [pl.BlockSpec((p.shape[0], block), lambda i, at: (0, i)) for p in pieces],
            out_specs=[
                pl.BlockSpec((o.shape[0], block), lambda i, at: (0, i))
                for o in out_shape
            ],
        ),
        out_shape=out_shape,
        compiler_params=params(24),
        cost_estimate=cost(),
        name="widened",
    )(at, low, bias, *pieces)


def narrowed(at, normal1, gain1, shift1, bias, gain, shift, grad_output, act, weights):
    rows, d = normal1.shape
    block = 256
    steps = d // block
    flat = [p for w in weights for p in w]
    cut = [w for w in weights if len(w) > 1]
    n = len(act)

    def kernel(at_ref, nm_ref, g1_ref, s1_ref, b_ref, g_ref, s_ref, go_ref, *refs):
        a, w = refs[:n], refs[n : n + len(flat)]
        low_ref, grad_ref, result_ref, sum_ref, acc = refs[n + len(flat) :][:5]
        held = list(refs[n + len(flat) + 5 :])
        total = nm_ref[...] * g1_ref[...] + s1_ref[...] + b_ref[...]
        k = 0
        for i, ps in enumerate(weights):
            value = w[k]
            if len(ps) > 1:
                value = held.pop(0)
                size = value.shape[0] // len(BROUGHT)
                for q, (m, j) in enumerate(BROUGHT):
                    row = pl.multiple_of(at_ref[q] * size, size)
                    value[pl.ds(row, size), :] = w[k + m][j * size : (j + 1) * size, :]
            total = total + contract(a[i][...], value[...], 1, 0)
            k += len(ps)
        acc[pl.program_id(0)] = total

        @pl.when(pl.program_id(0) == steps - 1)
        def _():
            sums = [jnp.zeros((1, d), F32) for _ in range(3)]
            for r in range(0, rows, 64):
                cut = slice(r, r + 64)
                hidden = jnp.concatenate([acc[i, cut, :] for i in range(steps)], axis=1)
                normal, scale = norm(hidden)
                result_ref[cut, :] = (normal * g_ref[...] + s_ref[...]).astype(BF16)
                grad = go_ref[cut, :].astype(F32)
                g_two = norm_back(grad, normal, scale, g_ref[...])
                grad_ref[cut, :] = g_two
                low_ref[cut, :] = g_two.astype(BF16)
                for j, v in enumerate((g_two, grad * normal, grad)):
                    sums[j] = sums[j] + jnp.sum(v, axis=0, keepdims=True)
            for j in range(3):
                sum_ref[j : j + 1, :] = sums[j]

    def col(rows):
        return pl.BlockSpec((rows, block), lambda s, at: (0, s))

    vecs = [v.reshape(1, d) for v in (gain1, shift1, bias, gain, shift)]
    out_shape = [
        jax.ShapeDtypeStruct((rows, d), BF16),
        jax.ShapeDtypeStruct((rows, d), F32),
        jax.ShapeDtypeStruct((rows, d), BF16),
        jax.ShapeDtypeStruct((3, d), F32),
    ]
    return pl.pallas_call(
        kernel,
        grid_spec=pltpu.PrefetchScalarGridSpec(
            num_scalar_prefetch=1,
            grid=(steps,),
            in_specs=[col(rows), col(1), col(1), col(1)]
            + [whole_spec(v) for v in vecs[3:]]
            + [whole_spec(grad_output)]
            + [whole_spec(a) for a in act]
            + [col(p.shape[0]) for p in flat],
            out_specs=[whole_spec(o) for o in out_shape],
            scratch_shapes=[pltpu.VMEM((steps, rows, block), F32)]
            + [pltpu.VMEM((act[0].shape[1], block), BF16) for _ in cut],
        ),
        out_shape=out_shape,
        compiler_params=params(32 if cut else 48),
        cost_estimate=cost(),
        name="narrowed",
    )(at, normal1, *vecs, grad_output, *act, *flat)


def gelu_back(at, g, slope, *pieces):
    rows, d = g.shape
    width = slope.shape[1]
    n = len(pieces)
    size = min(512, width)

    def kernel(at_ref, g_ref, s_ref, *refs):
        out_ref, sum_ref = refs[n : n + 2]
        w = refs[0][...]
        if n > 1:
            held, cut = refs[n + 2], width // len(BROUGHT)

            @pl.when(pl.program_id(0) == 0)
            def _():
                for i, (k, j) in enumerate(BROUGHT):
                    row = pl.multiple_of(at_ref[i] * cut, cut)
                    held[pl.ds(row, cut), :] = refs[k][j * cut : (j + 1) * cut, :]

            w = held[pl.ds(pl.multiple_of(pl.program_id(0) * size, size), size), :]
        low = (contract(g_ref[...], w, 1, 1) * s_ref[...].astype(F32)).astype(BF16)
        out_ref[...] = low
        sum_ref[...] = jnp.sum(low.astype(F32), axis=0, keepdims=True)

    def column(rows):
        return pl.BlockSpec((rows, size), lambda s, at: (0, s))

    w_specs = [pl.BlockSpec((size, d), lambda s, at: (s, 0))]
    return pl.pallas_call(
        kernel,
        grid_spec=pltpu.PrefetchScalarGridSpec(
            num_scalar_prefetch=1,
            grid=(width // size,),
            in_specs=[whole_spec(g), column(rows)]
            + ([whole_spec(p) for p in pieces] if n > 1 else w_specs),
            out_specs=[column(rows), column(1)],
            scratch_shapes=[pltpu.VMEM((width, d), BF16)] if n > 1 else [],
        ),
        out_shape=[
            jax.ShapeDtypeStruct((rows, width), BF16),
            jax.ShapeDtypeStruct((1, width), F32),
        ],
        compiler_params=params(24),
        cost_estimate=cost(),
        name="gelu_back",
    )(at, g, slope, *pieces)


def attended_back(g_two, normal, scale, gain, g_up, up_w):
    rows, d = g_two.shape
    block = 256
    steps, n = d // block, len(g_up)

    def kernel(g2_ref, nm_ref, sc_ref, gain_ref, *refs):
        g, w = refs[:n], refs[n : 2 * n]
        low_ref, grad_ref, sum_ref, acc = refs[2 * n :]
        total = g2_ref[...]
        for i in range(n):
            total = total + contract(g[i][...], w[i][...], 1, 1)
        acc[pl.program_id(0)] = total

        @pl.when(pl.program_id(0) == steps - 1)
        def _():
            sums = [jnp.zeros((1, d), F32) for _ in range(3)]
            for r in range(0, rows, 64):
                cut = slice(r, r + 64)
                g_in = jnp.concatenate([acc[i, cut, :] for i in range(steps)], axis=1)
                nm = nm_ref[cut, :]
                g_one = norm_back(g_in, nm, sc_ref[cut, :], gain_ref[...])
                grad_ref[cut, :] = g_one
                low_ref[cut, :] = g_one.astype(BF16)
                for j, v in enumerate((g_one, g_in * nm, g_in)):
                    sums[j] = sums[j] + jnp.sum(v, axis=0, keepdims=True)
            for j in range(3):
                sum_ref[j : j + 1, :] = sums[j]

    out_shape = [
        jax.ShapeDtypeStruct((rows, d), BF16),
        jax.ShapeDtypeStruct((rows, d), F32),
        jax.ShapeDtypeStruct((3, d), F32),
    ]
    gain = gain.reshape(1, d)
    return pl.pallas_call(
        kernel,
        grid=(steps,),
        in_specs=[pl.BlockSpec((rows, block), lambda s: (0, s))]
        + [whole_spec(a) for a in (normal, scale, gain, *g_up)]
        + [pl.BlockSpec((block, w.shape[1]), lambda s: (s, 0)) for w in up_w],
        out_specs=[whole_spec(o) for o in out_shape],
        out_shape=out_shape,
        scratch_shapes=[pltpu.VMEM((steps, rows, block), F32)],
        compiler_params=params(28 if n > 1 else 48),
        cost_estimate=cost(),
        name="attended_back",
    )(g_two, normal, scale, gain, *g_up, *up_w)


def input_grad(g_one, g_proj, qkv_w):
    rows, d = g_one.shape
    width, n = g_proj[0].shape[2], len(g_proj)
    block = 256

    def kernel(g1_ref, *refs):
        g, w, out_ref = refs[:n], refs[n : 2 * n], refs[-1]
        total = g1_ref[...]
        for i in range(n):
            for c in range(3):
                total = total + contract(g[i][c], w[i][c], 1, 1)
        out_ref[...] = total

    col = pl.BlockSpec((rows, block), lambda s: (0, s))
    return pl.pallas_call(
        kernel,
        grid=(d // block,),
        in_specs=[col]
        + [whole_spec(g) for g in g_proj]
        + [pl.BlockSpec((3, block, width), lambda s: (0, s, 0))] * n,
        out_specs=col,
        out_shape=jax.ShapeDtypeStruct((rows, d), F32),
        compiler_params=params(24),
        cost_estimate=cost(),
        name="input_grad",
    )(g_one, *g_proj, *qkv_w)


def pick(index, pieces):
    n = len(pieces)
    views = [(i, j) for i, p in enumerate(pieces) for j in range(len(p[3]))]

    def kernel(index_ref, *refs):
        for v, (i, j) in enumerate(views):
            axis, size = pieces[i][1:3]
            at = tuple([slice(None)] * axis + [slice(j * size, (j + 1) * size)])
            refs[len(views) + i][at] = refs[v][...]

    specs, shapes = [], []
    for i, j in views:
        a, axis, size, places = pieces[i]
        specs.append(
            pl.BlockSpec(
                a.shape[:axis] + (size,) + a.shape[axis + 1 :],
                lambda s, at, p=places[j], axis=axis, n=a.ndim: tuple(
                    at[p] if k == axis else 0 for k in range(n)
                ),
            )
        )
    for a, axis, size, places in pieces:
        shape = a.shape[:axis] + (size * len(places),) + a.shape[axis + 1 :]
        shapes.append(jax.ShapeDtypeStruct(shape, a.dtype))
    return pl.pallas_call(
        kernel,
        grid_spec=pltpu.PrefetchScalarGridSpec(
            num_scalar_prefetch=1,
            grid=(1,),
            in_specs=specs,
            out_specs=[whole_spec(s) for s in shapes],
        ),
        out_shape=shapes,
        compiler_params=params(60),
        cost_estimate=cost(),
        name="pick",
    )(index, *[pieces[i][0] for i, _ in views])


def add(a, b):
    return (a.astype(F32) + b.astype(F32)).astype(BF16)


def add_split(bits, which, a, b):
    rows, columns = a.shape
    half = rows // 2
    if half % 16:
        total, bit = add(a, b), bits[BITS + which]
        return (
            lax.dynamic_slice_in_dim(total, bit * half, half, 0),
            lax.dynamic_slice_in_dim(total, (1 - bit) * half, half, 0),
        )
    block = half // 2 if half >= 256 else half
    per = half // block

    def kernel(bits_ref, a0, b0, a1, b1, keep_ref, send_ref):
        send_ref[...] = add(a1[...], b1[...])
        keep_ref[...] = add(a0[...], b0[...])

    def spec(of):
        return pl.BlockSpec((block, columns), lambda s, bits: (of(s, bits), 0))

    kept = spec(lambda s, bits: bits[BITS + which] * per + s)
    sent = spec(lambda s, bits: (1 - bits[BITS + which]) * per + s)
    plain = spec(lambda s, bits: s)
    out = jax.ShapeDtypeStruct((half, columns), BF16)
    return pl.pallas_call(
        kernel,
        grid_spec=pltpu.PrefetchScalarGridSpec(
            num_scalar_prefetch=1,
            grid=(per,),
            in_specs=[kept, kept, sent, sent],
            out_specs=[plain, plain],
        ),
        out_shape=[out, out],
        compiler_params=params(12),
        cost_estimate=cost(),
        name="add_split",
    )(bits, a, b, a, b)


def grad_stack(bits, outs, rows, width):
    jobs = [job for out in outs for job in out]
    sizes = [sum(job[4] for job in out) for out in outs]

    def depth_of(a):
        a = a[0] if isinstance(a, tuple) else a
        return a.shape[-2]

    depth = depth_of(jobs[0][0])
    total = sum(sizes)

    def kernel(bits_ref, *refs):
        s = pl.program_id(0)
        at = first = 0
        j = 0
        for o, out in enumerate(outs):
            for job in out:

                @pl.when((s >= at) & (s < at + job[4]))
                def _(j=j, o=o):
                    x1, y1, x2, y2 = (
                        r[0] if len(r.shape) == 3 else r[...]
                        for r in refs[4 * j : 4 * j + 4]
                    )
                    value = contract(x1, y1, 0, 0) + contract(x2, y2, 0, 0)
                    refs[4 * len(jobs) + o][...] = value.astype(BF16)

                at += job[4]
                j += 1

    def column(place, bits):
        return place[0] + sum(k * bits[BITS + i] for i, k in enumerate(place[1:]) if k)

    def spec(a, block, of):
        if isinstance(a, tuple):
            return pl.BlockSpec((1, *block), lambda s, bits: (a[1], 0, of(s, bits)))
        return pl.BlockSpec(block, lambda s, bits: (0, of(s, bits)))

    specs, args, at = [], [], 0
    for a1, b1, a2, b2, n, a_at, b_at in jobs:

        def a_of(s, bits, at=at, n=n, p=a_at):
            return column(p, bits) + jnp.clip(s - at, 0, n - 1)

        def b_of(s, bits, p=b_at):
            return column(p, bits)

        for a, b in ((a1, b1), (a2, b2)):
            specs += [spec(a, (depth, rows), a_of), spec(b, (depth, width), b_of)]
            args += [a, b]
        at += n
    out_specs, at = [], 0
    for size in sizes:
        out_specs.append(
            pl.BlockSpec(
                (rows, width),
                lambda s, bits, at=at, n=size: (jnp.clip(s - at, 0, n - 1), 0),
            )
        )
        at += size
    return pl.pallas_call(
        kernel,
        grid_spec=pltpu.PrefetchScalarGridSpec(
            num_scalar_prefetch=1, grid=(total,), in_specs=specs, out_specs=out_specs
        ),
        out_shape=[jax.ShapeDtypeStruct((n * rows, width), BF16) for n in sizes],
        compiler_params=params(24),
        cost_estimate=cost(),
        name="grad_stack",
    )(bits, *[a[0] if isinstance(a, tuple) else a for a in args])


class Box:
    def __init__(self, value):
        self.value = value


class Steps:
    def __init__(self):
        self.kept = []

    def keep(self, value):
        self.kept.append(Box(value))
        return self.kept[-1]

    def fence(self):
        held = lax.optimization_barrier(tuple(b.value for b in self.kept))
        for b, value in zip(self.kept, held):
            b.value = value

    def __call__(self, name, work, *ins):
        self.fence()
        with jax.named_scope(name):
            out = work(*[b.value for b in ins])
        out = [self.keep(v) for v in jax.tree.leaves(out)]
        self.fence()
        return out

    def wait(self, flight):
        self.kept.append(flight)
        self.fence()


class Moves:
    def __init__(self, n_dp, n_tensor):
        self.n_dp, self.n_tensor = n_dp, n_tensor
        self.dp = lax.axis_index("dp")
        self.core = self.dp & 1
        self.chip_bits = [b for b in (2, 4, 8, 16, 32, 64) if b < n_dp]

    def bit(self, mask):
        return (self.dp // mask) & 1

    def index(self, masks):
        return sum(self.bit(m) << i for i, m in enumerate(masks))

    def over(self, a, axis, mask, name):
        with jax.named_scope(name):
            n = self.n_dp if axis == "dp" else self.n_tensor
            return Box(lax.ppermute(a.value, axis, [(i, i ^ mask) for i in range(n)]))


def widen(core, sources, block, out_shape, steps, name):
    n, count = len(sources), len(steps[0])
    tables = []
    for bit in (0, 1):
        rows = np.zeros((n + 1 + len(out_shape), count), np.int32)
        for q in range(n):
            used = [s for s in range(count) if steps[bit][s][0] == q]
            for s in range(count):
                later = [u for u in used if u >= s]
                at = later[0] if later else used[-1]
                rows[q, s] = steps[bit][at][1]
        for s in range(count):
            rows[n, s] = steps[bit][s][0]
            rows[n + 1 :, s] = steps[bit][s][2]
        tables.append(rows)
    table = jnp.where(core == 0, jnp.asarray(tables[0]), jnp.asarray(tables[1]))

    def kernel(table_ref, *refs):
        s = pl.program_id(0)
        for q in range(n):

            @pl.when(table_ref[n, s] == q)
            def _():
                refs[n][...] = refs[q][...].astype(F32).reshape(refs[n].shape)

    lead = len(out_shape) - 2
    return pl.pallas_call(
        kernel,
        grid_spec=pltpu.PrefetchScalarGridSpec(
            num_scalar_prefetch=1,
            grid=(count,),
            in_specs=[
                pl.BlockSpec(block, lambda s, t, q=q: (t[q, s], 0)) for q in range(n)
            ],
            out_specs=pl.BlockSpec(
                (1,) * lead + block,
                lambda s, t: tuple(t[n + 1 + j, s] for j in range(len(out_shape))),
            ),
        ),
        out_shape=jax.ShapeDtypeStruct(out_shape, F32),
        compiler_params=params(24),
        cost_estimate=cost(),
        name=name,
    )(table, *sources)


def spread(gathered, unit, tables, block, out_shape, name):
    count, views = len(tables), len(tables[0][0])
    columns = gathered.shape[-1]
    lead = len(out_shape) - 2
    table = np.asarray([list(t[0]) + list(t[1]) for t in tables], np.int32).T

    def kernel(table_ref, *refs):
        out = refs[views]
        for v in range(views):
            part = refs[v][0].astype(F32)
            if lead:
                out[0, v * unit : (v + 1) * unit, :] = part
            else:
                out[v * unit : (v + 1) * unit, :] = part

    return pl.pallas_call(
        kernel,
        grid_spec=pltpu.PrefetchScalarGridSpec(
            num_scalar_prefetch=1,
            grid=(count,),
            in_specs=[
                pl.BlockSpec((1, unit, columns), lambda s, t, v=v: (t[v, s], 0, 0))
                for v in range(views)
            ],
            out_specs=pl.BlockSpec(
                (1,) * lead + block,
                lambda s, t: tuple(t[views + j, s] for j in range(len(out_shape))),
            ),
        ),
        out_shape=jax.ShapeDtypeStruct(out_shape, F32),
        compiler_params=params(40),
        cost_estimate=cost(),
        name=name,
    )(jnp.asarray(table), *[gathered.reshape(-1, unit, columns)] * views)


START, LATENCY = 1.4, 3.0
RATES = {"y": 46e3, "x": 46e3, "z": 46e3, "core": 500e3}
GATHER = 52.0
FLIGHTS = 5
MARGIN, PATIENCE = 4.0, 8.0


class Plan:
    def __init__(self, mv):
        self.mv, self.steps = mv, Steps()
        self.box, self.when, self.free = {}, {}, {}
        self.tasks, self.flying, self.waiting = [], [], []
        self.clock, self.gap, self.sent, self.flown = 0.0, 0, {}, {}
        LOG.clear()
        FLOWN.clear()

    def given(self, **arrays):
        for key, value in arrays.items():
            self.box[key], self.when[key] = self.steps.keep(value), 0.0

    def task(self, name, rank, cost, needs, makes, work, sends=()):
        self.tasks.append((rank, len(self.tasks), name, cost, needs, makes, work, sends))

    def link(self, axis, mask):
        if axis == "tensor":
            return "y", mask
        if mask < 4:
            return ("core", "x")[mask // 2], 1
        return "z", mask // 4

    def send(self, new, key, axis, mask):
        a = self.box[key]
        if mask is None:
            with jax.named_scope(new):
                self.box[new] = Box(lax.all_gather(a.value, axis))
            self.clock += 0.7
            self.free["sc"] = max(self.free.get("sc", 0.0), self.clock) + GATHER
            self.when[new] = self.free["sc"]
            return
        while len(self.flying) >= FLIGHTS:
            self.land(min(self.flying, key=lambda k: self.when[k]))
        self.box[new] = self.mv.over(a, axis, mask, new)
        link, often = self.link(axis, mask)
        took = often * a.value.size * a.value.dtype.itemsize / RATES[link]
        self.clock += 0.5 if link == "core" else START
        self.free[link] = max(self.free.get(link, 0.0), self.clock) + took
        self.when[new] = self.free[link] + (1.0 if link == "core" else LATENCY)
        self.flying.append(new)
        self.sent[new] = (self.gap,)
        self.flown[new] = (a.value.size * a.value.dtype.itemsize, link, took)
        FLOWN.append((new, self.clock, self.when[new]))

    def send_due(self):
        for s in list(self.waiting):
            after = s[4] if len(s) > 4 else None
            if after and not (after in self.when and self.when[after] <= self.clock):
                continue
            if after in self.flying:
                self.land(after)
            self.waiting.remove(s)
            held = []
            if s[3] is not None:
                value = self.box[s[1]].value
                size = value.size * value.dtype.itemsize
                held = [
                    k
                    for k in self.flying
                    if self.sent[k][0] < self.gap and self.flown[k][0] <= size
                ]
                for k in [k for k in held if self.when[k] <= self.clock + PATIENCE]:
                    self.land(k)
                    held.remove(k)
            for k in held:
                self.free[self.flown[k][1]] = max(
                    [self.clock]
                    + [
                        self.when[j] - LATENCY
                        for j in self.flying
                        if j not in held and self.flown[j][1] == self.flown[k][1]
                    ]
                )
            self.send(*s[:4])
            for k in held:
                if k in self.flying:
                    _, link, took = self.flown[k]
                    self.sent[k] = (self.gap,)
                    self.free[link] = max(self.free[link], self.clock) + took
                    self.when[k] = self.free[link] + LATENCY
                    HELD.append((k, s[0]))

    def land(self, key):
        self.flying.remove(key)
        self.steps.wait(self.box[key])
        self.clock = max(self.clock, self.when[key])

    def run(self):
        while self.tasks:
            self.send_due()
            known = [
                t
                for t in sorted(self.tasks, key=lambda t: t[:2])
                if all(k in self.when for k in t[4])
            ]
            start = {
                t[1]: max([self.when[k] for k in t[4]] + [self.clock]) for t in known
            }
            soonest = min(start.values(), default=1e9)
            due = [self.when[s[4]] for s in self.waiting if s[4] in self.when]
            if due and min(due) <= soonest:
                self.clock = max(self.clock, min(due))
                continue
            chosen = next(t for t in known if start[t[1]] <= soonest + 0.01)
            self.tasks.remove(chosen)
            rank, _, name, cost, needs, makes, work, sends = chosen
            self.clock = begun = start[chosen[1]]
            for key in sorted(self.flying, key=lambda k: self.when[k]):
                if self.when[key] <= self.clock - MARGIN and key not in needs:
                    self.land(key)
            for key in needs:
                if key in self.flying:
                    self.flying.remove(key)
                    if work is None:
                        self.steps.wait(self.box[key])
            if work is not None:
                COST[0] = cost
                out = self.steps(name, work, *[self.box[k] for k in needs])
                self.clock += cost
                self.gap += 1
                for key, b in zip(makes, out, strict=True):
                    self.box[key], self.when[key] = b, self.clock
            LOG.append((name, begun, self.clock, [s[0] for s in sends]))
            self.waiting += sends


    def fetch(self, rank, name, d, masks, axis):
        y, sib = f"{name}.y{d}", f"{name}.sib{d}"
        cut = [f"{name}.cut{i}.{d}" for i in (0, 1)]
        come = [f"{name}.c{i}.{d}" for i in (0, 1)]
        far = [f"{name}.far{i}.{d}" for i in (0, 1)]
        self.task(f"{sib}.send", rank, 0.0, [y], [], None, [(sib, y, "dp", 1)])
        self.task(
            f"{name}.cut{d}",
            rank + 0.01,
            1.3,
            [y],
            cut,
            lambda a: jnp.split(a, 2, axis),
            [(c, k, "dp", m) for c, k, m in zip(come, cut, masks)],
        )
        for c, f in zip(come, far):
            self.task(f, rank, 0.0, [c], [], None, [(f, c, "dp", 1)])
        return [y, sib, *come, *far]


    def reduce(self, rank, name, levels, back=False):
        s = self.mv.n_tensor // 2
        cur = [f"{name}.p{d}" for d in range(2 * s)]
        while s > 1:
            new = [f"{name}.p{d}.{s}" for d in range(s)]
            for d in range(s):
                far = d >= s // 2
                self.task(
                    new[d],
                    rank,
                    1.5,
                    [cur[d], f"{name}.y{d + s}.{s}"],
                    [new[d]],
                    lambda a, b: [add(a, b)],
                    [(f"{name}.y{d}.{s // 2}", new[d], "tensor", s // 2)] * far,
                )
            cur, s = new, s // 2
        needs = [cur[0], f"{name}.y1.1"]
        costs = (2.0, 1.3, 0.9, 0.9, 0.9)
        for i, m in enumerate(levels):
            keep, send, come = f"{name}.k{i}", f"{name}.s{i}", f"{name}.d{i}"

            def work(info, a, b, m=m):
                return add_split(info, m.bit_length() - 1, a, b)

            self.task(
                send,
                rank,
                costs[i],
                ["info", *needs],
                [keep, send],
                work,
                [(come, send, "dp", m)],
            )
            needs = [keep, come]
        own, up = f"{name}.own", list(reversed(levels)) + [1]
        sends = [(f"{name}.u0", own, "dp", up[0])] if back else []
        self.task(own, rank, 0.5, needs, [own], lambda a, b: [add(a, b)], sends)
        for i, m in enumerate(up[:-1] if back else []):
            last = i + 2 == len(up)
            out = f"{name}.mine" if last else f"{name}.j{i}"
            come = f"{name}.other" if last else f"{name}.u{i + 1}"

            def work(a, b, m=m):
                bit = self.mv.bit(m)
                low, high = jnp.where(bit == 0, a, b), jnp.where(bit == 0, b, a)
                return [jnp.concatenate([low, high], axis=0)]

            self.task(
                out,
                rank,
                1.0,
                [own, f"{name}.u{i}"],
                [out],
                work,
                [(come, out, "dp", up[i + 1])],
            )
            own = out

    def gather(self, rank, name, chunks):
        self.task(
            name,
            rank,
            0.8,
            [f"{c}.own" for c in chunks],
            [name],
            lambda *a: [jnp.concatenate(a, axis=0) if len(a) > 1 else a[0]],
            [(f"{name}.all", name, "dp", None)],
        )


def plain(
    n_dp,
    n_tensor,
    x,
    qkv_weight,
    qv_bias,
    out_weight,
    out_bias,
    norm1_gain,
    norm1_shift,
    up_weight,
    up_bias,
    down_weight,
    down_bias,
    norm2_gain,
    norm2_shift,
    lengths,
    grad_output,
):
    width = x.shape[1]

    def whole(w, axis):
        return lax.all_gather(w, "tensor", axis=axis, tiled=True)

    info = jnp.zeros((BITS + 1,), jnp.int32)
    length = lax.dynamic_slice_in_dim(lengths, lax.axis_index("tensor"), 1, 0)
    q_bias, v_bias = whole(qv_bias, 1)
    bias = [q_bias, jnp.zeros_like(q_bias), v_bias, whole(up_bias, 0).astype(F32)]
    bias = jnp.concatenate(bias).reshape(-1, 1, width)
    qkv_w, out_w = whole(qkv_weight, 2), whole(out_weight, 0)
    up_w, down_w = whole(up_weight, 1), whole(down_weight, 0)
    (qkv,) = project(info, x, bias, qkv_w)
    mixed, lse = attend(length, qkv)
    normed, normal1, scale1 = attended(
        info, x, out_bias, norm1_gain, norm1_shift, [mixed], [[out_w]]
    )
    act, slope = widened(info, normed, bias, up_w)
    g2, g_two, result, sums2 = narrowed(
        info,
        normal1,
        norm1_gain,
        norm1_shift,
        down_bias,
        norm2_gain,
        norm2_shift,
        grad_output,
        [act],
        [[down_w]],
    )
    g_up, up_sum = gelu_back(info, g2, slope, down_w)
    g1, g_one, sums1 = attended_back(
        g_two, normal1, scale1, norm1_gain, [g_up], [up_w]
    )
    g_qkv, qkv_sum = attend_back(length, qkv, g1, out_w, lse)
    g_input = input_grad(g_one, [g_qkv], [qkv_w])

    def total(a, axis):
        part = lax.psum_scatter(a, "tensor", scatter_dimension=axis, tiled=True)
        return lax.psum(part, "dp")

    grad_qkv = jnp.stack([contract(x, g_qkv[c], 0, 0) for c in range(3)])
    small = lax.psum(jnp.concatenate([sums1, sums2]), ("dp", "tensor"))
    return (
        result,
        g_input,
        total(grad_qkv, 2),
        total(jnp.stack([qkv_sum[0], qkv_sum[2]]), 1),
        total(contract(mixed, g1, 0, 0), 0),
        small[0],
        small[1],
        small[2],
        total(contract(normed, g_up, 0, 0), 1),
        total(up_sum[0], 0),
        total(contract(act, g2, 0, 0), 0),
        small[3],
        small[4],
        small[5],
    )


def body(
    n_dp,
    n_tensor,
    x,
    qkv_weight,
    qv_bias,
    out_weight,
    out_bias,
    norm1_gain,
    norm1_shift,
    up_weight,
    up_bias,
    down_weight,
    down_bias,
    norm2_gain,
    norm2_shift,
    lengths,
    grad_output,
):
    mv = Moves(n_dp, n_tensor)
    plan = Plan(mv)
    task = plan.task
    parts = range(n_tensor)
    back = list(parts)[::-1]
    width = x.shape[1]
    half = width // 2
    core = mv.core
    hw = qkv_weight.shape[2]
    fw = up_weight.shape[1]
    same = hw == half
    X, Z1, Z = 2, 4, tuple(mv.chip_bits[1:])

    mine_x, mine_z = mv.index((X, 1)), mv.index((Z1, 1))
    place = [mine_x ^ i for i in range(4)] + [4 + (mine_z ^ i) for i in range(4)]
    place += [core, 1 - core, mv.dp]
    place += [mv.bit(m) for m in (1, *mv.chip_bits)]

    plan.given(
        info=jnp.stack(place).astype(jnp.int32),
        lengths=lengths,
        x=x,
        qkv_w0=qkv_weight,
        out_w0=out_weight,
        up_w0=up_weight,
        down_w0=down_weight,
        qv_bias=qv_bias,
        up_bias=up_bias,
        grad_output=grad_output,
    )

    def others(name):
        return [(f"{name}.y{d}", name, "tensor", d) for d in parts[1:]]

    def swap(key):
        return (f"{key}.sib", key, "dp", 1)

    def keys(name):
        return [f"{name}{d}" for d in parts]

    both = (AT, AT + 4)

    def pick_q(info, q):
        return pick(info, [(q, 1, width // 8, both)])

    def pick_ou(info, o, u, _):
        return pick(info, [(o, 0, hw // 2, (CORES,)), (u, 0, width // 8, both)])

    def pick_d(info, d, _):
        return pick(info, [(d, 0, fw // 8, both)])

    task(
        "pick_q",
        0,
        2.8,
        ["info", "qkv_w0"],
        ["q"],
        pick_q,
        [(*s, "bias1") for s in others("q")],
    )
    task(
        "length",
        0.5,
        1.0,
        ["lengths"],
        ["length"],
        lambda n: [lax.dynamic_slice_in_dim(n, lax.axis_index("tensor"), 1, 0)],
    )

    def bias_rows(qv, up):
        q, v = qv[0], qv[1]
        rows = jnp.concatenate([q, jnp.zeros_like(q), v, up.astype(F32)])
        return [rows.reshape(-1, 1, hw)]

    task(
        "bias0",
        -1,
        1.5,
        ["qv_bias", "up_bias"],
        ["bias0"],
        bias_rows,
        [(f"bias{d}", "bias0", "tensor", d) for d in parts[1:]],
    )
    task(
        "pick_ou",
        1.0,
        3.2,
        ["info", "out_w0", "up_w0", "qkv0"],
        ["o", "u"],
        pick_ou,
        [(*s, "q.y1") for s in others("o")] + [(*s, "o.y1") for s in others("u")],
    )
    task(
        "pick_d",
        2.5,
        3.0,
        ["info", "down_w0", "heads0"],
        ["d"],
        pick_d,
        [(*s, "u.y1") for s in others("d")],
    )
    qkv_from, out_from = [["qkv_w0"]], [["out_w0"]]
    up_from, down_from = [["up_w0"]], [["down_w0"]]
    for d in parts[1:]:
        qkv_from.append(plan.fetch(0.2, "q", d, (X, Z1), 1))
        o = f"o.y{d}"
        task(f"o.sib{d}", 0.3, 0.0, [o], [], None, [(f"o.sib{d}", o, "dp", 1)])
        out_from.append([o, f"o.sib{d}"])
        up_from.append(plan.fetch(0.4, "u", d, (X, Z1), 0))
        down_from.append(plan.fetch(0.5, "d", d, (X, Z1), 0))

    for d in parts:
        made = [f"qkv{d}", f"qkv_w{d}"] if d else [f"qkv{d}"]
        task(
            f"project{d}",
            2 + d,
            4.5 if d else 3.5,
            ["info", "x", f"bias{d}", *qkv_from[d]],
            made,
            lambda info, x, b, *w: project(info, x, b, *w),
        )
        task(
            f"heads{d}",
            2 + d,
            6.5,
            ["length", f"qkv{d}"],
            [f"heads{d}", f"lse{d}"],
            attend,
            [],
        )

    def split_args(a, groups):
        out, at = [], 0
        for g in groups:
            out.append(a[at : at + len(g)])
            at += len(g)
        return out

    def attended_task(info, x, *rest):
        mixed, weights = rest[:n_tensor], split_args(rest[n_tensor:], out_from)
        return attended(
            info, x, out_bias, norm1_gain, norm1_shift, mixed, weights
        )

    task(
        "attended",
        20,
        5.0,
        ["info", "x", *keys("heads"), *[k for g in out_from for k in g]],
        ["normed", "normal1", "scale1", *keys("out_w")[1:]],
        attended_task,
        [(*swap("normed"), "u.y1")],
    )
    for d in parts:
        task(
            f"widened{d}",
            21 + d,
            10.0,
            ["info", "normed", f"bias{d}", *up_from[d]],
            [f"act{d}", f"slope{d}"] + [f"up_w{d}"] * (d > 0),
            widened,
            [(*swap(f"act{d}"), "d.y1")],
        )

    def narrowed_task(info, normal1, grad_output, *rest):
        act, weights = rest[:n_tensor], split_args(rest[n_tensor:], down_from)
        low, g_two, result, sums = narrowed(
            info,
            normal1,
            norm1_gain,
            norm1_shift,
            down_bias,
            norm2_gain,
            norm2_shift,
            grad_output,
            act,
            weights,
        )
        return low, g_two, result, sums

    task(
        "narrowed",
        40,
        14.5,
        ["info", "normal1", "grad_output", *keys("act")]
        + [k for g in down_from for k in g],
        ["g2", "g_two", "result", "sums2"],
        narrowed_task,
        [swap("g2")] + [swap(k) for k in ("x", *keys("heads"))],
    )

    block = fw // 4

    def made(name, rank, cost, items, rows, columns, after=None, of=back):
        args = []
        for d in of:
            for a, _, b, _, *_ in items(d):
                args += [a, b, f"{a}.sib", f"{b}.sib"]

        def work(info, *a):
            outs, at = [], 0
            for d in of:
                jobs = []
                for _, ai, _, bi, *rest in items(d):
                    a1, b1, a2, b2 = a[at : at + 4]
                    a1, a2 = ((v if ai is None else (v, ai)) for v in (a1, a2))
                    b1, b2 = ((v if bi is None else (v, bi)) for v in (b1, b2))
                    jobs.append((a1, b1, a2, b2, *rest))
                    at += 4
                outs.append(jobs)
            return grad_stack(info, outs, rows, columns)

        s = n_tensor // 2
        task(
            f"{name}.p{of[0]}",
            rank,
            cost,
            ["info", *args],
            [f"{name}.p{d}" for d in of],
            work,
            [
                (f"{name}.y{d}.{s}", f"{name}.p{d}", "tensor", s, after)
                for d in of
                if d >= s
            ],
        )

    chunks = {}
    first_y = f"{n_tensor // 2}.{n_tensor // 2}"

    def chunk(rank, name, levels, rows, back=False):
        chunks[name] = (levels, rows)
        plan.reduce(rank, name, levels, back)

    made(
        "down",
        51.5,
        9.5,
        lambda d: [(f"act{d}", None, "g2", None, 4, (0,), (0, 1))],
        block,
        half,
    )
    chunk(1.0, "down", (X, *Z), fw)
    for i, d in enumerate(back):
        task(
            f"gelu_back{d}",
            51 + i,
            6.5,
            ["info", "g2", f"slope{d}", *down_from[d]],
            [f"g_up{d}", f"up_sum{d}"],
            gelu_back,
            [(*swap(f"g_up{d}"), None if d else f"down.y{first_y}")],
        )
    for i, of in enumerate((back[: n_tensor // 2], back[n_tensor // 2 :])):
        made(
            "up",
            64 + 4 * i,
            5.5,
            lambda d: [("normed", None, f"g_up{d}", None, 2, (0, 2), (0,))],
            half // 2,
            fw,
            f"down.y{first_y}",
            of,
        )
    chunk(1.2, "up", (X, *Z), half)

    def attended_back_task(g_two, normal, scale, *rest):
        return attended_back(
            g_two, normal, scale, norm1_gain, rest[:n_tensor], rest[n_tensor:]
        )

    task(
        "attended_back",
        56,
        11.5,
        ["g_two", "normal1", "scale1", *keys("g_up"), *keys("up_w")],
        ["g1", "g_one", "sums1"],
        attended_back_task,
        [(*swap("g1"), f"down.y{first_y}")],
    )
    for i, d in enumerate(back):
        task(
            f"heads_back{d}",
            62 + i,
            12.0,
            ["length", f"qkv{d}", "g1", f"out_w{d}", f"lse{d}"],
            [f"g_qkv{d}", f"qkv_sum{d}"],
            attend_back,
            [(*swap(f"g_qkv{d}"), f"down.y{first_y}")],
        )

    def out_item(d):
        return (f"heads{d}", None, "g1", None, 1, (0,), (0, 1))

    def qkv_item(c):
        return lambda d: ("x", None, f"g_qkv{d}", c, 1, (0, 1), (0,))

    if same:
        groups = {"att0": [out_item, qkv_item(2)], "att1": [qkv_item(1), qkv_item(0)]}
    else:
        groups = {"att0": [out_item], "att1": [qkv_item(c) for c in (2, 1, 0)]}
    for i, (name, items) in enumerate(groups.items()):
        rows = hw if items[0] is out_item else half
        made(
            name,
            66 + i,
            7.5,
            lambda d, items=items: [it(d) for it in items],
            rows,
            half if items[0] is out_item else hw,
            f"{('up', 'att0')[i]}.y{first_y}",
        )
        chunk(1.4 + 0.1 * i, name, (X, *Z), rows * len(items), back=True)

    def pack(one, two, *rest):
        packs = []
        for d in parts:
            g, up = rest[2 * d : 2 * d + 2]
            packs.append(
                jnp.concatenate([one.ravel(), two.ravel(), g[0], g[2], up[0]])
            )
        return packs

    needs = [k for d in parts for k in (f"qkv_sum{d}", f"up_sum{d}")]
    packs, s = keys("pack"), n_tensor // 2
    task(
        "pack",
        70,
        3.0,
        ["sums1", "sums2", *needs],
        packs,
        pack,
        [
            (f"pack{d}.y", f"pack{d}", "tensor", s, f"att1.y{first_y}")
            for d in range(s, n_tensor)
        ],
    )
    while s:
        new = [f"small{s}.{d}" for d in range(s)]
        for d in range(s):
            if s > 1:
                sends = [(f"{new[d]}.y", new[d], "tensor", s // 2)] * (d >= s // 2)
            else:
                sends = [("small.1", new[0], "dp", 1)]
            task(
                new[d],
                2.0,
                0.6,
                [packs[d], f"{packs[d + s]}.y"],
                [new[d]],
                lambda a, b: [a + b],
                sends,
            )
        packs, s = new, s // 2
    last, masks = packs[0], [1, *mv.chip_bits]
    for i, m in enumerate(masks):
        out = f"small.at{m}"
        nxt = masks[i + 1] if i + 1 < len(masks) else None
        sends = [(f"small.{nxt}", out, "dp", nxt)] if nxt else []
        task(out, 2.0, 0.6, [last, f"small.{m}"], [out], lambda a, b: [a + b], sends)
        last = out

    task(
        "input_grad",
        80,
        9.0,
        ["g_one", *keys("g_qkv"), *keys("qkv_w")],
        ["g_input"],
        lambda g, *a: [input_grad(g, a[:n_tensor], a[n_tensor:])],
    )

    def results(group, names, outputs):
        plan.gather(1.9, group, names)
        per_device = [chunks[n][1] // (n_dp // 2) for n in names]
        unit = min(per_device)
        total = sum(per_device) // unit
        first = {n: sum(per_device[:i]) // unit for i, n in enumerate(names)}

        def at(c, name, row):
            levels, rows = chunks[name]
            own = rows // (n_dp // 2)
            r, dp = row // own, c
            for i, m in enumerate(reversed(levels)):
                dp |= m * ((r >> i) & 1)
            return dp * total + first[name] + row % own // unit

        for name, cost, blocks, block, shape in outputs:
            tables = [
                ([at(c, n, row + r) for r in range(0, block[0], unit)], place)
                for c, n, row, place in blocks
            ]
            task(
                name,
                85,
                cost,
                [f"{group}.all"],
                [name],
                lambda a, *, rest=(unit, tables, block, shape, name): [
                    spread(a, *rest)
                ],
            )

    results(
        "down_all",
        ("down",),
        [
            (
                "grad_down",
                6.0,
                [(c, "down", r * block, (r, c)) for r in range(4) for c in (0, 1)],
                (block, half),
                (fw, width),
            )
        ],
    )
    rows = half // 4
    results(
        "up_all",
        ("up",),
        [
            (
                "grad_up",
                6.0,
                [
                    (c, "up", r * rows, (4 * c + r, 0))
                    for c in (0, 1)
                    for r in range(4)
                ],
                (rows, fw),
                (width, fw),
            )
        ],
    )

    def sources(*names):
        return [f"{n}.{k}" for n in names for k in ("mine", "other")]

    def cores_result(name, cost, names, blocks, block, shape):
        tables = [
            [(2 * names.index(n) + (c != bit), r, at) for c, n, r, at in blocks]
            for bit in (0, 1)
        ]
        task(
            name,
            85,
            cost,
            sources(*names),
            [name],
            lambda *a: [widen(core, a, block, shape, tables, name)],
        )

    cores_result(
        "grad_out",
        3.0,
        ("att0",),
        [(c, "att0", 0, (0, c)) for c in (0, 1)],
        (hw, half),
        (hw, width),
    )
    place = {2: ("att0", 1), 1: ("att1", 0), 0: ("att1", 1)}
    if not same:
        place = {c: ("att1", 2 - c) for c in range(3)}
    cores_result(
        "grad_qkv",
        5.0,
        ("att0", "att1") if same else ("att1",),
        [(c, *place[i], (i, c, 0)) for i in range(3) for c in (0, 1)],
        (half, hw),
        (3, width, hw),
    )

    plan.run()
    value = {k: b.value for k, b in plan.box.items()}
    small = value[last]
    vec = [small[i * width : (i + 1) * width] for i in range(6)]
    rest = small[6 * width :]
    return (
        value["result"],
        value["g_input"],
        value["grad_qkv"],
        rest[: 2 * hw].reshape(2, hw),
        value["grad_out"],
        vec[0],
        vec[1],
        vec[2],
        value["grad_up"],
        rest[2 * hw :],
        value["grad_down"],
        vec[3],
        vec[4],
        vec[5],
    )


def solution(mesh):
    n_dp, n_tensor = mesh.shape["dp"], mesh.shape["tensor"]
    pairs = n_tensor == 2 and n_dp >= 8 and n_dp & (n_dp - 1) == 0
    return jax.shard_map(
        functools.partial(body if pairs else plain, n_dp, n_tensor),
        mesh=mesh,
        in_specs=(
            P(("dp", "tensor"), None),
            P(None, None, "tensor"),
            P(None, "tensor"),
            P("tensor", None),
            P(),
            P(),
            P(),
            P(None, "tensor"),
            P("tensor"),
            P("tensor", None),
            P(),
            P(),
            P(),
            P("dp"),
            P(("dp", "tensor"), None),
        ),
        out_specs=(
            P(("dp", "tensor"), None),
            P(("dp", "tensor"), None),
            P(None, None, "tensor"),
            P(None, "tensor"),
            P("tensor", None),
            P(),
            P(),
            P(),
            P(None, "tensor"),
            P("tensor"),
            P("tensor", None),
            P(),
            P(),
            P(),
        ),
        check_vma=False,
    )
```

time: 690 us -> 470 us (0.68)
  waiting for transfers between devices: 372 us -> 206 us
  matrix products: 115 us -> 0 us
  Pallas kernels: 32 us -> 147 us
  other arithmetic: 50.9 us -> 3.82 us
  starting transfers between devices: 86.4 us -> 49.6 us
  local copies, waits for them, and re-layouts: 20.8 us -> 38.9 us
  between operations: 3.42 us -> 15.8 us
    ppermute x102 -> x62, waiting for transfers between devices: 372 us -> 206 us  [over(): return Box(lax.ppermute(a.value, axis, [(i, i ^ mask) for i in range(n)]))]
    dot_general x56 -> x0, matrix products: 115 us -> none  [contract(): lax.dot_general(a, b, (((ca,), (cb,)), ((), ())), preferred_element_type=...]
    pallas_call x0 -> x34, Pallas kernels: none -> 115 us  [the longest x5 22.5 us: grad_stack(): pl.pallas_call(kernel, grid_spec=pltpu.PrefetchScalarGridSpec(num_scalar_...]
    ppermute x102 -> x62, starting transfers between devices: 86.4 us -> 49.5 us  [over(): return Box(lax.ppermute(a.value, axis, [(i, i ^ mask) for i in range(n)]))]
    unnamed x139 -> x173, local copies, waits for them, and re-layouts: 7.36 us -> 34.8 us
    concatenate x37 -> x7, other arithmetic: 21.2 us -> 0.26 us  [the longest x6 0.25 us: work(): return [jnp.concatenate([low, high], axis=0)]]
    select_n x40 -> x8, other arithmetic: 13 us -> 0.28 us  [the longest x6 0.27 us: work(): low, high = (jnp.where(bit == 0, a, b), jnp.where(bit == 0, b, a))]
    dynamic_slice x33 -> x1, local copies, waits for them, and re-layouts: 10.1 us -> 0.58 us  [body(): lax.dynamic_slice_in_dim(n, lax.axis_index('tensor'), 1, 0)]
  transfers between devices with their start and end apart: 102 -> 64, of which waited for: 56 -> 36; matrix products, arithmetic and copies ran while one was open for 24% -> 1% of each run, Pallas kernels for 5% -> 29%
where the time goes in v2:
time: 470 us; the launch traced here: 462 us
  waiting for transfers between devices  206 us (44%)
  Pallas kernels  147 us (31%)
  starting transfers between devices  49.6 us (11%)
  local copies, waits for them, and re-layouts  38.9 us (8%)
  between operations  15.8 us (3%)
    ppermute x62, waiting for transfers between devices, over(): return Box(lax.ppermute(a.value, axis, [(i, i ^ mask) for i in range(n)]))  206 us
    ppermute x62, starting transfers between devices, over(): return Box(lax.ppermute(a.value, axis, [(i, i ^ mask) for i in range(n)]))  49.5 us
    unnamed x173, local copies, waits for them, and re-layouts  34.8 us
    pallas_call x5, Pallas kernels, grad_stack(): pl.pallas_call(kernel, grid_spec=pltpu.PrefetchScalarGridSpec(num_scalar_...  22.5 us
    pallas_call x2, Pallas kernels, attend_back(): pl.pallas_call(attend_back_kernel, grid=(width // wide,), in_specs=[pl.Bl...  20.2 us
    pallas_call x2, Pallas kernels, widened(): pl.pallas_call(kernel, grid_spec=pltpu.PrefetchScalarGridSpec(num_scalar_...  15.5 us
    pallas_call x2, Pallas kernels, attend(): pl.pallas_call(attend_kernel, grid=(steps,), in_specs=[pl.BlockSpec(memor...  12.6 us
    pallas_call x12, Pallas kernels, add_split(): pl.pallas_call(kernel, grid_spec=pltpu.PrefetchScalarGridSpec(num_scalar_...  11 us
  transfers between devices with their start and end apart: 64, of which 36 were waited for; matrix products, arithmetic and copies ran while one was open for 1% of the time, Pallas kernels for 29%

profile of v2, /device:TPU:0, one launch (start us, length us, event | category | flops | bytes accessed | tf_op | source)
XLA Modules:
  0.0 461.5 jit_solution(17575743547839453229)
XLA Ops:
  9.4 3.0 collective-permute-start
  12.4 2.8 pick.3
  18.0 2.7 project.2.q_ref.k_ref.v_ref
  20.7 3.2 pick.4
  23.9 6.3 %attend.2 = (bf16[512,512]{1,0:T(8,128)(2,1)S(1)}, f32[4,2,512]{2,1,0:T(2,128)S(1)}) custom-call(s32[1]{0:T(128)} %dynamic_slice.3.len_ref, bf16[3,512,512]{2,1,0:T(8,128)(2,1)S(1)} %project.2.q_ref.k_ref.v_ref, bf16[3,512,512]{2,1,0:T(8,128)(2,1)S(1)} %project.2.q_ref.k_ref.v_ref, bf16[3,512,512]{2,1,0:T(8,128)(2,1)S(1)} %project.2.q_ref.k_ref.v_ref), custom_call_target="tpu_custom_call" | custom-call | tf_op jit(solution)/shard_map/heads0/attend/pallas_call | solution.py:99
  30.2 3.0 pick.5
  35.4 14.2 %collective-permute-done.2.refs_3_ = bf16[256,1024]{1,0:T(8,128)(2,1)S(1)} collective-permute-done((bf16[256,1024]{1,0:T(8,128)(2,1)}, bf16[256,1024]{1,0:T(8,128)(2,1)S(1)}, u32[]{:S(2)}, u32[]{:S(2)}) %collective-permute-start.2) | collective-permute-done | bytes 524320 | tf_op jit(solution)/shard_map/o.y1/ppermute | solution.py:748
  53.2 7.2 %collective-permute-done.4.refs_2_ = bf16[3,128,512]{2,1,0:T(8,128)(2,1)S(1)} collective-permute-done((bf16[3,128,512]{2,1,0:T(8,128)(2,1)S(1)}, bf16[3,128,512]{2,1,0:T(8,128)(2,1)S(1)}, u32[]{:S(2)}, u32[]{:S(2)}) %collective-permute-start.4) | collective-permute-done | bytes 393248 | tf_op jit(solution)/shard_map/q.c0.1/ppermute | solution.py:748
  64.8 2.9 project.3
  69.4 6.4 %attend.3 = (bf16[512,512]{1,0:T(8,128)(2,1)S(1)}, f32[4,2,512]{2,1,0:T(2,128)S(1)}) custom-call(s32[1]{0:T(128)} %dynamic_slice.3.len_ref, bf16[3,512,512]{2,1,0:T(8,128)(2,1)S(1)} %get-tuple-element.11341.q_ref.k_ref.v_ref, bf16[3,512,512]{2,1,0:T(8,128)(2,1)S(1)} %get-tuple-element.11341.q_ref.k_ref.v_ref, ...), custom_call_target="tpu_custom_call" | custom-call | tf_op jit(solution)/shard_map/heads1/attend/pallas_call | solution.py:99
  75.9 3.8 attended.1
  80.6 7.4 %widened.2 = (bf16[512,2048]{1,0:T(8,128)(2,1)S(1)}, bf16[512,2048]{1,0:T(8,128)(2,1)S(1)}) custom-call(s32[15]{0:T(128)S(1)} %copy-done.63, bf16[512,1024]{1,0:T(8,128)(2,1)S(1)} %get-tuple-element.11345.x_ref.refs_0_, f32[7,1,512]{2,1,0:T(1,128)S(1)} %reshape.69.b_ref, bf16[1024,2048]{1,0:T(8,128)(2,1)S(1)} %copy-done.2), custom_call_target="tpu_custom_call" | custom-call | tf_op jit(solution)/shard_map/widened0/widened/pallas_call | solution.py:328
  93.8 10.3 %collective-permute-done.12.refs_2_ = bf16[128,2048]{1,0:T(8,128)(2,1)S(1)} collective-permute-done((bf16[128,2048]{1,0:T(8,128)(2,1)S(1)}, bf16[128,2048]{1,0:T(8,128)(2,1)S(1)}, u32[]{:S(2)}, u32[]{:S(2)}) %collective-permute-start.12) | collective-permute-done | bytes 524320 | tf_op jit(solution)/shard_map/u.c0.1/ppermute | solution.py:748
  106.9 8.1 %widened.3 = (bf16[512,2048]{1,0:T(8,128)(2,1)S(1)}, bf16[512,2048]{1,0:T(8,128)(2,1)S(1)}, bf16[1024,2048]{1,0:T(8,128)(2,1)S(1)}) custom-call(s32[15]{0:T(128)S(1)} %copy-done.63, bf16[512,1024]{1,0:T(8,128)(2,1)S(1)} %get-tuple-element.11345.x_ref.refs_0_, f32[7,1,512]{2,1,0:T(1,128)S(1)} %collective-permute-done.b_ref, ...), custom_call_target="tpu_custom_call" | custom-call | tf_op jit(solution)/shard_map/widened1/widened/pallas_call | solution.py:328
  127.0 6.3 %collective-permute-done.20.refs_5_.refs_2_ = bf16[256,1024]{1,0:T(8,128)(2,1)S(1)} collective-permute-done((bf16[256,1024]{1,0:T(8,128)(2,1)S(1)}, bf16[256,1024]{1,0:T(8,128)(2,1)S(1)}, u32[]{:S(2)}, u32[]{:S(2)}) %collective-permute-start.20) | collective-permute-done | bytes 524320 | tf_op jit(solution)/shard_map/d.c0.1/ppermute | solution.py:748
  139.0 10.3 %narrowed.1 = (bf16[512,1024]{1,0:T(8,128)(2,1)S(1)}, f32[512,1024]{1,0:T(8,128)S(1)}, bf16[512,1024]{1,0:T(8,128)(2,1)}, f32[3,1024]{1,0:T(4,128)S(1)}) custom-call(s32[15]{0:T(128)S(1)} %copy-done.63, f32[512,1024]{1,0:T(8,128)S(1)} %get-tuple-element.11346.nm_ref, f32[1,1024]{1,0:T(1,128)S(1)} %bitcast.35, f32[1,1024]{1,0:T(1,128)S(1)} %bitcast.38, ...), custom_call_target="tpu_custom_call" | custom-call | tf_op jit(solution)/shard_map/narrowed/narrowed/pallas_call | solution.py:403
  153.7 4.3 gelu_back.2
  162.4 7.7 %grad_stack.5 = (bf16[2048,512]{1,0:T(8,128)(2,1)S(1)}, bf16[2048,512]{1,0:T(8,128)(2,1)S(1)}) custom-call(s32[15]{0:T(128)S(1)} %copy-done.63, bf16[512,2048]{1,0:T(8,128)(2,1)S(1)} %copy-done.23, bf16[512,1024]{1,0:T(8,128)(2,1)S(1)} %get-tuple-element.11369.g_ref.refs_1_.refs_5_, bf16[512,2048]{1,0:T(8,128)(2,1)S(1)} %copy-done.41, ...), custom_call_target="tpu_custom_call" | custom-call | tf_op jit(solution)/shard_map/down.p1/grad_stack/pallas_call | solution.py:689
  174.3 4.0 gelu_back.3
  178.4 6.6 %attended_back.1 = (bf16[512,1024]{1,0:T(8,128)(2,1)S(1)}, f32[512,1024]{1,0:T(8,128)S(1)}, f32[3,1024]{1,0:T(4,128)S(1)}) custom-call(f32[512,1024]{1,0:T(8,128)S(1)} %copy-done.43, f32[512,1024]{1,0:T(8,128)S(1)} %get-tuple-element.11346.nm_ref, f32[512,1]{1,0:T(8,128)S(1)} %get-tuple-element.11347.sc_ref, f32[1,1024]{1,0:T(1,128)S(1)} %bitcast.36, ...), custom_call_target="tpu_custom_call" | custom-call | tf_op jit(solution)/shard_map/attended_back/attended_back/pallas_call | solution.py:505
  185.1 10.0 %attend_back.2 = (bf16[3,512,512]{2,1,0:T(8,128)(2,1)S(1)}, f32[3,512]{1,0:T(4,128)S(1)}) custom-call(s32[1]{0:T(128)} %dynamic_slice.3.len_ref, bf16[3,512,512]{2,1,0:T(8,128)(2,1)S(1)} %get-tuple-element.11341.q_ref.k_ref.v_ref, bf16[3,512,512]{2,1,0:T(8,128)(2,1)S(1)} %get-tuple-element.11341.q_ref.k_ref.v_ref, ...), custom_call_target="tpu_custom_call" | custom-call | tf_op jit(solution)/shard_map/heads_back1/attend_back/pallas_call | solution.py:158
  196.3 10.2 %attend_back.3 = (bf16[3,512,512]{2,1,0:T(8,128)(2,1)S(1)}, f32[3,512]{1,0:T(4,128)S(1)}) custom-call(s32[1]{0:T(128)} %dynamic_slice.3.len_ref, bf16[3,512,512]{2,1,0:T(8,128)(2,1)S(1)} %project.2.q_ref.k_ref.v_ref, bf16[3,512,512]{2,1,0:T(8,128)(2,1)S(1)} %project.2.q_ref.k_ref.v_ref, bf16[3,512,512]{2,1,0:T(8,128)(2,1)S(1)} %project.2.q_ref.k_ref.v_ref, ...), custom_call_target="tpu_custom_call" | custom-call | tf_op jit(solution)/shard_map/heads_back0/attend_back/pallas_call | solution.py:158
  207.6 3.3 grad_stack.6
  212.4 8.7 %collective-permute-done.29.b0.b1 = bf16[2048,512]{1,0:T(8,128)(2,1)} collective-permute-done((bf16[2048,512]{1,0:T(8,128)(2,1)}, bf16[2048,512]{1,0:T(8,128)(2,1)}, u32[]{:S(2)}, u32[]{:S(2)}) %collective-permute-start.29) | collective-permute-done | bytes 2097184 | tf_op jit(solution)/shard_map/down.y1.1/ppermute | solution.py:748
  225.2 2.3 add_split.12
  228.8 3.3 grad_stack.7.a0.a1
  232.2 4.1 grad_stack.8
  237.3 4.1 grad_stack.9
  241.5 5.5 %input_grad.1 = f32[512,1024]{1,0:T(8,128)} custom-call(f32[512,1024]{1,0:T(8,128)S(1)} %copy-done.51, bf16[3,512,512]{2,1,0:T(8,128)(2,1)S(1)} %copy-done.10, bf16[3,512,512]{2,1,0:T(8,128)(2,1)S(1)} %copy-done.8, bf16[3,1024,512]{2,1,0:T(8,128)(2,1)S(1)} %copy-done.4, bf16[3,1024,512]{2,1,0:T(8,128)(2,1)S(1)} %copy-done.37), custom_call_target="tpu_custom_call" | custom-call | tf_op jit(solution)/shard_map/input_grad/input_grad/pallas_call | solution.py:534
  247.0 6.7 %collective-permute-done.34.b0.b1 = bf16[1024,512]{1,0:T(8,128)(2,1)S(1)} collective-permute-done((bf16[1024,512]{1,0:T(8,128)(2,1)S(1)}, bf16[1024,512]{1,0:T(8,128)(2,1)S(1)}, u32[]{:S(2)}, u32[]{:S(2)}) %collective-permute-start.34) | collective-permute-done | bytes 1048608 | tf_op jit(solution)/shard_map/down.d0/ppermute | solution.py:748
  256.1 13.7 %collective-permute-done.35.b0.b1 = bf16[512,2048]{1,0:T(8,128)(2,1)S(1)} collective-permute-done((bf16[512,2048]{1,0:T(8,128)(2,1)}, bf16[512,2048]{1,0:T(8,128)(2,1)S(1)}, u32[]{:S(2)}, u32[]{:S(2)}) %collective-permute-start.35) | collective-permute-done | bytes 2097184 | tf_op jit(solution)/shard_map/up.y1.1/ppermute | solution.py:748
  271.9 2.6 collective-permute-start.37
  274.5 11.3 %collective-permute-done.37 = bf16[256,512]{1,0:T(8,128)(2,1)S(1)} collective-permute-done((bf16[256,512]{1,0:T(8,128)(2,1)S(1)}, bf16[256,512]{1,0:T(8,128)(2,1)S(1)}, u32[]{:S(2)}, u32[]{:S(2)}) %collective-permute-start.37) | collective-permute-done | bytes 262176 | tf_op jit(solution)/shard_map/down.d2/ppermute | solution.py:748
  288.7 22.2 %collective-permute-done.38.b0.b1 = bf16[1024,512]{1,0:T(8,128)(2,1)S(1)} collective-permute-done((bf16[1024,512]{1,0:T(8,128)(2,1)}, bf16[1024,512]{1,0:T(8,128)(2,1)S(1)}, u32[]{:S(2)}, u32[]{:S(2)}) %collective-permute-start.38) | collective-permute-done | bytes 1048608 | tf_op jit(solution)/shard_map/att0.y1.1/ppermute | solution.py:748
  310.9 4.0 collective-permute-done.39.b0.b1
  319.7 20.2 %collective-permute-done.40.b0.b1 = bf16[128,2048]{1,0:T(8,128)(2,1)S(1)} collective-permute-done((bf16[128,2048]{1,0:T(8,128)(2,1)S(1)}, bf16[128,2048]{1,0:T(8,128)(2,1)S(1)}, u32[]{:S(2)}, u32[]{:S(2)}) %collective-permute-start.40) | collective-permute-done | bytes 524320 | tf_op jit(solution)/shard_map/up.d1/ppermute | solution.py:748
  343.0 3.5 collective-permute-start.46
  348.7 8.6 %collective-permute-done.43.b0.b1 = bf16[256,512]{1,0:T(8,128)(2,1)S(1)} collective-permute-done((bf16[256,512]{1,0:T(8,128)(2,1)S(1)}, bf16[256,512]{1,0:T(8,128)(2,1)S(1)}, u32[]{:S(2)}, u32[]{:S(2)}) %collective-permute-start.43) | collective-permute-done | bytes 262176 | tf_op jit(solution)/shard_map/att0.d1/ppermute | solution.py:748
  363.4 5.1 %grad_down.1 = f32[2048,1024]{1,0:T(8,128)} custom-call(s32[4,8]{1,0:T(4,128)S(1)} %copy-done.71, bf16[16,256,512]{2,1,0:T(8,128)(2,1)S(1)} %bitcast.32, bf16[16,256,512]{2,1,0:T(8,128)(2,1)S(1)} %bitcast.33), custom_call_target="tpu_custom_call" | custom-call | tf_op jit(solution)/shard_map/grad_down/grad_down/pallas_call | solution.py:812
  375.1 7.7 %collective-permute-done.50.b0.b1 = bf16[256,512]{1,0:T(8,128)(2,1)S(1)} collective-permute-done((bf16[256,512]{1,0:T(8,128)(2,1)S(1)}, bf16[256,512]{1,0:T(8,128)(2,1)S(1)}, u32[]{:S(2)}, u32[]{:S(2)}) %collective-permute-start.50) | collective-permute-done | bytes 262176 | tf_op jit(solution)/shard_map/att1.d1/ppermute | solution.py:748
  387.2 10.5 %collective-permute-done.53 = bf16[128,512]{1,0:T(8,128)(2,1)S(1)} collective-permute-done((bf16[128,512]{1,0:T(8,128)(2,1)S(1)}, bf16[128,512]{1,0:T(8,128)(2,1)S(1)}, u32[]{:S(2)}, u32[]{:S(2)}) %collective-permute-start.53) | collective-permute-done | bytes 131104 | tf_op jit(solution)/shard_map/att1.d2/ppermute | solution.py:748
  397.8 2.4 collective-permute-start.55
  400.8 17.7 %collective-permute-done.54 = bf16[256,512]{1,0:T(8,128)(2,1)S(1)} collective-permute-done((bf16[256,512]{1,0:T(8,128)(2,1)S(1)}, bf16[256,512]{1,0:T(8,128)(2,1)S(1)}, u32[]{:S(2)}, u32[]{:S(2)}) %collective-permute-start.54) | collective-permute-done | bytes 262176 | tf_op jit(solution)/shard_map/att0.u1/ppermute | solution.py:748
  418.8 11.8 %collective-permute-done.57 = bf16[256,512]{1,0:T(8,128)(2,1)S(1)} collective-permute-done((bf16[256,512]{1,0:T(8,128)(2,1)S(1)}, bf16[256,512]{1,0:T(8,128)(2,1)S(1)}, u32[]{:S(2)}, u32[]{:S(2)}) %collective-permute-start.57) | collective-permute-done | bytes 262176 | tf_op jit(solution)/shard_map/att1.u1/ppermute | solution.py:748
  433.9 5.1 %grad_up.1 = f32[1024,2048]{1,0:T(8,128)} custom-call(s32[4,8]{1,0:T(4,128)S(1)} %copy-done.70, bf16[16,64,2048]{2,1,0:T(8,128)(2,1)S(1)} %bitcast.30, bf16[16,64,2048]{2,1,0:T(8,128)(2,1)S(1)} %bitcast.31), custom_call_target="tpu_custom_call" | custom-call | tf_op jit(solution)/shard_map/grad_up/grad_up/pallas_call | solution.py:812
  441.1 4.3 collective-permute-done.60
  445.7 2.6 collective-permute-done.61.refs_3_
  448.3 4.2 grad_qkv.1
  (334 shorter events, 109.4 us)
Async XLA Ops:
  7.2 354.1 %all-gather.5.cloned.1.call-start = ((), (), s32[]{:S(2)}) async-start(), calls=%async_computation | async-start | bytes 4456448 | tf_op jit(solution)/shard_map/down_all.all/all_gather | solution.py:867
  15.8 19.2 %collective-permute-start.1 = (bf16[3,256,512]{2,1,0:T(8,128)(2,1)}, bf16[3,256,512]{2,1,0:T(8,128)(2,1)S(1)}, u32[]{:S(2)}, u32[]{:S(2)}) collective-permute-start(bf16[3,256,512]{2,1,0:T(8,128)(2,1)} %pick.3), channel_id=1, source_target_pairs={{0,1},{1,0},{2,3},{3,2},{4,5},{5,4},{6,7},{7,6},{8,9},{9,8},{10,11... | collective-permute-start | bytes 2359304 | tf_op jit(solution)/shard_map/q.y1/ppermute | solution.py:748
  35.1 14.6 %collective-permute-start.3 = (bf16[3,256,512]{2,1,0:T(8,128)(2,1)S(1)}, bf16[3,256,512]{2,1,0:T(8,128)(2,1)S(1)}, u32[]{:S(2)}, u32[]{:S(2)}) collective-permute-start(bf16[3,256,512]{2,1,0:T(8,128)(2,1)S(1)} %collective-permute-done.1.refs_0_), channel_id=1, source_target_pairs={{0,2},{2,0},{4,6},{6,4},{8,10},{10,8},{12,14},{14,12},{16,18},{18,... | collective-permute-start | bytes 2359304 | tf_op jit(solution)/shard_map/q.sib1/ppermute | solution.py:748
  35.1 14.5 %collective-permute-start.2 = (bf16[256,1024]{1,0:T(8,128)(2,1)}, bf16[256,1024]{1,0:T(8,128)(2,1)S(1)}, u32[]{:S(2)}, u32[]{:S(2)}) collective-permute-start(bf16[256,1024]{1,0:T(8,128)(2,1)} %get-tuple-element.11329), channel_id=1, source_target_pairs={{0,1},{1,0},{2,3},{3,2},{4,5},{5,4},{6,7},{7,6},{8,9},{9,8},{10,11... | collective-permute-start | bytes 1572872 | tf_op jit(solution)/shard_map/o.y1/ppermute | solution.py:748
  49.6 39.9 %collective-permute-start.9 = (bf16[256,2048]{1,0:T(8,128)(2,1)}, bf16[256,2048]{1,0:T(8,128)(2,1)S(1)}, u32[]{:S(2)}, u32[]{:S(2)}) collective-permute-start(bf16[256,2048]{1,0:T(8,128)(2,1)} %get-tuple-element.11330), channel_id=1, source_target_pairs={{0,1},{1,0},{2,3},{3,2},{4,5},{5,4},{6,7},{7,6},{8,9},{9,8},{10,11... | collective-permute-start | bytes 3145736 | tf_op jit(solution)/shard_map/u.y1/ppermute | solution.py:748
  49.9 10.5 %collective-permute-start.4 = (bf16[3,128,512]{2,1,0:T(8,128)(2,1)S(1)}, bf16[3,128,512]{2,1,0:T(8,128)(2,1)S(1)}, u32[]{:S(2)}, u32[]{:S(2)}) collective-permute-start(bf16[3,128,512]{2,1,0:T(8,128)(2,1)S(1)} %get-tuple-element.11335), channel_id=1, source_target_pairs={{0,4},{2,6},{4,0},{6,2},{8,12},{10,14},{12,8},{14,10},{16,20},{18,... | collective-permute-start | bytes 1179656 | tf_op jit(solution)/shard_map/q.c0.1/ppermute | solution.py:748
  51.6 10.2 %collective-permute-start.5 = (bf16[3,128,512]{2,1,0:T(8,128)(2,1)S(1)}, bf16[3,128,512]{2,1,0:T(8,128)(2,1)S(1)}, u32[]{:S(2)}, u32[]{:S(2)}) collective-permute-start(bf16[3,128,512]{2,1,0:T(8,128)(2,1)S(1)} %get-tuple-element.11336), channel_id=1, source_target_pairs={{0,8},{2,10},{4,12},{6,14},{8,0},{10,2},{12,4},{14,6},{16,24},{18,... | collective-permute-start | bytes 1179656 | tf_op jit(solution)/shard_map/q.c1.1/ppermute | solution.py:748
  61.8 14.0 %collective-permute-start.8 = (bf16[256,1024]{1,0:T(8,128)(2,1)S(1)}, bf16[256,1024]{1,0:T(8,128)(2,1)S(1)}, u32[]{:S(2)}, u32[]{:S(2)}) collective-permute-start(bf16[256,1024]{1,0:T(8,128)(2,1)S(1)} %collective-permute-done.2.refs_3_), channel_id=1, source_target_pairs={{0,2},{2,0},{4,6},{6,4},{8,10},{10,8},{12,14},{14,12},{16,18},{18,... | collective-permute-start | bytes 1572872 | tf_op jit(solution)/shard_map/o.sib1/ppermute | solution.py:748
  90.1 14.0 %collective-permute-start.12 = (bf16[128,2048]{1,0:T(8,128)(2,1)S(1)}, bf16[128,2048]{1,0:T(8,128)(2,1)S(1)}, u32[]{:S(2)}, u32[]{:S(2)}) collective-permute-start(bf16[128,2048]{1,0:T(8,128)(2,1)S(1)} %get-tuple-element.11352), channel_id=1, source_target_pairs={{0,4},{2,6},{4,0},{6,2},{8,12},{10,14},{12,8},{14,10},{16,20},{18,... | collective-permute-start | bytes 1572872 | tf_op jit(solution)/shard_map/u.c0.1/ppermute | solution.py:748
  90.5 13.7 %collective-permute-start.13 = (bf16[128,2048]{1,0:T(8,128)(2,1)S(1)}, bf16[128,2048]{1,0:T(8,128)(2,1)S(1)}, u32[]{:S(2)}, u32[]{:S(2)}) collective-permute-start(bf16[128,2048]{1,0:T(8,128)(2,1)S(1)} %get-tuple-element.11353), channel_id=1, source_target_pairs={{0,8},{2,10},{4,12},{6,14},{8,0},{10,2},{12,4},{14,6},{16,24},{18,... | collective-permute-start | bytes 1572872 | tf_op jit(solution)/shard_map/u.c1.1/ppermute | solution.py:748
  92.2 26.0 %collective-permute-start.16 = (bf16[512,1024]{1,0:T(8,128)(2,1)S(1)}, bf16[512,1024]{1,0:T(8,128)(2,1)S(1)}, u32[]{:S(2)}, u32[]{:S(2)}) collective-permute-start(bf16[512,1024]{1,0:T(8,128)(2,1)S(1)} %copy-done.77), channel_id=1, source_target_pairs={{0,1},{1,0},{2,3},{3,2},{4,5},{5,4},{6,7},{7,6},{8,9},{9,8},{10,11... | collective-permute-start | bytes 3145736 | tf_op jit(solution)/shard_map/d.y1/ppermute | solution.py:748
  118.9 8.1 %collective-permute-start.19 = (bf16[512,1024]{1,0:T(8,128)(2,1)S(1)}, bf16[512,1024]{1,0:T(8,128)(2,1)S(1)}, u32[]{:S(2)}, u32[]{:S(2)}) collective-permute-start(bf16[512,1024]{1,0:T(8,128)(2,1)S(1)} %collective-permute-done.16.refs_3_.refs_0_), channel_id=1, source_target_pairs={{0,2},{2,0},{4,6},{6,4},{8,10},{10,8},{12,14},{14,12},{16,18},{18,... | collective-permute-start | bytes 3145736 | tf_op jit(solution)/shard_map/d.sib1/ppermute | solution.py:748
  119.1 14.3 %collective-permute-start.20 = (bf16[256,1024]{1,0:T(8,128)(2,1)S(1)}, bf16[256,1024]{1,0:T(8,128)(2,1)S(1)}, u32[]{:S(2)}, u32[]{:S(2)}) collective-permute-start(bf16[256,1024]{1,0:T(8,128)(2,1)S(1)} %get-tuple-element.11362), channel_id=1, source_target_pairs={{0,4},{2,6},{4,0},{6,2},{8,12},{10,14},{12,8},{14,10},{16,20},{18,... | collective-permute-start | bytes 1572872 | tf_op jit(solution)/shard_map/d.c0.1/ppermute | solution.py:748
  120.8 13.9 %collective-permute-start.21 = (bf16[256,1024]{1,0:T(8,128)(2,1)S(1)}, bf16[256,1024]{1,0:T(8,128)(2,1)S(1)}, u32[]{:S(2)}, u32[]{:S(2)}) collective-permute-start(bf16[256,1024]{1,0:T(8,128)(2,1)S(1)} %get-tuple-element.11363), channel_id=1, source_target_pairs={{0,8},{2,10},{4,12},{6,14},{8,0},{10,2},{12,4},{14,6},{16,24},{18,... | collective-permute-start | bytes 1572872 | tf_op jit(solution)/shard_map/d.c1.1/ppermute | solution.py:748
  151.1 7.9 %collective-permute-start.26 = (bf16[512,512]{1,0:T(8,128)(2,1)S(1)}, bf16[512,512]{1,0:T(8,128)(2,1)S(1)}, u32[]{:S(2)}, u32[]{:S(2)}) collective-permute-start(bf16[512,512]{1,0:T(8,128)(2,1)S(1)} %copy-done.45), channel_id=1, source_target_pairs={{0,2},{2,0},{4,6},{6,4},{8,10},{10,8},{12,14},{14,12},{16,18},{18,... | collective-permute-start | bytes 1572872 | tf_op jit(solution)/shard_map/heads0.sib/ppermute | solution.py:748
  151.3 8.6 %collective-permute-start.27 = (bf16[512,512]{1,0:T(8,128)(2,1)S(1)}, bf16[512,512]{1,0:T(8,128)(2,1)S(1)}, u32[]{:S(2)}, u32[]{:S(2)}) collective-permute-start(bf16[512,512]{1,0:T(8,128)(2,1)S(1)} %get-tuple-element.11343.refs_1_.refs_0_), channel_id=1, source_target_pairs={{0,2},{2,0},{4,6},{6,4},{8,10},{10,8},{12,14},{14,12},{16,18},{18,... | collective-permute-start | bytes 1572872 | tf_op jit(solution)/shard_map/heads1.sib/ppermute | solution.py:748
  160.7 12.1 %collective-permute-start.28 = (bf16[512,2048]{1,0:T(8,128)(2,1)S(1)}, bf16[512,2048]{1,0:T(8,128)(2,1)S(1)}, u32[]{:S(2)}, u32[]{:S(2)}) collective-permute-start(bf16[512,2048]{1,0:T(8,128)(2,1)S(1)} %get-tuple-element.11373.refs_1_), channel_id=1, source_target_pairs={{0,2},{2,0},{4,6},{6,4},{8,10},{10,8},{12,14},{14,12},{16,18},{18,... | collective-permute-start | bytes 6291464 | tf_op jit(solution)/shard_map/g_up1.sib/ppermute | solution.py:748
  172.8 48.3 %collective-permute-start.29 = (bf16[2048,512]{1,0:T(8,128)(2,1)}, bf16[2048,512]{1,0:T(8,128)(2,1)}, u32[]{:S(2)}, u32[]{:S(2)}) collective-permute-start(bf16[2048,512]{1,0:T(8,128)(2,1)} %copy-done.72), channel_id=1, source_target_pairs={{0,1},{1,0},{2,3},{3,2},{4,5},{5,4},{6,7},{7,6},{8,9},{9,8},{10,11... | collective-permute-start | bytes 6291464 | tf_op jit(solution)/shard_map/down.y1.1/ppermute | solution.py:748
  221.1 7.7 %collective-permute-start.31 = (bf16[512,2048]{1,0:T(8,128)(2,1)}, bf16[512,2048]{1,0:T(8,128)(2,1)S(1)}, u32[]{:S(2)}, u32[]{:S(2)}) collective-permute-start(bf16[512,2048]{1,0:T(8,128)(2,1)} %copy-done.24), channel_id=1, source_target_pairs={{0,2},{2,0},{4,6},{6,4},{8,10},{10,8},{12,14},{14,12},{16,18},{18,... | collective-permute-start | bytes 6291464 | tf_op jit(solution)/shard_map/g_up0.sib/ppermute | solution.py:748
  221.6 10.6 %collective-permute-start.32 = (bf16[3,512,512]{2,1,0:T(8,128)(2,1)S(1)}, bf16[3,512,512]{2,1,0:T(8,128)(2,1)S(1)}, u32[]{:S(2)}, u32[]{:S(2)}) collective-permute-start(bf16[3,512,512]{2,1,0:T(8,128)(2,1)S(1)} %copy-done.8), channel_id=1, source_target_pairs={{0,2},{2,0},{4,6},{6,4},{8,10},{10,8},{12,14},{14,12},{16,18},{18,... | collective-permute-start | bytes 4718600 | tf_op jit(solution)/shard_map/g_qkv1.sib/ppermute | solution.py:748
  221.6 10.6 %collective-permute-start.33 = (bf16[3,512,512]{2,1,0:T(8,128)(2,1)}, bf16[3,512,512]{2,1,0:T(8,128)(2,1)S(1)}, u32[]{:S(2)}, u32[]{:S(2)}) collective-permute-start(bf16[3,512,512]{2,1,0:T(8,128)(2,1)} %copy-done.9), channel_id=1, source_target_pairs={{0,2},{2,0},{4,6},{6,4},{8,10},{10,8},{12,14},{14,12},{16,18},{18,... | collective-permute-start | bytes 4718600 | tf_op jit(solution)/shard_map/g_qkv0.sib/ppermute | solution.py:748
  222.1 47.7 %collective-permute-start.35 = (bf16[512,2048]{1,0:T(8,128)(2,1)}, bf16[512,2048]{1,0:T(8,128)(2,1)S(1)}, u32[]{:S(2)}, u32[]{:S(2)}) collective-permute-start(bf16[512,2048]{1,0:T(8,128)(2,1)} %copy-done.52), channel_id=1, source_target_pairs={{0,1},{1,0},{2,3},{3,2},{4,5},{5,4},{6,7},{7,6},{8,9},{9,8},{10,11... | collective-permute-start | bytes 6291464 | tf_op jit(solution)/shard_map/up.y1.1/ppermute | solution.py:748
  228.5 25.2 %collective-permute-start.34 = (bf16[1024,512]{1,0:T(8,128)(2,1)S(1)}, bf16[1024,512]{1,0:T(8,128)(2,1)S(1)}, u32[]{:S(2)}, u32[]{:S(2)}) collective-permute-start(bf16[1024,512]{1,0:T(8,128)(2,1)S(1)} %get-tuple-element.11396), channel_id=1, source_target_pairs={{0,4},{2,6},{4,0},{6,2},{8,12},{10,14},{12,8},{14,10},{16,20},{18,... | collective-permute-start | bytes 3145736 | tf_op jit(solution)/shard_map/down.d0/ppermute | solution.py:748
  254.5 16.5 %collective-permute-start.36 = (bf16[512,512]{1,0:T(8,128)(2,1)S(1)}, bf16[512,512]{1,0:T(8,128)(2,1)S(1)}, u32[]{:S(2)}, u32[]{:S(2)}) collective-permute-start(bf16[512,512]{1,0:T(8,128)(2,1)S(1)} %get-tuple-element.11405), channel_id=1, source_target_pairs={{0,8},{2,10},{4,12},{6,14},{8,0},{10,2},{12,4},{14,6},{16,24},{18,... | collective-permute-start | bytes 1572872 | tf_op jit(solution)/shard_map/down.d1/ppermute | solution.py:748
  271.9 13.9 %collective-permute-start.37 = (bf16[256,512]{1,0:T(8,128)(2,1)S(1)}, bf16[256,512]{1,0:T(8,128)(2,1)S(1)}, u32[]{:S(2)}, u32[]{:S(2)}) collective-permute-start(bf16[256,512]{1,0:T(8,128)(2,1)S(1)} %get-tuple-element.11411), channel_id=1, source_target_pairs={{0,16},{2,18},{4,20},{6,22},{8,24},{10,26},{12,28},{14,30},{16,0},... | collective-permute-start | bytes 786440 | tf_op jit(solution)/shard_map/down.d2/ppermute | solution.py:748
  286.6 145.1 %all-gather.7.cloned.1.call-start = ((), (), s32[]{:S(2)}) async-start(), calls=%async_computation.1 | async-start | bytes 4456448 | tf_op jit(solution)/shard_map/up_all.all/all_gather | solution.py:867
  286.6 24.3 %collective-permute-start.38 = (bf16[1024,512]{1,0:T(8,128)(2,1)}, bf16[1024,512]{1,0:T(8,128)(2,1)S(1)}, u32[]{:S(2)}, u32[]{:S(2)}) collective-permute-start(bf16[1024,512]{1,0:T(8,128)(2,1)} %copy-done.75), channel_id=1, source_target_pairs={{0,1},{1,0},{2,3},{3,2},{4,5},{5,4},{6,7},{7,6},{8,9},{9,8},{10,11... | collective-permute-start | bytes 3145736 | tf_op jit(solution)/shard_map/att0.y1.1/ppermute | solution.py:748
  288.2 26.7 %collective-permute-start.39 = (bf16[256,2048]{1,0:T(8,128)(2,1)}, bf16[256,2048]{1,0:T(8,128)(2,1)S(1)}, u32[]{:S(2)}, u32[]{:S(2)}) collective-permute-start(bf16[256,2048]{1,0:T(8,128)(2,1)} %copy-done.76), channel_id=1, source_target_pairs={{0,4},{2,6},{4,0},{6,2},{8,12},{10,14},{12,8},{14,10},{16,20},{18,... | collective-permute-start | bytes 3145736 | tf_op jit(solution)/shard_map/up.d0/ppermute | solution.py:748
  314.9 31.6 %collective-permute-start.42 = (bf16[1024,512]{1,0:T(8,128)(2,1)S(1)}, bf16[1024,512]{1,0:T(8,128)(2,1)S(1)}, u32[]{:S(2)}, u32[]{:S(2)}) collective-permute-start(bf16[1024,512]{1,0:T(8,128)(2,1)S(1)} %copy-done.74), channel_id=1, source_target_pairs={{0,1},{1,0},{2,3},{3,2},{4,5},{5,4},{6,7},{7,6},{8,9},{9,8},{10,11... | collective-permute-start | bytes 3145736 | tf_op jit(solution)/shard_map/att1.y1.1/ppermute | solution.py:748
  316.3 23.7 %collective-permute-start.40 = (bf16[128,2048]{1,0:T(8,128)(2,1)S(1)}, bf16[128,2048]{1,0:T(8,128)(2,1)S(1)}, u32[]{:S(2)}, u32[]{:S(2)}) collective-permute-start(bf16[128,2048]{1,0:T(8,128)(2,1)S(1)} %get-tuple-element.11417), channel_id=1, source_target_pairs={{0,8},{2,10},{4,12},{6,14},{8,0},{10,2},{12,4},{14,6},{16,24},{18,... | collective-permute-start | bytes 1572872 | tf_op jit(solution)/shard_map/up.d1/ppermute | solution.py:748
  319.2 21.5 %collective-permute-start.41 = (bf16[512,512]{1,0:T(8,128)(2,1)S(1)}, bf16[512,512]{1,0:T(8,128)(2,1)S(1)}, u32[]{:S(2)}, u32[]{:S(2)}) collective-permute-start(bf16[512,512]{1,0:T(8,128)(2,1)S(1)} %get-tuple-element.11419), channel_id=1, source_target_pairs={{0,4},{2,6},{4,0},{6,2},{8,12},{10,14},{12,8},{14,10},{16,20},{18,... | collective-permute-start | bytes 1572872 | tf_op jit(solution)/shard_map/att0.d0/ppermute | solution.py:748
  341.4 15.9 %collective-permute-start.43 = (bf16[256,512]{1,0:T(8,128)(2,1)S(1)}, bf16[256,512]{1,0:T(8,128)(2,1)S(1)}, u32[]{:S(2)}, u32[]{:S(2)}) collective-permute-start(bf16[256,512]{1,0:T(8,128)(2,1)S(1)} %get-tuple-element.11423), channel_id=1, source_target_pairs={{0,8},{2,10},{4,12},{6,14},{8,0},{10,2},{12,4},{14,6},{16,24},{18,... | collective-permute-start | bytes 786440 | tf_op jit(solution)/shard_map/att0.d1/ppermute | solution.py:748
  343.0 25.6 %collective-permute-start.46 = (bf16[64,2048]{1,0:T(8,128)(2,1)S(1)}, bf16[64,2048]{1,0:T(8,128)(2,1)}, u32[]{:S(2)}, u32[]{:S(2)}) collective-permute-start(bf16[64,2048]{1,0:T(8,128)(2,1)S(1)} %get-tuple-element.11906), channel_id=1, source_target_pairs={{0,16},{2,18},{4,20},{6,22},{8,24},{10,26},{12,28},{14,30},{16,0},... | collective-permute-start | bytes 786440 | tf_op jit(solution)/shard_map/up.d2/ppermute | solution.py:748
  346.5 10.8 %collective-permute-start.44 = (f32[9216]{0:T(1024)S(1)}, f32[9216]{0:T(1024)S(1)}, u32[]{:S(2)}, u32[]{:S(2)}) collective-permute-start(f32[9216]{0:T(1024)S(1)} %constant_dynamic-update-slice_fusion.1), channel_id=1, source_target_pairs={{0,1},{1,0},{2,3},{3,2},{4,5},{5,4},{6,7},{7,6},{8,9},{9,8},{10,11... | collective-permute-start | bytes 110600 | tf_op jit(solution)/shard_map/pack1.y/ppermute | solution.py:748
  357.3 13.9 %collective-permute-start.47 = (bf16[512,512]{1,0:T(8,128)(2,1)S(1)}, bf16[512,512]{1,0:T(8,128)(2,1)S(1)}, u32[]{:S(2)}, u32[]{:S(2)}) collective-permute-start(bf16[512,512]{1,0:T(8,128)(2,1)S(1)} %get-tuple-element.12028), channel_id=1, source_target_pairs={{0,4},{2,6},{4,0},{6,2},{8,12},{10,14},{12,8},{14,10},{16,20},{18,... | collective-permute-start | bytes 1572872 | tf_op jit(solution)/shard_map/att1.d0/ppermute | solution.py:748
  358.8 13.1 %collective-permute-start.48 = (bf16[128,512]{1,0:T(8,128)(2,1)S(1)}, bf16[128,512]{1,0:T(8,128)(2,1)S(1)}, u32[]{:S(2)}, u32[]{:S(2)}) collective-permute-start(bf16[128,512]{1,0:T(8,128)(2,1)S(1)} %get-tuple-element.12154), channel_id=1, source_target_pairs={{0,16},{2,18},{4,20},{6,22},{8,24},{10,26},{12,28},{14,30},{16,0},... | collective-permute-start | bytes 393224 | tf_op jit(solution)/shard_map/att0.d2/ppermute | solution.py:748
  360.0 11.9 %collective-permute-start.49 = (f32[9216]{0:T(1024)S(1)}, f32[9216]{0:T(1024)S(1)}, u32[]{:S(2)}, u32[]{:S(2)}) collective-permute-start(f32[9216]{0:T(1024)S(1)} %add.61), channel_id=1, source_target_pairs={{0,4},{2,6},{4,0},{6,2},{8,12},{10,14},{12,8},{14,10},{16,20},{18,... | collective-permute-start | bytes 110600 | tf_op jit(solution)/shard_map/small.2/ppermute | solution.py:748
  372.0 10.8 %collective-permute-start.50 = (bf16[256,512]{1,0:T(8,128)(2,1)S(1)}, bf16[256,512]{1,0:T(8,128)(2,1)S(1)}, u32[]{:S(2)}, u32[]{:S(2)}) collective-permute-start(bf16[256,512]{1,0:T(8,128)(2,1)S(1)} %get-tuple-element.12786), channel_id=1, source_target_pairs={{0,8},{2,10},{4,12},{6,14},{8,0},{10,2},{12,4},{14,6},{16,24},{18,... | collective-permute-start | bytes 786440 | tf_op jit(solution)/shard_map/att1.d1/ppermute | solution.py:748
  372.8 11.0 %collective-permute-start.51 = (bf16[128,512]{1,0:T(8,128)(2,1)S(1)}, bf16[128,512]{1,0:T(8,128)(2,1)S(1)}, u32[]{:S(2)}, u32[]{:S(2)}) collective-permute-start(bf16[128,512]{1,0:T(8,128)(2,1)S(1)} %add_convert_fusion.3), channel_id=1, source_target_pairs={{0,16},{2,18},{4,20},{6,22},{8,24},{10,26},{12,28},{14,30},{16,0},... | collective-permute-start | bytes 393224 | tf_op jit(solution)/shard_map/att0.u0/ppermute | solution.py:748
  375.1 10.3 %collective-permute-start.52 = (f32[9216]{0:T(1024)S(1)}, f32[9216]{0:T(1024)S(1)}, u32[]{:S(2)}, u32[]{:S(2)}) collective-permute-start(f32[9216]{0:T(1024)S(1)} %add.64), channel_id=1, source_target_pairs={{0,8},{2,10},{4,12},{6,14},{8,0},{10,2},{12,4},{14,6},{16,24},{18,... | collective-permute-start | bytes 110600 | tf_op jit(solution)/shard_map/small.4/ppermute | solution.py:748
  385.4 12.4 %collective-permute-start.53 = (bf16[128,512]{1,0:T(8,128)(2,1)S(1)}, bf16[128,512]{1,0:T(8,128)(2,1)S(1)}, u32[]{:S(2)}, u32[]{:S(2)}) collective-permute-start(bf16[128,512]{1,0:T(8,128)(2,1)S(1)} %get-tuple-element.13317), channel_id=1, source_target_pairs={{0,16},{2,18},{4,20},{6,22},{8,24},{10,26},{12,28},{14,30},{16,0},... | collective-permute-start | bytes 393224 | tf_op jit(solution)/shard_map/att1.d2/ppermute | solution.py:748
  397.8 20.7 %collective-permute-start.54 = (bf16[256,512]{1,0:T(8,128)(2,1)S(1)}, bf16[256,512]{1,0:T(8,128)(2,1)S(1)}, u32[]{:S(2)}, u32[]{:S(2)}) collective-permute-start(bf16[256,512]{1,0:T(8,128)(2,1)S(1)} %pad_maximum_fusion.4), channel_id=1, source_target_pairs={{0,8},{2,10},{4,12},{6,14},{8,0},{10,2},{12,4},{14,6},{16,24},{18,... | collective-permute-start | bytes 786440 | tf_op jit(solution)/shard_map/att0.u1/ppermute | solution.py:748
  397.8 20.8 %collective-permute-start.55 = (bf16[128,512]{1,0:T(8,128)(2,1)S(1)}, bf16[128,512]{1,0:T(8,128)(2,1)S(1)}, u32[]{:S(2)}, u32[]{:S(2)}) collective-permute-start(bf16[128,512]{1,0:T(8,128)(2,1)S(1)} %add_convert_fusion.2), channel_id=1, source_target_pairs={{0,16},{2,18},{4,20},{6,22},{8,24},{10,26},{12,28},{14,30},{16,0},... | collective-permute-start | bytes 393224 | tf_op jit(solution)/shard_map/att1.u0/ppermute | solution.py:748
  400.2 18.3 %collective-permute-start.56 = (f32[9216]{0:T(1024)S(1)}, f32[9216]{0:T(1024)S(1)}, u32[]{:S(2)}, u32[]{:S(2)}) collective-permute-start(f32[9216]{0:T(1024)S(1)} %add.66), channel_id=1, source_target_pairs={{0,16},{2,18},{4,20},{6,22},{8,24},{10,26},{12,28},{14,30},{16,0},... | collective-permute-start | bytes 110600 | tf_op jit(solution)/shard_map/small.8/ppermute | solution.py:748
  418.6 12.0 %collective-permute-start.57 = (bf16[256,512]{1,0:T(8,128)(2,1)S(1)}, bf16[256,512]{1,0:T(8,128)(2,1)S(1)}, u32[]{:S(2)}, u32[]{:S(2)}) collective-permute-start(bf16[256,512]{1,0:T(8,128)(2,1)S(1)} %pad_maximum_fusion.5), channel_id=1, source_target_pairs={{0,8},{2,10},{4,12},{6,14},{8,0},{10,2},{12,4},{14,6},{16,24},{18,... | collective-permute-start | bytes 786440 | tf_op jit(solution)/shard_map/att1.u1/ppermute | solution.py:748
  418.7 12.1 %collective-permute-start.58 = (bf16[512,512]{1,0:T(8,128)(2,1)S(1)}, bf16[512,512]{1,0:T(8,128)(2,1)S(1)}, u32[]{:S(2)}, u32[]{:S(2)}) collective-permute-start(bf16[512,512]{1,0:T(8,128)(2,1)S(1)} %pad_maximum_fusion.2), channel_id=1, source_target_pairs={{0,4},{2,6},{4,0},{6,2},{8,12},{10,14},{12,8},{14,10},{16,20},{18,... | collective-permute-start | bytes 1572872 | tf_op jit(solution)/shard_map/att0.u2/ppermute | solution.py:748
  431.0 8.1 %collective-permute-start.59 = (bf16[1024,512]{1,0:T(8,128)(2,1)S(1)}, bf16[1024,512]{1,0:T(8,128)(2,1)S(1)}, u32[]{:S(2)}, u32[]{:S(2)}) collective-permute-start(bf16[1024,512]{1,0:T(8,128)(2,1)S(1)} %pad_maximum_fusion.refs_0_), channel_id=1, source_target_pairs={{0,2},{2,0},{4,6},{6,4},{8,10},{10,8},{12,14},{14,12},{16,18},{18,... | collective-permute-start | bytes 3145736 | tf_op jit(solution)/shard_map/att0.other/ppermute | solution.py:748
  431.1 14.3 %collective-permute-start.60 = (bf16[512,512]{1,0:T(8,128)(2,1)S(1)}, bf16[512,512]{1,0:T(8,128)(2,1)S(1)}, u32[]{:S(2)}, u32[]{:S(2)}) collective-permute-start(bf16[512,512]{1,0:T(8,128)(2,1)S(1)} %pad_maximum_fusion.3), channel_id=1, source_target_pairs={{0,4},{2,6},{4,0},{6,2},{8,12},{10,14},{12,8},{14,10},{16,20},{18,... | collective-permute-start | bytes 1572872 | tf_op jit(solution)/shard_map/att1.u2/ppermute | solution.py:748
  (99 other events, 1069.2 us)
Sparse Core Ops, SparseCore 0:
  286.7 68.9 all-gather.4
  372.1 58.7 all-gather.6

commit v3 on v2

--- a/solution.py
+++ b/solution.py
@@ -9,6 +9,7 @@
 from jax.sharding import PartitionSpec as P
 
 HD = 64
+TENSOR, DATA = "tensor", "dp"
 F32 = jnp.float32
 BF16 = jnp.bfloat16
 NEG = -1000000000.0
@@ -111,7 +112,6 @@
         ],
         compiler_params=params(20),
         cost_estimate=cost(),
-        name="attend",
     )(length, qkv, qkv, qkv)
 
 
@@ -175,7 +175,6 @@
         ],
         compiler_params=params(28),
         cost_estimate=cost(),
-        name="attend_back",
     )(length, qkv, qkv, qkv, g_one, out_w, lse)
 
 
@@ -217,7 +216,6 @@
         out_shape=out_shape,
         compiler_params=params(20),
         cost_estimate=cost(),
-        name="project",
     )(at, x, bias, *pieces)
 
 
@@ -297,7 +295,6 @@
         out_shape=out_shape,
         compiler_params=params(20),
         cost_estimate=cost(),
-        name="attended",
     )(at, x, *vecs, *mixed, *flat)
 
 
@@ -343,7 +340,6 @@
         out_shape=out_shape,
         compiler_params=params(24),
         cost_estimate=cost(),
-        name="widened",
     )(at, low, bias, *pieces)
 
 
@@ -417,7 +413,6 @@
         out_shape=out_shape,
         compiler_params=params(32 if cut else 48),
         cost_estimate=cost(),
-        name="narrowed",
     )(at, normal1, *vecs, grad_output, *act, *flat)
 
 
@@ -464,7 +459,6 @@
         ],
         compiler_params=params(24),
         cost_estimate=cost(),
-        name="gelu_back",
     )(at, g, slope, *pieces)
 
 
@@ -513,7 +507,6 @@
         scratch_shapes=[pltpu.VMEM((steps, rows, block), F32)],
         compiler_params=params(28 if n > 1 else 48),
         cost_estimate=cost(),
-        name="attended_back",
     )(g_two, normal, scale, gain, *g_up, *up_w)
 
 
@@ -541,7 +534,6 @@
         out_shape=jax.ShapeDtypeStruct((rows, d), F32),
         compiler_params=params(24),
         cost_estimate=cost(),
-        name="input_grad",
     )(g_one, *g_proj, *qkv_w)
 
 
@@ -580,7 +572,6 @@
         out_shape=shapes,
         compiler_params=params(60),
         cost_estimate=cost(),
-        name="pick",
     )(index, *[pieces[i][0] for i, _ in views])
 
 
@@ -622,7 +613,6 @@
         out_shape=[out, out],
         compiler_params=params(12),
         cost_estimate=cost(),
-        name="add_split",
     )(bits, a, b, a, b)
 
 
@@ -694,7 +684,6 @@
         out_shape=[jax.ShapeDtypeStruct((n * rows, width), BF16) for n in sizes],
         compiler_params=params(24),
         cost_estimate=cost(),
-        name="grad_stack",
     )(bits, *[a[0] if isinstance(a, tuple) else a for a in args])
 
 
@@ -732,7 +721,7 @@
 class Moves:
     def __init__(self, n_dp, n_tensor):
         self.n_dp, self.n_tensor = n_dp, n_tensor
-        self.dp = lax.axis_index("dp")
+        self.dp = lax.axis_index(DATA)
         self.core = self.dp & 1
         self.chip_bits = [b for b in (2, 4, 8, 16, 32, 64) if b < n_dp]
 
@@ -744,7 +733,7 @@
 
     def over(self, a, axis, mask, name):
         with jax.named_scope(name):
-            n = self.n_dp if axis == "dp" else self.n_tensor
+            n = self.n_dp if axis == DATA else self.n_tensor
             return Box(lax.ppermute(a.value, axis, [(i, i ^ mask) for i in range(n)]))
 
 
@@ -830,11 +819,11 @@
     )(jnp.asarray(table), *[gathered.reshape(-1, unit, columns)] * views)
 
 
-START, LATENCY = 1.4, 3.0
-RATES = {"y": 46e3, "x": 46e3, "z": 46e3, "core": 500e3}
+START, LATENCY = 1.5, 2.5
+RATES = {"y": 46.5e3, "x": 46.5e3, "z": 46.5e3, "core": 500e3}
 GATHER = 52.0
 FLIGHTS = 5
-MARGIN, PATIENCE = 4.0, 8.0
+MARGIN, PATIENCE, EARLY = 4.0, 8.0, 2.0
 
 
 class Plan:
@@ -854,7 +843,7 @@
         self.tasks.append((rank, len(self.tasks), name, cost, needs, makes, work, sends))
 
     def link(self, axis, mask):
-        if axis == "tensor":
+        if axis == TENSOR:
             return "y", mask
         if mask < 4:
             return ("core", "x")[mask // 2], 1
@@ -890,18 +879,16 @@
             if after in self.flying:
                 self.land(after)
             self.waiting.remove(s)
-            held = []
-            if s[3] is not None:
-                value = self.box[s[1]].value
-                size = value.size * value.dtype.itemsize
-                held = [
-                    k
-                    for k in self.flying
-                    if self.sent[k][0] < self.gap and self.flown[k][0] <= size
-                ]
-                for k in [k for k in held if self.when[k] <= self.clock + PATIENCE]:
-                    self.land(k)
-                    held.remove(k)
+            value = self.box[s[1]].value
+            size = 1e9 if s[3] is None else value.size * value.dtype.itemsize
+            held = [
+                k
+                for k in self.flying
+                if self.sent[k][0] < self.gap and self.flown[k][0] <= size
+            ]
+            for k in [k for k in held if self.when[k] <= self.clock + PATIENCE]:
+                self.land(k)
+                held.remove(k)
             for k in held:
                 self.free[self.flown[k][1]] = max(
                     [self.clock]
@@ -923,7 +910,9 @@
     def land(self, key):
         self.flying.remove(key)
         self.steps.wait(self.box[key])
-        self.clock = max(self.clock, self.when[key])
+        if self.when[key] > self.clock:
+            self.clock = self.when[key]
+            self.gap += 1
 
     def run(self):
         while self.tasks:
@@ -939,11 +928,24 @@
             soonest = min(start.values(), default=1e9)
             due = [self.when[s[4]] for s in self.waiting if s[4] in self.when]
             if due and min(due) <= soonest:
-                self.clock = max(self.clock, min(due))
+                if min(due) > self.clock:
+                    self.clock = min(due)
+                    self.gap += 1
                 continue
-            chosen = next(t for t in known if start[t[1]] <= soonest + 0.01)
+            ready = [t for t in known if start[t[1]] <= soonest + 0.01]
+            chosen = ready[0]
+            soon = min((t for t in due if t > soonest), default=1e9)
+            if soonest + chosen[3] > soon + EARLY:
+                fits = [t for t in ready if soonest + t[3] <= soon + EARLY]
+                if not fits:
+                    self.clock = soon
+                    self.gap += 1
+                    continue
+                chosen = fits[0]
             self.tasks.remove(chosen)
             rank, _, name, cost, needs, makes, work, sends = chosen
+            if start[chosen[1]] > self.clock:
+                self.gap += 1
             self.clock = begun = start[chosen[1]]
             for key in sorted(self.flying, key=lambda k: self.when[k]):
                 if self.when[key] <= self.clock - MARGIN and key not in needs:
@@ -953,6 +955,7 @@
                     self.flying.remove(key)
                     if work is None:
                         self.steps.wait(self.box[key])
+                        self.gap += 1
             if work is not None:
                 COST[0] = cost
                 out = self.steps(name, work, *[self.box[k] for k in needs])
@@ -969,18 +972,18 @@
         cut = [f"{name}.cut{i}.{d}" for i in (0, 1)]
         come = [f"{name}.c{i}.{d}" for i in (0, 1)]
         far = [f"{name}.far{i}.{d}" for i in (0, 1)]
-        self.task(f"{sib}.send", rank, 0.0, [y], [], None, [(sib, y, "dp", 1)])
+        self.task(f"{sib}.send", rank, 0.0, [y], [], None, [(sib, y, DATA, 1)])
         self.task(
             f"{name}.cut{d}",
             rank + 0.01,
-            1.3,
+            0.4,
             [y],
             cut,
             lambda a: jnp.split(a, 2, axis),
-            [(c, k, "dp", m) for c, k, m in zip(come, cut, masks)],
+            [(c, k, DATA, m) for c, k, m in zip(come, cut, masks)],
         )
         for c, f in zip(come, far):
-            self.task(f, rank, 0.0, [c], [], None, [(f, c, "dp", 1)])
+            self.task(f, rank, 0.0, [c], [], None, [(f, c, DATA, 1)])
         return [y, sib, *come, *far]
 
 
@@ -998,7 +1001,7 @@
                     [cur[d], f"{name}.y{d + s}.{s}"],
                     [new[d]],
                     lambda a, b: [add(a, b)],
-                    [(f"{name}.y{d}.{s // 2}", new[d], "tensor", s // 2)] * far,
+                    [(f"{name}.y{d}.{s // 2}", new[d], TENSOR, s // 2)] * far,
                 )
             cur, s = new, s // 2
         needs = [cur[0], f"{name}.y1.1"]
@@ -1013,14 +1016,14 @@
                 send,
                 rank,
                 costs[i],
-                ["info", *needs],
+                ["i", *needs],
                 [keep, send],
                 work,
-                [(come, send, "dp", m)],
+                [(come, send, DATA, m)],
             )
             needs = [keep, come]
         own, up = f"{name}.own", list(reversed(levels)) + [1]
-        sends = [(f"{name}.u0", own, "dp", up[0])] if back else []
+        sends = [(f"{name}.u0", own, DATA, up[0])] if back else []
         self.task(own, rank, 0.5, needs, [own], lambda a, b: [add(a, b)], sends)
         for i, m in enumerate(up[:-1] if back else []):
             last = i + 2 == len(up)
@@ -1039,11 +1042,11 @@
                 [own, f"{name}.u{i}"],
                 [out],
                 work,
-                [(come, out, "dp", up[i + 1])],
+                [(come, out, DATA, up[i + 1])],
             )
             own = out
 
-    def gather(self, rank, name, chunks):
+    def gather(self, rank, name, chunks, after):
         self.task(
             name,
             rank,
@@ -1051,7 +1054,7 @@
             [f"{c}.own" for c in chunks],
             [name],
             lambda *a: [jnp.concatenate(a, axis=0) if len(a) > 1 else a[0]],
-            [(f"{name}.all", name, "dp", None)],
+            [(f"{name}.all", name, DATA, None, after)],
         )
 
 
@@ -1077,10 +1080,10 @@
     width = x.shape[1]
 
     def whole(w, axis):
-        return lax.all_gather(w, "tensor", axis=axis, tiled=True)
+        return lax.all_gather(w, TENSOR, axis=axis, tiled=True)
 
     info = jnp.zeros((BITS + 1,), jnp.int32)
-    length = lax.dynamic_slice_in_dim(lengths, lax.axis_index("tensor"), 1, 0)
+    length = lax.dynamic_slice_in_dim(lengths, lax.axis_index(TENSOR), 1, 0)
     q_bias, v_bias = whole(qv_bias, 1)
     bias = [q_bias, jnp.zeros_like(q_bias), v_bias, whole(up_bias, 0).astype(F32)]
     bias = jnp.concatenate(bias).reshape(-1, 1, width)
@@ -1112,11 +1115,11 @@
     g_input = input_grad(g_one, [g_qkv], [qkv_w])
 
     def total(a, axis):
-        part = lax.psum_scatter(a, "tensor", scatter_dimension=axis, tiled=True)
-        return lax.psum(part, "dp")
+        part = lax.psum_scatter(a, TENSOR, scatter_dimension=axis, tiled=True)
+        return lax.psum(part, DATA)
 
     grad_qkv = jnp.stack([contract(x, g_qkv[c], 0, 0) for c in range(3)])
-    small = lax.psum(jnp.concatenate([sums1, sums2]), ("dp", "tensor"))
+    small = lax.psum(jnp.concatenate([sums1, sums2]), (DATA, TENSOR))
     return (
         result,
         g_input,
@@ -1173,23 +1176,23 @@
     place += [mv.bit(m) for m in (1, *mv.chip_bits)]
 
     plan.given(
-        info=jnp.stack(place).astype(jnp.int32),
-        lengths=lengths,
+        i=jnp.stack(place).astype(jnp.int32),
+        lns=lengths,
         x=x,
         qkv_w0=qkv_weight,
         out_w0=out_weight,
         up_w0=up_weight,
         down_w0=down_weight,
-        qv_bias=qv_bias,
-        up_bias=up_bias,
-        grad_output=grad_output,
+        qvb=qv_bias,
+        upb=up_bias,
+        go=grad_output,
     )
 
     def others(name):
-        return [(f"{name}.y{d}", name, "tensor", d) for d in parts[1:]]
+        return [(f"{name}.y{d}", name, TENSOR, d) for d in parts[1:]]
 
     def swap(key):
-        return (f"{key}.sib", key, "dp", 1)
+        return (f"{key}.sib", key, DATA, 1)
 
     def keys(name):
         return [f"{name}{d}" for d in parts]
@@ -1209,18 +1212,18 @@
         "pick_q",
         0,
         2.8,
-        ["info", "qkv_w0"],
+        ["i", "qkv_w0"],
         ["q"],
         pick_q,
-        [(*s, "bias1") for s in others("q")],
+        [(*s, "b1") for s in others("q")],
     )
     task(
-        "length",
+        "ln",
         0.5,
         1.0,
-        ["lengths"],
-        ["length"],
-        lambda n: [lax.dynamic_slice_in_dim(n, lax.axis_index("tensor"), 1, 0)],
+        ["lns"],
+        ["ln"],
+        lambda n: [lax.dynamic_slice_in_dim(n, lax.axis_index(TENSOR), 1, 0)],
     )
 
     def bias_rows(qv, up):
@@ -1229,19 +1232,19 @@
         return [rows.reshape(-1, 1, hw)]
 
     task(
-        "bias0",
+        "b0",
         -1,
         1.5,
-        ["qv_bias", "up_bias"],
-        ["bias0"],
+        ["qvb", "upb"],
+        ["b0"],
         bias_rows,
-        [(f"bias{d}", "bias0", "tensor", d) for d in parts[1:]],
+        [(f"b{d}", "b0", TENSOR, d) for d in parts[1:]],
     )
     task(
         "pick_ou",
         1.0,
         3.2,
-        ["info", "out_w0", "up_w0", "qkv0"],
+        ["i", "out_w0", "up_w0", "qkv0"],
         ["o", "u"],
         pick_ou,
         [(*s, "q.y1") for s in others("o")] + [(*s, "o.y1") for s in others("u")],
@@ -1250,7 +1253,7 @@
         "pick_d",
         2.5,
         3.0,
-        ["info", "down_w0", "heads0"],
+        ["i", "down_w0", "h0"],
         ["d"],
         pick_d,
         [(*s, "u.y1") for s in others("d")],
@@ -1260,7 +1263,7 @@
     for d in parts[1:]:
         qkv_from.append(plan.fetch(0.2, "q", d, (X, Z1), 1))
         o = f"o.y{d}"
-        task(f"o.sib{d}", 0.3, 0.0, [o], [], None, [(f"o.sib{d}", o, "dp", 1)])
+        task(f"o.sib{d}", 0.3, 0.0, [o], [], None, [(f"o.sib{d}", o, DATA, 1)])
         out_from.append([o, f"o.sib{d}"])
         up_from.append(plan.fetch(0.4, "u", d, (X, Z1), 0))
         down_from.append(plan.fetch(0.5, "d", d, (X, Z1), 0))
@@ -1268,19 +1271,19 @@
     for d in parts:
         made = [f"qkv{d}", f"qkv_w{d}"] if d else [f"qkv{d}"]
         task(
-            f"project{d}",
+            f"pj{d}",
             2 + d,
-            4.5 if d else 3.5,
-            ["info", "x", f"bias{d}", *qkv_from[d]],
+            3.0,
+            ["i", "x", f"b{d}", *qkv_from[d]],
             made,
             lambda info, x, b, *w: project(info, x, b, *w),
         )
         task(
-            f"heads{d}",
+            f"h{d}",
             2 + d,
             6.5,
-            ["length", f"qkv{d}"],
-            [f"heads{d}", f"lse{d}"],
+            ["ln", f"qkv{d}"],
+            [f"h{d}", f"lse{d}"],
             attend,
             [],
         )
@@ -1299,23 +1302,23 @@
         )
 
     task(
-        "attended",
+        "at",
         20,
-        5.0,
-        ["info", "x", *keys("heads"), *[k for g in out_from for k in g]],
-        ["normed", "normal1", "scale1", *keys("out_w")[1:]],
+        4.2,
+        ["i", "x", *keys("h"), *[k for g in out_from for k in g]],
+        ["nb", "n1", "sc1", *keys("out_w")[1:]],
         attended_task,
-        [(*swap("normed"), "u.y1")],
+        [(*swap("nb"), "u.y1")],
     )
     for d in parts:
         task(
-            f"widened{d}",
+            f"wd{d}",
             21 + d,
-            10.0,
-            ["info", "normed", f"bias{d}", *up_from[d]],
-            [f"act{d}", f"slope{d}"] + [f"up_w{d}"] * (d > 0),
+            8.5,
+            ["i", "nb", f"b{d}", *up_from[d]],
+            [f"a{d}", f"sl{d}"] + [f"up_w{d}"] * (d > 0),
             widened,
-            [(*swap(f"act{d}"), "d.y1")],
+            [(*swap(f"a{d}"), "d.y1")],
         )
 
     def narrowed_task(info, normal1, grad_output, *rest):
@@ -1335,14 +1338,14 @@
         return low, g_two, result, sums
 
     task(
-        "narrowed",
+        "nw",
         40,
-        14.5,
-        ["info", "normal1", "grad_output", *keys("act")]
+        12.5,
+        ["i", "n1", "go", *keys("a")]
         + [k for g in down_from for k in g],
-        ["g2", "g_two", "result", "sums2"],
+        ["g2", "gt", "res", "sums2"],
         narrowed_task,
-        [swap("g2")] + [swap(k) for k in ("x", *keys("heads"))],
+        [swap("g2")],
     )
 
     block = fw // 4
@@ -1371,11 +1374,11 @@
             f"{name}.p{of[0]}",
             rank,
             cost,
-            ["info", *args],
+            ["i", *args],
             [f"{name}.p{d}" for d in of],
             work,
             [
-                (f"{name}.y{d}.{s}", f"{name}.p{d}", "tensor", s, after)
+                (f"{name}.y{d}.{s}", f"{name}.p{d}", TENSOR, s, after)
                 for d in of
                 if d >= s
             ],
@@ -1388,31 +1391,35 @@
         chunks[name] = (levels, rows)
         plan.reduce(rank, name, levels, back)
 
-    made(
-        "down",
-        51.5,
-        9.5,
-        lambda d: [(f"act{d}", None, "g2", None, 4, (0,), (0, 1))],
-        block,
-        half,
-    )
+    for i, of in enumerate((back[: n_tensor // 2], back[n_tensor // 2 :])):
+        made(
+            "down",
+            50 + 2.5 * i,
+            6.0,
+            lambda d: [(f"a{d}", None, "g2", None, 4, (0,), (0, 1))],
+            block,
+            half,
+            None,
+            of,
+        )
     chunk(1.0, "down", (X, *Z), fw)
     for i, d in enumerate(back):
         task(
-            f"gelu_back{d}",
+            f"gb{d}",
             51 + i,
-            6.5,
-            ["info", "g2", f"slope{d}", *down_from[d]],
-            [f"g_up{d}", f"up_sum{d}"],
-            gelu_back,
-            [(*swap(f"g_up{d}"), None if d else f"down.y{first_y}")],
+            6.0,
+            ["i", "g2", f"sl{d}", *down_from[d], f"down.p{back[0]}"],
+            [f"gu{d}", f"us{d}"],
+            lambda *a: gelu_back(*a[:-1]),
+            [(*swap(f"gu{d}"), None if d else f"down.y{first_y}")]
+            + [swap(k) for k in ("x", *keys("h")) if d],
         )
     for i, of in enumerate((back[: n_tensor // 2], back[n_tensor // 2 :])):
         made(
             "up",
             64 + 4 * i,
-            5.5,
-            lambda d: [("normed", None, f"g_up{d}", None, 2, (0, 2), (0,))],
+            4.0,
+            lambda d: [("nb", None, f"gu{d}", None, 2, (0, 2), (0,))],
             half // 2,
             fw,
             f"down.y{first_y}",
@@ -1426,30 +1433,30 @@
         )
 
     task(
-        "attended_back",
+        "ab",
         56,
-        11.5,
-        ["g_two", "normal1", "scale1", *keys("g_up"), *keys("up_w")],
-        ["g1", "g_one", "sums1"],
+        7.5,
+        ["gt", "n1", "sc1", *keys("gu"), *keys("up_w")],
+        ["g1", "go1", "sums1"],
         attended_back_task,
         [(*swap("g1"), f"down.y{first_y}")],
     )
     for i, d in enumerate(back):
         task(
-            f"heads_back{d}",
+            f"hb{d}",
             62 + i,
-            12.0,
-            ["length", f"qkv{d}", "g1", f"out_w{d}", f"lse{d}"],
-            [f"g_qkv{d}", f"qkv_sum{d}"],
+            10.8,
+            ["ln", f"qkv{d}", "g1", f"out_w{d}", f"lse{d}"],
+            [f"gq{d}", f"qs{d}"],
             attend_back,
-            [(*swap(f"g_qkv{d}"), f"down.y{first_y}")],
+            [(*swap(f"gq{d}"), f"down.y{first_y}")],
         )
 
     def out_item(d):
-        return (f"heads{d}", None, "g1", None, 1, (0,), (0, 1))
+        return (f"h{d}", None, "g1", None, 1, (0,), (0, 1))
 
     def qkv_item(c):
-        return lambda d: ("x", None, f"g_qkv{d}", c, 1, (0, 1), (0,))
+        return lambda d: ("x", None, f"gq{d}", c, 1, (0, 1), (0,))
 
     if same:
         groups = {"att0": [out_item, qkv_item(2)], "att1": [qkv_item(1), qkv_item(0)]}
@@ -1460,7 +1467,7 @@
         made(
             name,
             66 + i,
-            7.5,
+            5.2,
             lambda d, items=items: [it(d) for it in items],
             rows,
             half if items[0] is out_item else hw,
@@ -1477,27 +1484,27 @@
             )
         return packs
 
-    needs = [k for d in parts for k in (f"qkv_sum{d}", f"up_sum{d}")]
-    packs, s = keys("pack"), n_tensor // 2
+    needs = [k for d in parts for k in (f"qs{d}", f"us{d}")]
+    packs, s = keys("pk"), n_tensor // 2
     task(
-        "pack",
+        "pk",
         70,
-        3.0,
+        1.5,
         ["sums1", "sums2", *needs],
         packs,
         pack,
         [
-            (f"pack{d}.y", f"pack{d}", "tensor", s, f"att1.y{first_y}")
+            (f"pk{d}.y", f"pk{d}", TENSOR, s, f"att1.y{first_y}")
             for d in range(s, n_tensor)
         ],
     )
     while s:
-        new = [f"small{s}.{d}" for d in range(s)]
+        new = [f"sm{s}.{d}" for d in range(s)]
         for d in range(s):
             if s > 1:
-                sends = [(f"{new[d]}.y", new[d], "tensor", s // 2)] * (d >= s // 2)
+                sends = [(f"{new[d]}.y", new[d], TENSOR, s // 2)] * (d >= s // 2)
             else:
-                sends = [("small.1", new[0], "dp", 1)]
+                sends = [("sm.1", new[0], DATA, 1)]
             task(
                 new[d],
                 2.0,
@@ -1510,23 +1517,23 @@
         packs, s = new, s // 2
     last, masks = packs[0], [1, *mv.chip_bits]
     for i, m in enumerate(masks):
-        out = f"small.at{m}"
+        out = f"sm.at{m}"
         nxt = masks[i + 1] if i + 1 < len(masks) else None
-        sends = [(f"small.{nxt}", out, "dp", nxt)] if nxt else []
-        task(out, 2.0, 0.6, [last, f"small.{m}"], [out], lambda a, b: [a + b], sends)
+        sends = [(f"sm.{nxt}", out, DATA, nxt)] if nxt else []
+        task(out, 2.0, 0.6, [last, f"sm.{m}"], [out], lambda a, b: [a + b], sends)
         last = out
 
     task(
-        "input_grad",
+        "ig",
         80,
-        9.0,
-        ["g_one", *keys("g_qkv"), *keys("qkv_w")],
-        ["g_input"],
+        7.0,
+        ["go1", *keys("gq"), *keys("qkv_w")],
+        ["gi"],
         lambda g, *a: [input_grad(g, a[:n_tensor], a[n_tensor:])],
     )
 
-    def results(group, names, outputs):
-        plan.gather(1.9, group, names)
+    def results(group, names, outputs, after=None):
+        plan.gather(1.9, group, names, after)
         per_device = [chunks[n][1] // (n_dp // 2) for n in names]
         unit = min(per_device)
         total = sum(per_device) // unit
@@ -1557,25 +1564,26 @@
             )
 
     results(
-        "down_all",
+        "da",
         ("down",),
         [
             (
-                "grad_down",
+                "gd",
                 6.0,
                 [(c, "down", r * block, (r, c)) for r in range(4) for c in (0, 1)],
                 (block, half),
                 (fw, width),
             )
         ],
+        f"att0.y{first_y}",
     )
     rows = half // 4
     results(
-        "up_all",
+        "ua",
         ("up",),
         [
             (
-                "grad_up",
+                "gup",
                 6.0,
                 [
                     (c, "up", r * rows, (4 * c + r, 0))
@@ -1606,7 +1614,7 @@
         )
 
     cores_result(
-        "grad_out",
+        "gout",
         3.0,
         ("att0",),
         [(c, "att0", 0, (0, c)) for c in (0, 1)],
@@ -1617,7 +1625,7 @@
     if not same:
         place = {c: ("att1", 2 - c) for c in range(3)}
     cores_result(
-        "grad_qkv",
+        "gqkv",
         5.0,
         ("att0", "att1") if same else ("att1",),
         [(c, *place[i], (i, c, 0)) for i in range(3) for c in (0, 1)],
@@ -1631,17 +1639,17 @@
     vec = [small[i * width : (i + 1) * width] for i in range(6)]
     rest = small[6 * width :]
     return (
-        value["result"],
-        value["g_input"],
-        value["grad_qkv"],
+        value["res"],
+        value["gi"],
+        value["gqkv"],
         rest[: 2 * hw].reshape(2, hw),
-        value["grad_out"],
+        value["gout"],
         vec[0],
         vec[1],
         vec[2],
-        value["grad_up"],
+        value["gup"],
         rest[2 * hw :],
-        value["grad_down"],
+        value["gd"],
         vec[3],
         vec[4],
         vec[5],
@@ -1649,40 +1657,40 @@
 
 
 def solution(mesh):
-    n_dp, n_tensor = mesh.shape["dp"], mesh.shape["tensor"]
+    n_dp, n_tensor = mesh.shape[DATA], mesh.shape[TENSOR]
     pairs = n_tensor == 2 and n_dp >= 8 and n_dp & (n_dp - 1) == 0
     return jax.shard_map(
         functools.partial(body if pairs else plain, n_dp, n_tensor),
         mesh=mesh,
         in_specs=(
-            P(("dp", "tensor"), None),
-            P(None, None, "tensor"),
-            P(None, "tensor"),
-            P("tensor", None),
+            P((DATA, TENSOR), None),
+            P(None, None, TENSOR),
+            P(None, TENSOR),
+            P(TENSOR, None),
             P(),
             P(),
             P(),
-            P(None, "tensor"),
-            P("tensor"),
-            P("tensor", None),
+            P(None, TENSOR),
+            P(TENSOR),
+            P(TENSOR, None),
             P(),
             P(),
             P(),
-            P("dp"),
-            P(("dp", "tensor"), None),
+            P(DATA),
+            P((DATA, TENSOR), None),
         ),
         out_specs=(
-            P(("dp", "tensor"), None),
-            P(("dp", "tensor"), None),
-            P(None, None, "tensor"),
-            P(None, "tensor"),
-            P("tensor", None),
+            P((DATA, TENSOR), None),
+            P((DATA, TENSOR), None),
+            P(None, None, TENSOR),
+            P(None, TENSOR),
+            P(TENSOR, None),
             P(),
             P(),
             P(),
-            P(None, "tensor"),
-            P("tensor"),
-            P("tensor", None),
+            P(None, TENSOR),
+            P(TENSOR),
+            P(TENSOR, None),
             P(),
             P(),
             P(),

time: 470 us -> 443 us (0.943)
  waiting for transfers between devices: 206 us -> 177 us
  local copies, waits for them, and re-layouts: 38.9 us -> 31.5 us
  Pallas kernels: 147 us -> 153 us
    ppermute x62, waiting for transfers between devices: 206 us -> 168 us  [over(): return Box(lax.ppermute(a.value, axis, [(i, i ^ mask) for i in range(n)]))]
    all_gather x2, waiting for transfers between devices: 0.02 us -> 9.12 us  [send(): self.box[new] = Box(lax.all_gather(a.value, axis))]
    unnamed x173 -> x171, local copies, waits for them, and re-layouts: 34.8 us -> 27.5 us
    pallas_call x5 -> x6, Pallas kernels: 22.5 us -> 27.2 us  [grad_stack(): pl.pallas_call(kernel, grid_spec=pltpu.PrefetchScalarGridSpec(num_scalar_...]
  transfers between devices with their start and end apart: 64 -> 64, of which waited for: 36 -> 30; matrix products, arithmetic and copies ran while one was open for 1% -> 1% of each run, Pallas kernels for 29% -> 32%
where the time goes in v3:
time: 443 us; the launch traced here: 435 us
  waiting for transfers between devices  177 us (40%)
  Pallas kernels  153 us (35%)
  starting transfers between devices  54.2 us (12%)
  local copies, waits for them, and re-layouts  31.5 us (7%)
  between operations  15.8 us (4%)
    ppermute x62, waiting for transfers between devices, over(): return Box(lax.ppermute(a.value, axis, [(i, i ^ mask) for i in range(n)]))  168 us
    ppermute x62, starting transfers between devices, over(): return Box(lax.ppermute(a.value, axis, [(i, i ^ mask) for i in range(n)]))  54.2 us
    unnamed x171, local copies, waits for them, and re-layouts  27.5 us
    pallas_call x6, Pallas kernels, grad_stack(): pl.pallas_call(kernel, grid_spec=pltpu.PrefetchScalarGridSpec(num_scalar_...  27.2 us
    pallas_call x2, Pallas kernels, attend_back(): pl.pallas_call(attend_back_kernel, grid=(width // wide,), in_specs=[pl.Bl...  20.2 us
    pallas_call x2, Pallas kernels, widened(): pl.pallas_call(kernel, grid_spec=pltpu.PrefetchScalarGridSpec(num_scalar_...  15.5 us
    pallas_call x2, Pallas kernels, attend(): pl.pallas_call(attend_kernel, grid=(steps,), in_specs=[pl.BlockSpec(memor...  12.8 us
    pallas_call x12, Pallas kernels, add_split(): pl.pallas_call(kernel, grid_spec=pltpu.PrefetchScalarGridSpec(num_scalar_...  12 us
  transfers between devices with their start and end apart: 64, of which 30 were waited for; matrix products, arithmetic and copies ran while one was open for 1% of the time, Pallas kernels for 32%

profile of v3, /device:TPU:0, one launch (start us, length us, event | category | flops | bytes accessed | tf_op | source)
XLA Modules:
  0.0 435.2 jit_solution(7507886730522134744)
XLA Ops:
  9.4 3.0 collective-permute-start
  12.4 2.8 pick_q.1
  18.0 2.7 pj0.1.q_ref.k_ref.v_ref
  20.7 3.2 pick_ou.1
  23.9 6.3 %h0.1 = (bf16[512,512]{1,0:T(8,128)(2,1)S(1)}, f32[4,2,512]{2,1,0:T(2,128)S(1)}) custom-call(s32[1]{0:T(128)} %dynamic_slice.3.len_ref, bf16[3,512,512]{2,1,0:T(8,128)(2,1)S(1)} %pj0.1.q_ref.k_ref.v_ref, bf16[3,512,512]{2,1,0:T(8,128)(2,1)S(1)} %pj0.1.q_ref.k_ref.v_ref, bf16[3,512,512]{2,1,0:T(8,128)(2,1)S(1)} %pj0.1.q_ref.k_ref.v_ref), custom_call_target="tpu_custom_call" | custom-call | tf_op jit(solution)/shard_map/h0/pallas_call | solution.py:100
  31.0 3.0 pick_d.1
  39.1 8.1 %collective-permute-done.3.refs_2_ = bf16[3,128,512]{2,1,0:T(8,128)(2,1)S(1)} collective-permute-done((bf16[3,128,512]{2,1,0:T(8,128)(2,1)S(1)}, bf16[3,128,512]{2,1,0:T(8,128)(2,1)S(1)}, u32[]{:S(2)}, u32[]{:S(2)}) %collective-permute-start.3) | collective-permute-done | bytes 393248 | tf_op jit(solution)/shard_map/q.c0.1/ppermute | solution.py:737
  53.2 2.9 pj1.1
  56.2 6.6 %h1.1 = (bf16[512,512]{1,0:T(8,128)(2,1)S(1)}, f32[4,2,512]{2,1,0:T(2,128)S(1)}) custom-call(s32[1]{0:T(128)} %dynamic_slice.3.len_ref, bf16[3,512,512]{2,1,0:T(8,128)(2,1)S(1)} %get-tuple-element.11485.q_ref.k_ref.v_ref, bf16[3,512,512]{2,1,0:T(8,128)(2,1)S(1)} %get-tuple-element.11485.q_ref.k_ref.v_ref, ...), custom_call_target="tpu_custom_call" | custom-call | tf_op jit(solution)/shard_map/h1/pallas_call | solution.py:100
  62.9 3.8 at.1
  67.6 7.5 %wd0.1 = (bf16[512,2048]{1,0:T(8,128)(2,1)S(1)}, bf16[512,2048]{1,0:T(8,128)(2,1)S(1)}) custom-call(s32[15]{0:T(128)S(1)} %copy-done.65, bf16[512,1024]{1,0:T(8,128)(2,1)S(1)} %get-tuple-element.11489.x_ref.refs_0_, f32[7,1,512]{2,1,0:T(1,128)S(1)} %reshape.69.b_ref, bf16[1024,2048]{1,0:T(8,128)(2,1)S(1)} %copy-done.2), custom_call_target="tpu_custom_call" | custom-call | tf_op jit(solution)/shard_map/wd0/pallas_call | solution.py:325
  80.2 9.6 %collective-permute-done.12.refs_2_ = bf16[128,2048]{1,0:T(8,128)(2,1)S(1)} collective-permute-done((bf16[128,2048]{1,0:T(8,128)(2,1)S(1)}, bf16[128,2048]{1,0:T(8,128)(2,1)S(1)}, u32[]{:S(2)}, u32[]{:S(2)}) %collective-permute-start.12) | collective-permute-done | bytes 524320 | tf_op jit(solution)/shard_map/u.c0.1/ppermute | solution.py:737
  91.5 12.0 %collective-permute-done.14.refs_3_.refs_0_ = bf16[512,1024]{1,0:T(8,128)(2,1)S(1)} collective-permute-done((bf16[512,1024]{1,0:T(8,128)(2,1)S(1)}, bf16[512,1024]{1,0:T(8,128)(2,1)S(1)}, u32[]{:S(2)}, u32[]{:S(2)}) %collective-permute-start.14) | collective-permute-done | bytes 1048608 | tf_op jit(solution)/shard_map/d.y1/ppermute | solution.py:737
  106.1 8.1 %wd1.1 = (bf16[512,2048]{1,0:T(8,128)(2,1)S(1)}, bf16[512,2048]{1,0:T(8,128)(2,1)S(1)}, bf16[1024,2048]{1,0:T(8,128)(2,1)S(1)}) custom-call(s32[15]{0:T(128)S(1)} %copy-done.65, bf16[512,1024]{1,0:T(8,128)(2,1)S(1)} %get-tuple-element.11489.x_ref.refs_0_, f32[7,1,512]{2,1,0:T(1,128)S(1)} %collective-permute-done.b_ref, ...), custom_call_target="tpu_custom_call" | custom-call | tf_op jit(solution)/shard_map/wd1/pallas_call | solution.py:325
  119.6 4.0 collective-permute-done.21.refs_7_.refs_4_
  127.2 10.3 %nw.1 = (bf16[512,1024]{1,0:T(8,128)(2,1)S(1)}, f32[512,1024]{1,0:T(8,128)S(1)}, bf16[512,1024]{1,0:T(8,128)(2,1)}, f32[3,1024]{1,0:T(4,128)S(1)}) custom-call(s32[15]{0:T(128)S(1)} %copy-done.65, f32[512,1024]{1,0:T(8,128)S(1)} %get-tuple-element.11490.nm_ref, f32[1,1024]{1,0:T(1,128)S(1)} %bitcast.35, f32[1,1024]{1,0:T(1,128)S(1)} %bitcast.38, ...), custom_call_target="tpu_custom_call" | custom-call | tf_op jit(solution)/shard_map/nw/pallas_call | solution.py:399
  140.3 6.0 %down.p1.1 = bf16[2048,512]{1,0:T(8,128)(2,1)} custom-call(s32[15]{0:T(128)S(1)} %copy-done.65, bf16[512,2048]{1,0:T(8,128)(2,1)S(1)} %get-tuple-element.11507.refs_1_.refs_0_, bf16[512,1024]{1,0:T(8,128)(2,1)S(1)} %get-tuple-element.11514.refs_1_.g_ref, bf16[512,2048]{1,0:T(8,128)(2,1)} %collective-permute-done.23.refs_2_, ...), custom_call_target="tpu_custom_call" | custom-call | tf_op jit(solution)/shard_map/down.p1/pallas_call | solution.py:679
  146.3 4.3 gb1.1
  153.1 4.0 gb0.1
  157.2 4.0 down.p0.1.a0.a1
  165.2 6.6 %ab.1 = (bf16[512,1024]{1,0:T(8,128)(2,1)S(1)}, f32[512,1024]{1,0:T(8,128)S(1)}, f32[3,1024]{1,0:T(4,128)S(1)}) custom-call(f32[512,1024]{1,0:T(8,128)S(1)} %copy-done.38, f32[512,1024]{1,0:T(8,128)S(1)} %get-tuple-element.11490.nm_ref, f32[512,1]{1,0:T(8,128)S(1)} %get-tuple-element.11491.sc_ref, f32[1,1024]{1,0:T(1,128)S(1)} %bitcast.36, ...), custom_call_target="tpu_custom_call" | custom-call | tf_op jit(solution)/shard_map/ab/pallas_call | solution.py:499
  171.9 10.0 %hb1.1 = (bf16[3,512,512]{2,1,0:T(8,128)(2,1)S(1)}, f32[3,512]{1,0:T(4,128)S(1)}) custom-call(s32[1]{0:T(128)} %dynamic_slice.3.len_ref, bf16[3,512,512]{2,1,0:T(8,128)(2,1)S(1)} %get-tuple-element.11485.q_ref.k_ref.v_ref, bf16[3,512,512]{2,1,0:T(8,128)(2,1)S(1)} %get-tuple-element.11485.q_ref.k_ref.v_ref, ...), custom_call_target="tpu_custom_call" | custom-call | tf_op jit(solution)/shard_map/hb1/pallas_call | solution.py:158
  183.0 10.2 %hb0.1 = (bf16[3,512,512]{2,1,0:T(8,128)(2,1)S(1)}, f32[3,512]{1,0:T(4,128)S(1)}) custom-call(s32[1]{0:T(128)} %dynamic_slice.3.len_ref, bf16[3,512,512]{2,1,0:T(8,128)(2,1)S(1)} %pj0.1.q_ref.k_ref.v_ref, bf16[3,512,512]{2,1,0:T(8,128)(2,1)S(1)} %pj0.1.q_ref.k_ref.v_ref, bf16[3,512,512]{2,1,0:T(8,128)(2,1)S(1)} %pj0.1.q_ref.k_ref.v_ref, ...), custom_call_target="tpu_custom_call" | custom-call | tf_op jit(solution)/shard_map/hb0/pallas_call | solution.py:158
  194.4 4.8 %up.p1.1 = bf16[512,2048]{1,0:T(8,128)(2,1)S(1)} custom-call(s32[15]{0:T(128)S(1)} %copy-done.65, bf16[512,1024]{1,0:T(8,128)(2,1)S(1)} %get-tuple-element.11489.x_ref.refs_0_, bf16[512,2048]{1,0:T(8,128)(2,1)S(1)} %get-tuple-element.11519.refs_1_, bf16[512,1024]{1,0:T(8,128)(2,1)S(1)} %collective-permute-done.10.refs_2_, ...), custom_call_target="tpu_custom_call" | custom-call | tf_op jit(solution)/shard_map/up.p1/pallas_call | solution.py:679
  209.1 3.3 up.p0.1.a0.a1
  212.5 5.5 %ig.1 = f32[512,1024]{1,0:T(8,128)} custom-call(f32[512,1024]{1,0:T(8,128)S(1)} %copy-done.50, bf16[3,512,512]{2,1,0:T(8,128)(2,1)S(1)} %copy-done.10, bf16[3,512,512]{2,1,0:T(8,128)(2,1)S(1)} %copy-done.8, bf16[3,1024,512]{2,1,0:T(8,128)(2,1)S(1)} %copy-done.4, bf16[3,1024,512]{2,1,0:T(8,128)(2,1)S(1)} %copy-done.36), custom_call_target="tpu_custom_call" | custom-call | tf_op jit(solution)/shard_map/ig/pallas_call | solution.py:527
  218.0 5.0 %att0.p1.1 = (bf16[1024,512]{1,0:T(8,128)(2,1)}, bf16[1024,512]{1,0:T(8,128)(2,1)S(1)}) custom-call(s32[15]{0:T(128)S(1)} %copy-done.65, bf16[512,512]{1,0:T(8,128)(2,1)S(1)} %copy-done.43, bf16[512,1024]{1,0:T(8,128)(2,1)S(1)} %copy-done.18, bf16[512,512]{1,0:T(8,128)(2,1)S(1)} %copy-done.63, ...), custom_call_target="tpu_custom_call" | custom-call | tf_op jit(solution)/shard_map/att0.p1/pallas_call | solution.py:679
  223.0 4.1 att1.p1.1
  227.1 6.3 %collective-permute-done.34.b0.b1 = bf16[1024,512]{1,0:T(8,128)(2,1)S(1)} collective-permute-done((bf16[1024,512]{1,0:T(8,128)(2,1)S(1)}, bf16[1024,512]{1,0:T(8,128)(2,1)S(1)}, u32[]{:S(2)}, u32[]{:S(2)}) %collective-permute-start.34) | collective-permute-done | bytes 1048608 | tf_op jit(solution)/shard_map/down.d0/ppermute | solution.py:737
  235.0 12.4 %collective-permute-done.35.b0.b1 = bf16[512,512]{1,0:T(8,128)(2,1)S(1)} collective-permute-done((bf16[512,512]{1,0:T(8,128)(2,1)S(1)}, bf16[512,512]{1,0:T(8,128)(2,1)S(1)}, u32[]{:S(2)}, u32[]{:S(2)}) %collective-permute-start.35) | collective-permute-done | bytes 524320 | tf_op jit(solution)/shard_map/down.d1/ppermute | solution.py:737
  255.6 10.8 %collective-permute-done.37 = bf16[256,512]{1,0:T(8,128)(2,1)S(1)} collective-permute-done((bf16[256,512]{1,0:T(8,128)(2,1)S(1)}, bf16[256,512]{1,0:T(8,128)(2,1)S(1)}, u32[]{:S(2)}, u32[]{:S(2)}) %collective-permute-start.37) | collective-permute-done | bytes 262176 | tf_op jit(solution)/shard_map/down.d2/ppermute | solution.py:737
  267.2 7.0 %collective-permute-done.38.b0.b1 = bf16[1024,512]{1,0:T(8,128)(2,1)S(1)} collective-permute-done((bf16[1024,512]{1,0:T(8,128)(2,1)}, bf16[1024,512]{1,0:T(8,128)(2,1)S(1)}, u32[]{:S(2)}, u32[]{:S(2)}) %collective-permute-start.38) | collective-permute-done | bytes 1048608 | tf_op jit(solution)/shard_map/att0.y1.1/ppermute | solution.py:737
  284.3 19.6 %collective-permute-done.40.b0.b1 = bf16[128,2048]{1,0:T(8,128)(2,1)S(1)} collective-permute-done((bf16[128,2048]{1,0:T(8,128)(2,1)S(1)}, bf16[128,2048]{1,0:T(8,128)(2,1)S(1)}, u32[]{:S(2)}, u32[]{:S(2)}) %collective-permute-start.40) | collective-permute-done | bytes 524320 | tf_op jit(solution)/shard_map/up.d1/ppermute | solution.py:737
  305.5 4.2 collective-permute-start.46
  311.1 3.9 collective-permute-done.43.b0.b1
  316.5 6.4 %collective-permute-start.48 = (bf16[128,512]{1,0:T(8,128)(2,1)S(1)}, bf16[128,512]{1,0:T(8,128)(2,1)S(1)}, u32[]{:S(2)}, u32[]{:S(2)}) collective-permute-start(bf16[128,512]{1,0:T(8,128)(2,1)S(1)} %get-tuple-element.12054), channel_id=1, source_target_pairs={{0,16},{2,18},{4,20},{6,22},{8,24},{10,26},{12,28},{14,30},{16,0},... | collective-permute-start | bytes 393224 | tf_op jit(solution)/shard_map/att0.d2/ppermute | solution.py:737
  323.8 8.7 %collective-permute-done.47.b0.b1 = bf16[512,512]{1,0:T(8,128)(2,1)S(1)} collective-permute-done((bf16[512,512]{1,0:T(8,128)(2,1)S(1)}, bf16[512,512]{1,0:T(8,128)(2,1)S(1)}, u32[]{:S(2)}, u32[]{:S(2)}) %collective-permute-start.47) | collective-permute-done | bytes 524320 | tf_op jit(solution)/shard_map/att1.d0/ppermute | solution.py:737
  333.2 3.8 collective-permute-done.48
  338.1 7.1 %collective-permute-done.50.b0.b1 = bf16[256,512]{1,0:T(8,128)(2,1)S(1)} collective-permute-done((bf16[256,512]{1,0:T(8,128)(2,1)S(1)}, bf16[256,512]{1,0:T(8,128)(2,1)S(1)}, u32[]{:S(2)}, u32[]{:S(2)}) %collective-permute-start.50) | collective-permute-done | bytes 262176 | tf_op jit(solution)/shard_map/att1.d1/ppermute | solution.py:737
  346.8 7.0 %collective-permute-done.51 = bf16[128,512]{1,0:T(8,128)(2,1)S(1)} collective-permute-done((bf16[128,512]{1,0:T(8,128)(2,1)S(1)}, bf16[128,512]{1,0:T(8,128)(2,1)S(1)}, u32[]{:S(2)}, u32[]{:S(2)}) %collective-permute-start.51) | collective-permute-done | bytes 131104 | tf_op jit(solution)/shard_map/att0.u0/ppermute | solution.py:737
  353.9 13.4 %collective-permute-done.52 = bf16[128,512]{1,0:T(8,128)(2,1)S(1)} collective-permute-done((bf16[128,512]{1,0:T(8,128)(2,1)S(1)}, bf16[128,512]{1,0:T(8,128)(2,1)S(1)}, u32[]{:S(2)}, u32[]{:S(2)}) %collective-permute-start.52) | collective-permute-done | bytes 131104 | tf_op jit(solution)/shard_map/att1.d2/ppermute | solution.py:737
  371.7 5.1 %gd.1 = f32[2048,1024]{1,0:T(8,128)} custom-call(s32[4,8]{1,0:T(4,128)S(1)} %copy-done.73, bf16[16,256,512]{2,1,0:T(8,128)(2,1)S(1)} %bitcast.30, bf16[16,256,512]{2,1,0:T(8,128)(2,1)S(1)} %bitcast.31), custom_call_target="tpu_custom_call" | custom-call | tf_op jit(solution)/shard_map/gd/gd/pallas_call | solution.py:801
  377.7 3.9 collective-permute-start.57
  381.9 9.5 %collective-permute-done.56 = bf16[256,512]{1,0:T(8,128)(2,1)S(1)} collective-permute-done((bf16[256,512]{1,0:T(8,128)(2,1)S(1)}, bf16[256,512]{1,0:T(8,128)(2,1)S(1)}, u32[]{:S(2)}, u32[]{:S(2)}) %collective-permute-start.56) | collective-permute-done | bytes 262176 | tf_op jit(solution)/shard_map/att1.u1/ppermute | solution.py:737
  391.6 7.6 %collective-permute-done.57 = bf16[512,512]{1,0:T(8,128)(2,1)S(1)} collective-permute-done((bf16[512,512]{1,0:T(8,128)(2,1)S(1)}, bf16[512,512]{1,0:T(8,128)(2,1)S(1)}, u32[]{:S(2)}, u32[]{:S(2)}) %collective-permute-start.57) | collective-permute-done | bytes 524320 | tf_op jit(solution)/shard_map/att0.u2/ppermute | solution.py:737
  400.6 9.1 %all-gather.7.cloned.1.call-done = bf16[1024,2048]{1,0:T(8,128)(2,1)} async-done(((bf16[64,2048]{1,0:T(8,128)(2,1)}), bf16[1024,2048]{1,0:T(8,128)(2,1)}) %all-gather.7.cloned.1.call-update) | async-done | bytes 4194320 | tf_op jit(solution)/shard_map/ua.all/all_gather | solution.py:856
  411.9 5.1 %gup.1 = f32[1024,2048]{1,0:T(8,128)} custom-call(s32[4,8]{1,0:T(4,128)S(1)} %copy-done.72, bf16[16,64,2048]{2,1,0:T(8,128)(2,1)S(1)} %bitcast.32, bf16[16,64,2048]{2,1,0:T(8,128)(2,1)S(1)} %bitcast.33), custom_call_target="tpu_custom_call" | custom-call | tf_op jit(solution)/shard_map/gup/gup/pallas_call | solution.py:801
  421.9 4.2 gqkv.1
  (333 shorter events, 102.5 us)
Async XLA Ops:
  7.2 362.3 %all-gather.5.cloned.1.call-start = ((), (), s32[]{:S(2)}) async-start(), calls=%async_computation | async-start | bytes 4456448 | tf_op jit(solution)/shard_map/da.all/all_gather | solution.py:856
  15.8 19.2 %collective-permute-start.1 = (bf16[3,256,512]{2,1,0:T(8,128)(2,1)}, bf16[3,256,512]{2,1,0:T(8,128)(2,1)S(1)}, u32[]{:S(2)}, u32[]{:S(2)}) collective-permute-start(bf16[3,256,512]{2,1,0:T(8,128)(2,1)} %pick_q.1), channel_id=1, source_target_pairs={{0,1},{1,0},{2,3},{3,2},{4,5},{5,4},{6,7},{7,6},{8,9},{9,8},{10,11... | collective-permute-start | bytes 2359304 | tf_op jit(solution)/shard_map/q.y1/ppermute | solution.py:737
  35.1 14.3 %collective-permute-start.5 = (bf16[256,1024]{1,0:T(8,128)(2,1)S(1)}, bf16[256,1024]{1,0:T(8,128)(2,1)S(1)}, u32[]{:S(2)}, u32[]{:S(2)}) collective-permute-start(bf16[256,1024]{1,0:T(8,128)(2,1)S(1)} %copy-done.80), channel_id=1, source_target_pairs={{0,1},{1,0},{2,3},{3,2},{4,5},{5,4},{6,7},{7,6},{8,9},{9,8},{10,11... | collective-permute-start | bytes 1572872 | tf_op jit(solution)/shard_map/o.y1/ppermute | solution.py:737
  35.9 11.2 %collective-permute-start.3 = (bf16[3,128,512]{2,1,0:T(8,128)(2,1)S(1)}, bf16[3,128,512]{2,1,0:T(8,128)(2,1)S(1)}, u32[]{:S(2)}, u32[]{:S(2)}) collective-permute-start(bf16[3,128,512]{2,1,0:T(8,128)(2,1)S(1)} %get-tuple-element.11479), channel_id=1, source_target_pairs={{0,4},{2,6},{4,0},{6,2},{8,12},{10,14},{12,8},{14,10},{16,20},{18,... | collective-permute-start | bytes 1179656 | tf_op jit(solution)/shard_map/q.c0.1/ppermute | solution.py:737
  37.5 10.9 %collective-permute-start.4 = (bf16[3,128,512]{2,1,0:T(8,128)(2,1)S(1)}, bf16[3,128,512]{2,1,0:T(8,128)(2,1)S(1)}, u32[]{:S(2)}, u32[]{:S(2)}) collective-permute-start(bf16[3,128,512]{2,1,0:T(8,128)(2,1)S(1)} %get-tuple-element.11480), channel_id=1, source_target_pairs={{0,8},{2,10},{4,12},{6,14},{8,0},{10,2},{12,4},{14,6},{16,24},{18,... | collective-permute-start | bytes 1179656 | tf_op jit(solution)/shard_map/q.c1.1/ppermute | solution.py:737
  49.4 25.7 %collective-permute-start.9 = (bf16[256,2048]{1,0:T(8,128)(2,1)}, bf16[256,2048]{1,0:T(8,128)(2,1)S(1)}, u32[]{:S(2)}, u32[]{:S(2)}) collective-permute-start(bf16[256,2048]{1,0:T(8,128)(2,1)} %get-tuple-element.11474), channel_id=1, source_target_pairs={{0,1},{1,0},{2,3},{3,2},{4,5},{5,4},{6,7},{7,6},{8,9},{9,8},{10,11... | collective-permute-start | bytes 3145736 | tf_op jit(solution)/shard_map/u.y1/ppermute | solution.py:737
  50.1 12.7 %collective-permute-start.8 = (bf16[256,1024]{1,0:T(8,128)(2,1)S(1)}, bf16[256,1024]{1,0:T(8,128)(2,1)S(1)}, u32[]{:S(2)}, u32[]{:S(2)}) collective-permute-start(bf16[256,1024]{1,0:T(8,128)(2,1)S(1)} %collective-permute-done.5.refs_3_), channel_id=1, source_target_pairs={{0,2},{2,0},{4,6},{6,4},{8,10},{10,8},{12,14},{14,12},{16,18},{18,... | collective-permute-start | bytes 1572872 | tf_op jit(solution)/shard_map/o.sib1/ppermute | solution.py:737
  75.8 14.0 %collective-permute-start.12 = (bf16[128,2048]{1,0:T(8,128)(2,1)S(1)}, bf16[128,2048]{1,0:T(8,128)(2,1)S(1)}, u32[]{:S(2)}, u32[]{:S(2)}) collective-permute-start(bf16[128,2048]{1,0:T(8,128)(2,1)S(1)} %get-tuple-element.11496), channel_id=1, source_target_pairs={{0,4},{2,6},{4,0},{6,2},{8,12},{10,14},{12,8},{14,10},{16,20},{18,... | collective-permute-start | bytes 1572872 | tf_op jit(solution)/shard_map/u.c0.1/ppermute | solution.py:737
  77.3 13.7 %collective-permute-start.13 = (bf16[128,2048]{1,0:T(8,128)(2,1)S(1)}, bf16[128,2048]{1,0:T(8,128)(2,1)S(1)}, u32[]{:S(2)}, u32[]{:S(2)}) collective-permute-start(bf16[128,2048]{1,0:T(8,128)(2,1)S(1)} %get-tuple-element.11497), channel_id=1, source_target_pairs={{0,8},{2,10},{4,12},{6,14},{8,0},{10,2},{12,4},{14,6},{16,24},{18,... | collective-permute-start | bytes 1572872 | tf_op jit(solution)/shard_map/u.c1.1/ppermute | solution.py:737
  78.9 24.6 %collective-permute-start.14 = (bf16[512,1024]{1,0:T(8,128)(2,1)S(1)}, bf16[512,1024]{1,0:T(8,128)(2,1)S(1)}, u32[]{:S(2)}, u32[]{:S(2)}) collective-permute-start(bf16[512,1024]{1,0:T(8,128)(2,1)S(1)} %copy-done.75), channel_id=1, source_target_pairs={{0,1},{1,0},{2,3},{3,2},{4,5},{5,4},{6,7},{7,6},{8,9},{9,8},{10,11... | collective-permute-start | bytes 3145736 | tf_op jit(solution)/shard_map/d.y1/ppermute | solution.py:737
  91.0 12.5 %collective-permute-start.15 = (bf16[128,2048]{1,0:T(8,128)(2,1)S(1)}, bf16[128,2048]{1,0:T(8,128)(2,1)S(1)}, u32[]{:S(2)}, u32[]{:S(2)}) collective-permute-start(bf16[128,2048]{1,0:T(8,128)(2,1)S(1)} %collective-permute-done.12.refs_2_), channel_id=1, source_target_pairs={{0,2},{2,0},{4,6},{6,4},{8,10},{10,8},{12,14},{14,12},{16,18},{18,... | collective-permute-start | bytes 1572872 | tf_op jit(solution)/shard_map/u.far0.1/ppermute | solution.py:737
  91.0 12.5 %collective-permute-start.16 = (bf16[128,2048]{1,0:T(8,128)(2,1)S(1)}, bf16[128,2048]{1,0:T(8,128)(2,1)S(1)}, u32[]{:S(2)}, u32[]{:S(2)}) collective-permute-start(bf16[128,2048]{1,0:T(8,128)(2,1)S(1)} %collective-permute-done.13.refs_3_), channel_id=1, source_target_pairs={{0,2},{2,0},{4,6},{6,4},{8,10},{10,8},{12,14},{14,12},{16,18},{18,... | collective-permute-start | bytes 1572872 | tf_op jit(solution)/shard_map/u.far1.1/ppermute | solution.py:737
  103.5 14.0 %collective-permute-start.17 = (bf16[512,2048]{1,0:T(8,128)(2,1)S(1)}, bf16[512,2048]{1,0:T(8,128)(2,1)S(1)}, u32[]{:S(2)}, u32[]{:S(2)}) collective-permute-start(bf16[512,2048]{1,0:T(8,128)(2,1)S(1)} %get-tuple-element.11493.refs_0_), channel_id=1, source_target_pairs={{0,2},{2,0},{4,6},{6,4},{8,10},{10,8},{12,14},{14,12},{16,18},{18,... | collective-permute-start | bytes 6291464 | tf_op jit(solution)/shard_map/a0.sib/ppermute | solution.py:737
  103.6 15.4 %collective-permute-start.18 = (bf16[512,1024]{1,0:T(8,128)(2,1)S(1)}, bf16[512,1024]{1,0:T(8,128)(2,1)S(1)}, u32[]{:S(2)}, u32[]{:S(2)}) collective-permute-start(bf16[512,1024]{1,0:T(8,128)(2,1)S(1)} %collective-permute-done.14.refs_3_.refs_0_), channel_id=1, source_target_pairs={{0,2},{2,0},{4,6},{6,4},{8,10},{10,8},{12,14},{14,12},{16,18},{18,... | collective-permute-start | bytes 3145736 | tf_op jit(solution)/shard_map/d.sib1/ppermute | solution.py:737
  104.2 14.7 %collective-permute-start.19 = (bf16[256,1024]{1,0:T(8,128)(2,1)S(1)}, bf16[256,1024]{1,0:T(8,128)(2,1)S(1)}, u32[]{:S(2)}, u32[]{:S(2)}) collective-permute-start(bf16[256,1024]{1,0:T(8,128)(2,1)S(1)} %get-tuple-element.11505), channel_id=1, source_target_pairs={{0,4},{2,6},{4,0},{6,2},{8,12},{10,14},{12,8},{14,10},{16,20},{18,... | collective-permute-start | bytes 1572872 | tf_op jit(solution)/shard_map/d.c0.1/ppermute | solution.py:737
  104.8 14.1 %collective-permute-start.20 = (bf16[256,1024]{1,0:T(8,128)(2,1)S(1)}, bf16[256,1024]{1,0:T(8,128)(2,1)S(1)}, u32[]{:S(2)}, u32[]{:S(2)}) collective-permute-start(bf16[256,1024]{1,0:T(8,128)(2,1)S(1)} %get-tuple-element.11506), channel_id=1, source_target_pairs={{0,8},{2,10},{4,12},{6,14},{8,0},{10,2},{12,4},{14,6},{16,24},{18,... | collective-permute-start | bytes 1572872 | tf_op jit(solution)/shard_map/d.c1.1/ppermute | solution.py:737
  119.0 21.3 %collective-permute-start.23 = (bf16[512,2048]{1,0:T(8,128)(2,1)S(1)}, bf16[512,2048]{1,0:T(8,128)(2,1)}, u32[]{:S(2)}, u32[]{:S(2)}) collective-permute-start(bf16[512,2048]{1,0:T(8,128)(2,1)S(1)} %get-tuple-element.11507.refs_1_.refs_0_), channel_id=1, source_target_pairs={{0,2},{2,0},{4,6},{6,4},{8,10},{10,8},{12,14},{14,12},{16,18},{18,... | collective-permute-start | bytes 6291464 | tf_op jit(solution)/shard_map/a1.sib/ppermute | solution.py:737
  150.7 11.9 %collective-permute-start.25 = (bf16[512,2048]{1,0:T(8,128)(2,1)S(1)}, bf16[512,2048]{1,0:T(8,128)(2,1)}, u32[]{:S(2)}, u32[]{:S(2)}) collective-permute-start(bf16[512,2048]{1,0:T(8,128)(2,1)S(1)} %get-tuple-element.11519.refs_1_), channel_id=1, source_target_pairs={{0,2},{2,0},{4,6},{6,4},{8,10},{10,8},{12,14},{14,12},{16,18},{18,... | collective-permute-start | bytes 6291464 | tf_op jit(solution)/shard_map/gu1.sib/ppermute | solution.py:737
  151.1 11.4 %collective-permute-start.26 = (bf16[512,1024]{1,0:T(8,128)(2,1)S(1)}, bf16[512,1024]{1,0:T(8,128)(2,1)S(1)}, u32[]{:S(2)}, u32[]{:S(2)}) collective-permute-start(bf16[512,1024]{1,0:T(8,128)(2,1)S(1)} %copy-done), channel_id=1, source_target_pairs={{0,2},{2,0},{4,6},{6,4},{8,10},{10,8},{12,14},{14,12},{16,18},{18,... | collective-permute-start | bytes 3145736 | tf_op jit(solution)/shard_map/x.sib/ppermute | solution.py:737
  151.2 49.5 %collective-permute-start.29 = (bf16[2048,512]{1,0:T(8,128)(2,1)}, bf16[2048,512]{1,0:T(8,128)(2,1)}, u32[]{:S(2)}, u32[]{:S(2)}) collective-permute-start(bf16[2048,512]{1,0:T(8,128)(2,1)} %down.p1.1), channel_id=1, source_target_pairs={{0,1},{1,0},{2,3},{3,2},{4,5},{5,4},{6,7},{7,6},{8,9},{9,8},{10,11... | collective-permute-start | bytes 6291464 | tf_op jit(solution)/shard_map/down.y1.1/ppermute | solution.py:737
  152.6 11.0 %collective-permute-start.27 = (bf16[512,512]{1,0:T(8,128)(2,1)S(1)}, bf16[512,512]{1,0:T(8,128)(2,1)S(1)}, u32[]{:S(2)}, u32[]{:S(2)}) collective-permute-start(bf16[512,512]{1,0:T(8,128)(2,1)S(1)} %copy-done.40), channel_id=1, source_target_pairs={{0,2},{2,0},{4,6},{6,4},{8,10},{10,8},{12,14},{14,12},{16,18},{18,... | collective-permute-start | bytes 1572872 | tf_op jit(solution)/shard_map/h0.sib/ppermute | solution.py:737
  152.6 11.7 %collective-permute-start.28 = (bf16[512,512]{1,0:T(8,128)(2,1)S(1)}, bf16[512,512]{1,0:T(8,128)(2,1)S(1)}, u32[]{:S(2)}, u32[]{:S(2)}) collective-permute-start(bf16[512,512]{1,0:T(8,128)(2,1)S(1)} %copy-done.42), channel_id=1, source_target_pairs={{0,2},{2,0},{4,6},{6,4},{8,10},{10,8},{12,14},{14,12},{16,18},{18,... | collective-permute-start | bytes 1572872 | tf_op jit(solution)/shard_map/h1.sib/ppermute | solution.py:737
  201.3 16.7 %collective-permute-start.32 = (bf16[3,512,512]{2,1,0:T(8,128)(2,1)S(1)}, bf16[3,512,512]{2,1,0:T(8,128)(2,1)S(1)}, u32[]{:S(2)}, u32[]{:S(2)}) collective-permute-start(bf16[3,512,512]{2,1,0:T(8,128)(2,1)S(1)} %copy-done.8), channel_id=1, source_target_pairs={{0,2},{2,0},{4,6},{6,4},{8,10},{10,8},{12,14},{14,12},{16,18},{18,... | collective-permute-start | bytes 4718600 | tf_op jit(solution)/shard_map/gq1.sib/ppermute | solution.py:737
  201.4 16.6 %collective-permute-start.33 = (bf16[3,512,512]{2,1,0:T(8,128)(2,1)}, bf16[3,512,512]{2,1,0:T(8,128)(2,1)S(1)}, u32[]{:S(2)}, u32[]{:S(2)}) collective-permute-start(bf16[3,512,512]{2,1,0:T(8,128)(2,1)} %copy-done.9), channel_id=1, source_target_pairs={{0,2},{2,0},{4,6},{6,4},{8,10},{10,8},{12,14},{14,12},{16,18},{18,... | collective-permute-start | bytes 4718600 | tf_op jit(solution)/shard_map/gq0.sib/ppermute | solution.py:737
  201.8 47.8 %collective-permute-start.36 = (bf16[512,2048]{1,0:T(8,128)(2,1)}, bf16[512,2048]{1,0:T(8,128)(2,1)S(1)}, u32[]{:S(2)}, u32[]{:S(2)}) collective-permute-start(bf16[512,2048]{1,0:T(8,128)(2,1)} %copy-done.46), channel_id=1, source_target_pairs={{0,1},{1,0},{2,3},{3,2},{4,5},{5,4},{6,7},{7,6},{8,9},{9,8},{10,11... | collective-permute-start | bytes 6291464 | tf_op jit(solution)/shard_map/up.y1.1/ppermute | solution.py:737
  208.2 25.2 %collective-permute-start.34 = (bf16[1024,512]{1,0:T(8,128)(2,1)S(1)}, bf16[1024,512]{1,0:T(8,128)(2,1)S(1)}, u32[]{:S(2)}, u32[]{:S(2)}) collective-permute-start(bf16[1024,512]{1,0:T(8,128)(2,1)S(1)} %get-tuple-element.11540), channel_id=1, source_target_pairs={{0,4},{2,6},{4,0},{6,2},{8,12},{10,14},{12,8},{14,10},{16,20},{18,... | collective-permute-start | bytes 3145736 | tf_op jit(solution)/shard_map/down.d0/ppermute | solution.py:737
  234.2 13.2 %collective-permute-start.35 = (bf16[512,512]{1,0:T(8,128)(2,1)S(1)}, bf16[512,512]{1,0:T(8,128)(2,1)S(1)}, u32[]{:S(2)}, u32[]{:S(2)}) collective-permute-start(bf16[512,512]{1,0:T(8,128)(2,1)S(1)} %get-tuple-element.11549), channel_id=1, source_target_pairs={{0,8},{2,10},{4,12},{6,14},{8,0},{10,2},{12,4},{14,6},{16,24},{18,... | collective-permute-start | bytes 1572872 | tf_op jit(solution)/shard_map/down.d1/ppermute | solution.py:737
  249.7 24.5 %collective-permute-start.38 = (bf16[1024,512]{1,0:T(8,128)(2,1)}, bf16[1024,512]{1,0:T(8,128)(2,1)S(1)}, u32[]{:S(2)}, u32[]{:S(2)}) collective-permute-start(bf16[1024,512]{1,0:T(8,128)(2,1)} %get-tuple-element.11544), channel_id=1, source_target_pairs={{0,1},{1,0},{2,3},{3,2},{4,5},{5,4},{6,7},{7,6},{8,9},{9,8},{10,11... | collective-permute-start | bytes 3145736 | tf_op jit(solution)/shard_map/att0.y1.1/ppermute | solution.py:737
  252.2 24.2 %collective-permute-start.39 = (bf16[256,2048]{1,0:T(8,128)(2,1)}, bf16[256,2048]{1,0:T(8,128)(2,1)S(1)}, u32[]{:S(2)}, u32[]{:S(2)}) collective-permute-start(bf16[256,2048]{1,0:T(8,128)(2,1)} %get-tuple-element.11554), channel_id=1, source_target_pairs={{0,4},{2,6},{4,0},{6,2},{8,12},{10,14},{12,8},{14,10},{16,20},{18,... | collective-permute-start | bytes 3145736 | tf_op jit(solution)/shard_map/up.d0/ppermute | solution.py:737
  253.1 13.4 %collective-permute-start.37 = (bf16[256,512]{1,0:T(8,128)(2,1)S(1)}, bf16[256,512]{1,0:T(8,128)(2,1)S(1)}, u32[]{:S(2)}, u32[]{:S(2)}) collective-permute-start(bf16[256,512]{1,0:T(8,128)(2,1)S(1)} %get-tuple-element.11551), channel_id=1, source_target_pairs={{0,16},{2,18},{4,20},{6,22},{8,24},{10,26},{12,28},{14,30},{16,0},... | collective-permute-start | bytes 786440 | tf_op jit(solution)/shard_map/down.d2/ppermute | solution.py:737
  277.4 132.3 %all-gather.7.cloned.1.call-start = ((), (), s32[]{:S(2)}) async-start(), calls=%async_computation.1 | async-start | bytes 4456448 | tf_op jit(solution)/shard_map/ua.all/all_gather | solution.py:856
  277.5 32.2 %collective-permute-start.42 = (bf16[1024,512]{1,0:T(8,128)(2,1)}, bf16[1024,512]{1,0:T(8,128)(2,1)S(1)}, u32[]{:S(2)}, u32[]{:S(2)}) collective-permute-start(bf16[1024,512]{1,0:T(8,128)(2,1)} %copy-done.74), channel_id=1, source_target_pairs={{0,1},{1,0},{2,3},{3,2},{4,5},{5,4},{6,7},{7,6},{8,9},{9,8},{10,11... | collective-permute-start | bytes 3145736 | tf_op jit(solution)/shard_map/att1.y1.1/ppermute | solution.py:737
  280.9 23.1 %collective-permute-start.40 = (bf16[128,2048]{1,0:T(8,128)(2,1)S(1)}, bf16[128,2048]{1,0:T(8,128)(2,1)S(1)}, u32[]{:S(2)}, u32[]{:S(2)}) collective-permute-start(bf16[128,2048]{1,0:T(8,128)(2,1)S(1)} %get-tuple-element.11560), channel_id=1, source_target_pairs={{0,8},{2,10},{4,12},{6,14},{8,0},{10,2},{12,4},{14,6},{16,24},{18,... | collective-permute-start | bytes 1572872 | tf_op jit(solution)/shard_map/up.d1/ppermute | solution.py:737
  282.8 21.9 %collective-permute-start.41 = (bf16[512,512]{1,0:T(8,128)(2,1)S(1)}, bf16[512,512]{1,0:T(8,128)(2,1)S(1)}, u32[]{:S(2)}, u32[]{:S(2)}) collective-permute-start(bf16[512,512]{1,0:T(8,128)(2,1)S(1)} %get-tuple-element.11562), channel_id=1, source_target_pairs={{0,4},{2,6},{4,0},{6,2},{8,12},{10,14},{12,8},{14,10},{16,20},{18,... | collective-permute-start | bytes 1572872 | tf_op jit(solution)/shard_map/att0.d0/ppermute | solution.py:737
  305.4 9.6 %collective-permute-start.43 = (bf16[256,512]{1,0:T(8,128)(2,1)S(1)}, bf16[256,512]{1,0:T(8,128)(2,1)S(1)}, u32[]{:S(2)}, u32[]{:S(2)}) collective-permute-start(bf16[256,512]{1,0:T(8,128)(2,1)S(1)} %get-tuple-element.11566), channel_id=1, source_target_pairs={{0,8},{2,10},{4,12},{6,14},{8,0},{10,2},{12,4},{14,6},{16,24},{18,... | collective-permute-start | bytes 786440 | tf_op jit(solution)/shard_map/att0.d1/ppermute | solution.py:737
  305.5 17.6 %collective-permute-start.46 = (bf16[64,2048]{1,0:T(8,128)(2,1)S(1)}, bf16[64,2048]{1,0:T(8,128)(2,1)S(1)}, u32[]{:S(2)}, u32[]{:S(2)}) collective-permute-start(bf16[64,2048]{1,0:T(8,128)(2,1)S(1)} %get-tuple-element.11810), channel_id=1, source_target_pairs={{0,16},{2,18},{4,20},{6,22},{8,24},{10,26},{12,28},{14,30},{16,0},... | collective-permute-start | bytes 786440 | tf_op jit(solution)/shard_map/up.d2/ppermute | solution.py:737
  315.0 17.5 %collective-permute-start.47 = (bf16[512,512]{1,0:T(8,128)(2,1)S(1)}, bf16[512,512]{1,0:T(8,128)(2,1)S(1)}, u32[]{:S(2)}, u32[]{:S(2)}) collective-permute-start(bf16[512,512]{1,0:T(8,128)(2,1)S(1)} %get-tuple-element.11930), channel_id=1, source_target_pairs={{0,4},{2,6},{4,0},{6,2},{8,12},{10,14},{12,8},{14,10},{16,20},{18,... | collective-permute-start | bytes 1572872 | tf_op jit(solution)/shard_map/att1.d0/ppermute | solution.py:737
  316.5 20.5 %collective-permute-start.48 = (bf16[128,512]{1,0:T(8,128)(2,1)S(1)}, bf16[128,512]{1,0:T(8,128)(2,1)S(1)}, u32[]{:S(2)}, u32[]{:S(2)}) collective-permute-start(bf16[128,512]{1,0:T(8,128)(2,1)S(1)} %get-tuple-element.12054), channel_id=1, source_target_pairs={{0,16},{2,18},{4,20},{6,22},{8,24},{10,26},{12,28},{14,30},{16,0},... | collective-permute-start | bytes 393224 | tf_op jit(solution)/shard_map/att0.d2/ppermute | solution.py:737
  323.0 14.1 %collective-permute-start.49 = (f32[9216]{0:T(1024)S(1)}, f32[9216]{0:T(1024)S(1)}, u32[]{:S(2)}, u32[]{:S(2)}) collective-permute-start(f32[9216]{0:T(1024)S(1)} %add.61), channel_id=1, source_target_pairs={{0,4},{2,6},{4,0},{6,2},{8,12},{10,14},{12,8},{14,10},{16,20},{18,... | collective-permute-start | bytes 110600 | tf_op jit(solution)/shard_map/sm.2/ppermute | solution.py:737
  353.8 13.5 %collective-permute-start.52 = (bf16[128,512]{1,0:T(8,128)(2,1)S(1)}, bf16[128,512]{1,0:T(8,128)(2,1)S(1)}, u32[]{:S(2)}, u32[]{:S(2)}) collective-permute-start(bf16[128,512]{1,0:T(8,128)(2,1)S(1)} %get-tuple-element.13067), channel_id=1, source_target_pairs={{0,16},{2,18},{4,20},{6,22},{8,24},{10,26},{12,28},{14,30},{16,0},... | collective-permute-start | bytes 393224 | tf_op jit(solution)/shard_map/att1.d2/ppermute | solution.py:737
  367.3 9.5 %collective-permute-start.53 = (bf16[256,512]{1,0:T(8,128)(2,1)S(1)}, bf16[256,512]{1,0:T(8,128)(2,1)S(1)}, u32[]{:S(2)}, u32[]{:S(2)}) collective-permute-start(bf16[256,512]{1,0:T(8,128)(2,1)S(1)} %pad_maximum_fusion.4), channel_id=1, source_target_pairs={{0,8},{2,10},{4,12},{6,14},{8,0},{10,2},{12,4},{14,6},{16,24},{18,... | collective-permute-start | bytes 786440 | tf_op jit(solution)/shard_map/att0.u1/ppermute | solution.py:737
  367.3 9.6 %collective-permute-start.54 = (bf16[128,512]{1,0:T(8,128)(2,1)S(1)}, bf16[128,512]{1,0:T(8,128)(2,1)S(1)}, u32[]{:S(2)}, u32[]{:S(2)}) collective-permute-start(bf16[128,512]{1,0:T(8,128)(2,1)S(1)} %add_convert_fusion.2), channel_id=1, source_target_pairs={{0,16},{2,18},{4,20},{6,22},{8,24},{10,26},{12,28},{14,30},{16,0},... | collective-permute-start | bytes 393224 | tf_op jit(solution)/shard_map/att1.u0/ppermute | solution.py:737
  368.1 8.8 %collective-permute-start.55 = (f32[9216]{0:T(1024)S(1)}, f32[9216]{0:T(1024)S(1)}, u32[]{:S(2)}, u32[]{:S(2)}) collective-permute-start(f32[9216]{0:T(1024)S(1)} %add.65), channel_id=1, source_target_pairs={{0,8},{2,10},{4,12},{6,14},{8,0},{10,2},{12,4},{14,6},{16,24},{18,... | collective-permute-start | bytes 110600 | tf_op jit(solution)/shard_map/sm.4/ppermute | solution.py:737
  377.0 14.5 %collective-permute-start.56 = (bf16[256,512]{1,0:T(8,128)(2,1)S(1)}, bf16[256,512]{1,0:T(8,128)(2,1)S(1)}, u32[]{:S(2)}, u32[]{:S(2)}) collective-permute-start(bf16[256,512]{1,0:T(8,128)(2,1)S(1)} %pad_maximum_fusion.5), channel_id=1, source_target_pairs={{0,8},{2,10},{4,12},{6,14},{8,0},{10,2},{12,4},{14,6},{16,24},{18,... | collective-permute-start | bytes 786440 | tf_op jit(solution)/shard_map/att1.u1/ppermute | solution.py:737
  377.7 21.5 %collective-permute-start.57 = (bf16[512,512]{1,0:T(8,128)(2,1)S(1)}, bf16[512,512]{1,0:T(8,128)(2,1)S(1)}, u32[]{:S(2)}, u32[]{:S(2)}) collective-permute-start(bf16[512,512]{1,0:T(8,128)(2,1)S(1)} %pad_maximum_fusion.2), channel_id=1, source_target_pairs={{0,4},{2,6},{4,0},{6,2},{8,12},{10,14},{12,8},{14,10},{16,20},{18,... | collective-permute-start | bytes 1572872 | tf_op jit(solution)/shard_map/att0.u2/ppermute | solution.py:737
  381.6 17.6 %collective-permute-start.58 = (f32[9216]{0:T(1024)S(1)}, f32[9216]{0:T(1024)S(1)}, u32[]{:S(2)}, u32[]{:S(2)}) collective-permute-start(f32[9216]{0:T(1024)S(1)} %add.66), channel_id=1, source_target_pairs={{0,16},{2,18},{4,20},{6,22},{8,24},{10,26},{12,28},{14,30},{16,0},... | collective-permute-start | bytes 110600 | tf_op jit(solution)/shard_map/sm.8/ppermute | solution.py:737
  399.3 17.7 %collective-permute-start.59 = (bf16[1024,512]{1,0:T(8,128)(2,1)S(1)}, bf16[1024,512]{1,0:T(8,128)(2,1)S(1)}, u32[]{:S(2)}, u32[]{:S(2)}) collective-permute-start(bf16[1024,512]{1,0:T(8,128)(2,1)S(1)} %pad_maximum_fusion.refs_0_), channel_id=1, source_target_pairs={{0,2},{2,0},{4,6},{6,4},{8,10},{10,8},{12,14},{14,12},{16,18},{18,... | collective-permute-start | bytes 3145736 | tf_op jit(solution)/shard_map/att0.other/ppermute | solution.py:737
  399.4 19.7 %collective-permute-start.60 = (bf16[512,512]{1,0:T(8,128)(2,1)S(1)}, bf16[512,512]{1,0:T(8,128)(2,1)S(1)}, u32[]{:S(2)}, u32[]{:S(2)}) collective-permute-start(bf16[512,512]{1,0:T(8,128)(2,1)S(1)} %pad_maximum_fusion.3), channel_id=1, source_target_pairs={{0,4},{2,6},{4,0},{6,2},{8,12},{10,14},{12,8},{14,10},{16,20},{18,... | collective-permute-start | bytes 1572872 | tf_op jit(solution)/shard_map/att1.u2/ppermute | solution.py:737
  (98 other events, 926.2 us)
Sparse Core Ops, SparseCore 0:
  277.5 63.6 all-gather.4
  345.3 64.3 all-gather.6
